TPU v7x, 32 devices: a whole 2x2x4 slice. The times are simulated.
32 devices in a mesh: seq: 4 (over y, core), head: 8 (over z, x).
Axes of the slice: x: 2, y: 2, z: 4, core: 2. Of those that a mesh axis runs over, the one named last changes fastest.
Arguments:
- gen_ids: int32 [4, 16], replicated, may hold values from 0 to 8191
- embed_rows: bfloat16 [8192, 8192], P('head', 'seq'), may hold values from -6 to 6
- w_query: bfloat16 [8192, 8192], P('seq', 'head'), may hold values from -0.0625 to 0.0625
- w_key: bfloat16 [8192, 8192], P('seq', 'head'), may hold values from -0.0625 to 0.0625
- w_value: bfloat16 [8192, 8192], P('seq', 'head'), may hold values from -0.0625 to 0.0625
- w_out: bfloat16 [8192, 8192], P('head', 'seq'), may hold values from -0.0625 to 0.0625
- prompt_keys: bfloat16 [2048, 8192], P('seq', 'head'), may hold values from -420 to 420
- prompt_values: bfloat16 [2048, 8192], P('seq', 'head'), may hold values from -6 to 6
Outputs:
- attn_out: bfloat16 [64, 8192], P('seq', 'head')
All inputs are finite; a program needn't handle non-finite values.
Results may differ from a plain program's by a relative error of at most 0.034.
Values may be sent and summed in bfloat16 or wider, within the bound.
No kernel may reach another device: no remote copies, remote signals or barrier semaphores. Data moves between devices by JAX's collectives and lax.ppermute only.
A program may use at most 128 MiB of HBM per device.

v0:
```python
import math

import jax
import jax.numpy as jnp
from jax import lax
from jax.sharding import PartitionSpec as P

HD = 128


def combined_all(part, axis, combine):
    gathered = jax.tree.map(lambda a: lax.all_gather(a, axis), part)

    def take(source):
        return jax.tree.map(lambda a: lax.dynamic_index_in_dim(a, source, 0, False), gathered)

    return lax.fori_loop(
        1, lax.axis_size(axis), lambda source, state: combine(state, take(source)), take(0)
    )


def rotate(vectors, positions):
    half_size = vectors.shape[-1] // 2
    frequency = 10000.0 ** (-jnp.arange(half_size, dtype=jnp.float32) / half_size)
    angles = positions.astype(jnp.float32)[:, None] * frequency[None, :]
    cosine = jnp.cos(angles)[:, None, :]
    sine_part = jnp.sin(angles)[:, None, :]
    former = vectors[..., :half_size]
    latter = vectors[..., half_size:]
    return jnp.concatenate(
        [former * cosine - latter * sine_part, former * sine_part + latter * cosine], axis=-1
    )


def joined(earlier, latter):
    peak = jnp.maximum(earlier[0], latter[0])
    left_factor = jnp.exp(earlier[0] - peak)
    right_factor = jnp.exp(latter[0] - peak)
    weight_sum = earlier[1] * left_factor + latter[1] * right_factor
    summed = earlier[2] * left_factor[..., None] + latter[2] * right_factor[..., None]
    return (peak, weight_sum, summed)


def score_block(queries, prompt_key, head_count, score_scale):
    key_heads = prompt_key.reshape(prompt_key.shape[0], head_count, -1)
    return (
        jnp.einsum("nhd,phd->nhp", queries, key_heads, preferred_element_type=jnp.float32)
        * score_scale
    )


def weigh_values(scores, peak, prompt_value, head_count):
    value_heads = prompt_value.reshape(prompt_value.shape[0], head_count, -1)
    weights = jnp.exp(scores - peak[..., None])
    weight_sum = jnp.sum(weights, axis=-1)
    summed = jnp.einsum(
        "nhp,phd->nhd",
        weights.astype(jnp.bfloat16),
        value_heads,
        preferred_element_type=jnp.float32,
    )
    return (weight_sum, summed)


def body(gen_ids, embed_rows, w_query, w_key, w_value, w_out, prompt_keys, prompt_values):
    cands_all, step_count = gen_ids.shape
    seq_count = lax.axis_size("seq")
    seq_index = lax.axis_index("seq")
    local_width = w_query.shape[1]
    head_count = local_width // HD
    own_tokens = cands_all * step_count // seq_count
    cand_count = own_tokens // step_count
    score_scale = 1.0 / math.sqrt(HD)
    vocab_local = embed_rows.shape[0]
    shifted_ids = gen_ids.reshape(-1) - lax.axis_index("head") * vocab_local
    selector = (shifted_ids[:, None] == jnp.arange(vocab_local, dtype=jnp.int32)[None, :]).astype(
        jnp.bfloat16
    )
    picked = jnp.dot(selector, embed_rows, preferred_element_type=jnp.float32)
    embedded = lax.psum(picked.astype(jnp.bfloat16), "head")
    stacked = jnp.concatenate([w_query, w_key, w_value], axis=1)
    projected = lax.psum_scatter(
        jnp.dot(embedded, stacked, preferred_element_type=jnp.float32),
        "seq",
        scatter_dimension=0,
        tiled=True,
    )
    positions = prompt_keys.shape[0] * seq_count + jnp.arange(step_count, dtype=jnp.int32)
    shaped = projected.reshape(cand_count, step_count, 3, head_count, HD)
    queries = rotate(shaped[:, :, 0], positions).astype(jnp.bfloat16)
    gen_keys = rotate(shaped[:, :, 1], positions).astype(jnp.bfloat16)
    gen_values = shaped[:, :, 2].astype(jnp.bfloat16)
    causal = jnp.arange(step_count)[None, :] <= jnp.arange(step_count)[:, None]
    own_scores = (
        jnp.einsum("cshd,cthd->csht", queries, gen_keys, preferred_element_type=jnp.float32)
        * score_scale
    )
    own_scores = jnp.where(causal[None, :, None, :], own_scores, -jnp.inf)
    own_peak = jnp.max(own_scores, axis=-1)
    own_weights = jnp.exp(own_scores - own_peak[..., None])
    own_sum = jnp.sum(own_weights, axis=-1)
    own_summed = jnp.einsum(
        "csht,cthd->cshd",
        own_weights.astype(jnp.bfloat16),
        gen_values,
        preferred_element_type=jnp.float32,
    )
    own_part = (
        own_peak.reshape(own_tokens, head_count),
        own_sum.reshape(own_tokens, head_count),
        own_summed.reshape(own_tokens, head_count, HD),
    )
    flat_queries = queries.reshape(own_tokens, head_count, HD)
    all_queries = lax.all_gather(flat_queries, "seq", axis=0, tiled=True)
    scores = score_block(all_queries, prompt_keys, head_count, score_scale)
    peak = jnp.max(scores, axis=-1)
    weight_sum, summed = weigh_values(scores, peak, prompt_values, head_count)
    merged = combined_all((peak, weight_sum, summed), "seq", joined)
    prompt_result = tuple(
        (
            lax.dynamic_slice_in_dim(member, seq_index * own_tokens, own_tokens, 0)
            for member in merged
        )
    )
    final_peak, final_sum, final_summed = joined(prompt_result, own_part)
    attended = (
        (final_summed / final_sum[..., None]).astype(jnp.bfloat16).reshape(own_tokens, local_width)
    )
    partials = jnp.dot(
        attended,
        lax.all_gather(w_out, "seq", axis=1, tiled=True),
        preferred_element_type=jnp.float32,
    )
    attn_out = lax.psum_scatter(
        partials.astype(jnp.bfloat16), "head", scatter_dimension=1, tiled=True
    )
    return attn_out


def solution(mesh):
    return jax.shard_map(
        body,
        mesh=mesh,
        in_specs=(
            P(),
            P("head", "seq"),
            P("seq", "head"),
            P("seq", "head"),
            P("seq", "head"),
            P("head", "seq"),
            P("seq", "head"),
            P("seq", "head"),
        ),
        out_specs=P("seq", "head"),
        check_vma=False,
    )
```

profile of v0, /device:TPU:0, one launch (start us, length us, event | category | flops | bytes accessed | tf_op | source)
XLA Modules:
  0.0 324.3 jit_solution(1242996104551373258)
XLA Ops:
  6.5 0.0 copy-start
  6.5 0.0 all-reduce.2.cloned.1.call-start
  6.5 0.8 broadcast_subtract_fusion
  7.3 0.1 sub.63
  7.4 3.8 %convolution_convert_fusion.1 = bf16[64,2048]{1,0:T(8,128)(2,1)} fusion(bf16[1024,2048]{1,0:T(8,128)(2,1)} %param.11, s32[64]{0:T(128)S(1)} %sub.63), kind=kOutput, calls=%fused_computation.17 | convolution fusion | flops 268632064 | bytes 4456704 | tf_op jit(solution)/shard_map/dot_general | solution.py:79
  11.2 0.0 all-reduce.2.cloned.1.call-update
  11.2 0.0 copy-start.1
  11.2 0.0 reduce-scatter.3.cloned.1.call-start
  11.2 73.4 %all-reduce.2.cloned.1.call-done = bf16[64,2048]{1,0:T(8,128)(2,1)} async-done(((bf16[64,2048]{1,0:T(8,128)(2,1)}), bf16[64,2048]{1,0:T(8,128)(2,1)}) %all-reduce.2.cloned.1.call-update) | async-done | bytes 262160 | tf_op jit(solution)/shard_map/psum | solution.py:80
  84.6 6.9 %fusion.4 = f32[64,3072]{1,0:T(8,128)} fusion(bf16[64,2048]{1,0:T(8,128)(2,1)} %all-reduce.2.cloned.1.call-done, bf16[2048,1024]{1,0:T(8,128)(2,1)} %param.14, bf16[2048,1024]{1,0:T(8,128)(2,1)} %param.13, bf16[2048,1024]{1,0:T(8,128)(2,1)} %param.12), kind=kOutput, calls=%fused_computation.10 | convolution fusion | flops 843055104 | bytes 13631488 | tf_op jit(solution)/shard_map/dot_general | solution.py:83
  91.5 0.0 reduce-scatter.3.cloned.1.call-update
  91.5 0.0 all-gather.10.cloned.1.call-start
  91.6 0.1 multiply_cosine_fusion
  91.7 22.5 %reduce-scatter.3.cloned.1.call-done = f32[16,3072]{1,0:T(8,128)} async-done(((f32[64,3072]{1,0:T(8,128)}), f32[16,3072]{1,0:T(8,128)}) %reduce-scatter.3.cloned.1.call-update) | async-done | bytes 196624 | tf_op jit(solution)/shard_map/reduce_scatter | solution.py:82
  114.2 1.0 copy.52
  115.3 0.1 fusion.33
  115.4 0.1 pad_maximum_fusion
  115.5 5.4 %all_gather.24 = bf16[64,8,128]{2,0,1:T(8,128)(2,1)S(1)} all-gather(bf16[16,8,128]{2,0,1:T(8,128)(2,1)S(1)} %pad_maximum_fusion), channel_id=1, replica_groups=mesh['seq'=4,'head'=8] {'seq'}, dimensions={0}, use_global_device_ids=true | all-gather | bytes 163840 | tf_op jit(solution)/shard_map/all_gather | solution.py:114
  120.9 0.0 copy-done
  120.9 0.6 fusion.51
  121.5 0.0 copy-done.1
  121.5 1.2 convolution_bitcast_fusion
  122.7 0.0 all-gather.10.cloned.1.call-update
  122.7 0.0 all-gather.8.cloned.1.call-start
  122.7 0.5 all-gather.8.cloned.1.call-update
  123.3 0.0 reduce-scatter.5.cloned.1.call-start
  123.3 0.4 fusion.23
  123.7 5.2 %all-gather.4 = f32[4,64,8]{1,2,0:T(8,128)S(1)} all-gather(f32[1,64,8]{1,2,0:T(8,128)S(1)} %bitcast.106), channel_id=3, replica_groups=mesh['seq'=4,'head'=8] {'seq'}, dimensions={0}, use_global_device_ids=true | all-gather | bytes 10240 | tf_op jit(solution)/shard_map/all_gather | solution.py:12
  128.9 5.2 %all-gather.3 = f32[4,64,8]{1,2,0:T(8,128)S(1)} all-gather(f32[1,64,8]{1,2,0:T(8,128)S(1)} %bitcast.105), channel_id=2, replica_groups=mesh['seq'=4,'head'=8] {'seq'}, dimensions={0}, use_global_device_ids=true | all-gather | bytes 10240 | tf_op jit(solution)/shard_map/all_gather | solution.py:12
  134.1 0.2 fusion.52
  134.3 5.3 %all-gather.10.cloned.1.call-done = f32[256,8,128]{2,0,1:T(8,128)} async-done(((f32[64,8,128]{2,0,1:T(8,128)}), f32[256,8,128]{2,0,1:T(8,128)}) %all-gather.10.cloned.1.call-update) | async-done | bytes 1048592 | tf_op jit(solution)/shard_map/all_gather | solution.py:12
  139.6 1.0 slice.42
  140.6 0.2 copy.37
  140.8 4.5 %while.19 = (s32[]{:T(128)}, f32[64,8]{0,1:T(8,128)S(1)}, f32[64,8]{0,1:T(8,128)S(1)}, f32[64,8,128]{2,1,0:T(8,128)S(1)}, f32[4,64,8]{1,2,0:T(8,128)S(1)}, /*ind...) while((s32[]{:T(128)}, f32[64,8]{0,1:T(8,128)S(1)}, ...), condition=%wide.region_5.6_spmd, body=%wide.region_4.5_spmd.sunk | while | flops 199685 | bytes 1339543 | solution.py:17
  140.8 0.1 copy.82
  140.9 0.1 copy.83
  141.0 1.0 constant_dynamic-slice_fusion.2
  142.0 0.3 fusion.63
  142.3 0.1 copy.82
  142.4 0.1 copy.83
  142.5 1.0 constant_dynamic-slice_fusion.2
  143.5 0.3 fusion.63
  143.8 0.1 copy.82
  143.9 0.1 copy.83
  144.0 1.0 constant_dynamic-slice_fusion.2
  144.9 0.3 fusion.63
  145.3 0.1 copy.39
  145.3 0.1 multiply_add_fusion
  145.4 0.2 fusion.17
  145.6 101.4 %all-gather.8.cloned.1.call-done = bf16[1024,8192]{1,0:T(8,128)(2,1)} async-done(((bf16[1024,2048]{1,0:T(8,128)(2,1)}), bf16[1024,8192]{1,0:T(8,128)(2,1)}) %all-gather.8.cloned.1.call-update) | async-done | bytes 16777232 | tf_op jit(solution)/shard_map/all_gather | solution.py:131
  247.0 8.8 %convolution_convert_fusion = bf16[16,8192]{1,0:T(8,128)(2,1)} fusion(bf16[1024,8192]{1,0:T(8,128)(2,1)} %all-gather.8.cloned.1.call-done, bf16[8,2,8,128]{3,2,1,0:T(8,128)(2,1)S(1)} %fusion.17), kind=kOutput, calls=%fused_computation.16 | convolution fusion | flops 268566528 | bytes 17072128 | tf_op jit(solution)/shard_map/dot_general | solution.py:129
  255.8 0.0 reduce-scatter.5.cloned.1.call-update
  255.8 62.0 %reduce-scatter.5.cloned.1.call-done = bf16[16,1024]{1,0:T(8,128)(2,1)} async-done(((bf16[16,8192]{1,0:T(8,128)(2,1)}), bf16[16,1024]{1,0:T(8,128)(2,1)}) %reduce-scatter.5.cloned.1.call-update) | async-done | bytes 32784 | tf_op jit(solution)/shard_map/reduce_scatter | solution.py:134
  (12 shorter events, 0.2 us)
Async XLA Ops:
  6.5 114.4 %copy-start = (bf16[512,1024]{1,0:T(8,128)(2,1)S(1)}, bf16[512,1024]{1,0:T(8,128)(2,1)}, u32[]{:S(2)}) copy-start(bf16[512,1024]{1,0:T(8,128)(2,1)} %param.16) | copy-start | bytes 3145732
  6.5 78.1 %all-reduce.2.cloned.1.call-start = ((), (), s32[]{:S(2)}) async-start(), calls=%async_computation.2 | async-start | bytes 524288 | tf_op jit(solution)/shard_map/psum | solution.py:80
  11.2 110.3 %copy-start.1 = (bf16[512,1024]{1,0:T(8,128)(2,1)S(1)}, bf16[512,1024]{1,0:T(8,128)(2,1)}, u32[]{:S(2)}) copy-start(bf16[512,1024]{1,0:T(8,128)(2,1)} %param.17) | copy-start | bytes 3145732
  11.2 103.0 %reduce-scatter.3.cloned.1.call-start = ((), (), s32[]{:S(2)}) async-start(), calls=%async_computation.3 | async-start | bytes 983040 | tf_op jit(solution)/shard_map/reduce_scatter | solution.py:82
  91.5 48.1 %all-gather.10.cloned.1.call-start = ((), (), s32[]{:S(2)}) async-start(), calls=%async_computation.6 | async-start | bytes 1310720 | tf_op jit(solution)/shard_map/all_gather | solution.py:12
  122.7 124.4 %all-gather.8.cloned.1.call-start = ((), (), s32[]{:S(2)}) async-start(), calls=%async_computation.4 | async-start | bytes 20971520 | tf_op jit(solution)/shard_map/all_gather | solution.py:131
  123.3 194.5 %reduce-scatter.5.cloned.1.call-start = ((), (), s32[]{:S(2)}) async-start(), calls=%async_computation.5 | async-start | bytes 294912 | tf_op jit(solution)/shard_map/reduce_scatter | solution.py:134
Sparse Core Ops, SparseCore 0:
  11.3 73.2 all-reduce.1
  91.6 22.5 reduce-scatter.2
  122.8 16.7 all-gather.9
  141.1 105.9 all-gather.7
  255.9 61.7 reduce-scatter.4
where the time goes:
time: 325 us; the launch traced here: 324 us
  waiting for transfers between devices  265 us (82%)
  matrix products  21.6 us (7%)
  blocking collectives  15.8 us (5%)
  between operations  13.3 us (4%)
  local copies, waits for them, and re-layouts  5.7 us (2%)
    all_gather x1, waiting for transfers between devices, body(): lax.all_gather(w_out, 'seq', axis=1, tiled=True)  101 us
    psum x1, waiting for transfers between devices, body(): embedded = lax.psum(picked.astype(jnp.bfloat16), 'head')  73.4 us
    reduce_scatter x1, waiting for transfers between devices, body(): lax.psum_scatter(partials.astype(jnp.bfloat16), 'head', scatter_dimension...  62 us
    reduce_scatter x1, waiting for transfers between devices, body(): lax.psum_scatter(jnp.dot(embedded, stacked, preferred_element_type=jnp.fl...  22.5 us
    all_gather x2, blocking collectives, combined_all(): gathered = jax.tree.map(lambda a: lax.all_gather(a, axis), part)  10.4 us
    dot_general x1, matrix products, body(): jnp.dot(attended, lax.all_gather(w_out, 'seq', axis=1, tiled=True), prefe...  8.77 us
    dot_general x1, matrix products, body(): jnp.dot(embedded, stacked, preferred_element_type=jnp.float32)  6.87 us
  transfers between devices with their start and end apart: 5, of which 5 were waited for; matrix products, arithmetic and copies ran while one was open for 2% of the time, Pallas kernels for 0%

commit v1 on v0

v1 whole, which is shorter than its diff:
```python
import math

import jax
import jax.numpy as jnp
from jax import lax
from jax.experimental import pallas as pl
from jax.experimental.pallas import tpu as pltpu
from jax.sharding import PartitionSpec as P

HD = 128
CORES = 2
MIB = 1 << 20
BF16 = jnp.bfloat16
F32 = jnp.float32


class Plan:
    def __init__(self, mesh, gen_ids, w_query, w_out, prompt_keys):
        self.seq, self.head = mesh.shape["seq"], mesh.shape["head"]
        self.cands, self.steps = gen_ids.shape
        self.tokens = self.cands * self.steps
        self.features, self.width = w_query.shape
        self.prompt_rows = prompt_keys.shape[0]
        self.inner = math.gcd(self.head, 4)
        self.outer = self.head // self.inner
        self.inner_rows = self.tokens // self.inner
        self.half = self.width // CORES
        self.chips = self.seq // CORES
        self.parts = self.head // self.seq
        self.share = self.tokens // self.seq
        self.owned = self.tokens // self.chips
        self.columns = w_out.shape[1] // self.parts

    def send(self, value, route):
        pairs = []
        for s in range(self.seq):
            for h in range(self.head):
                to_s, to_h = route(s, h)
                if (to_s, to_h) != (s, h):
                    pairs.append((s * self.head + h, to_s * self.head + to_h))
        return lax.ppermute(value, ("seq", "head"), pairs)

    def over_seq(self, value, step):
        return self.send(value, lambda s, h: (s ^ step, h))

    def over_head(self, value, step):
        return self.send(value, lambda s, h: (s, h ^ step))


VMEM_SPEC = pl.BlockSpec(memory_space=pltpu.VMEM)
ANY_SPEC = pl.BlockSpec(memory_space=pl.ANY)


def aligned(index, size):
    return pl.ds(pl.multiple_of(index * size, size), size)


def in_hbm(value):
    return pltpu.with_memory_space_constraint(value, pltpu.HBM)


def call(kernel, out_shape, in_specs, out_specs, scratch, limit, *args, cost=None):
    return pl.pallas_call(
        kernel,
        out_shape=out_shape,
        in_specs=in_specs,
        out_specs=out_specs,
        scratch_shapes=scratch,
        cost_estimate=cost,
        compiler_params=pltpu.CompilerParams(vmem_limit_bytes=limit * MIB),
    )(*args)


def pick(plan, gen_ids, embed_rows):
    vocab = embed_rows.shape[0]
    rows, inner, steps = plan.inner_rows, plan.inner, plan.steps
    cut = 2 * HD
    pieces = vocab // cut

    def kernel(ids_ref, embed_ref, *refs):
        outs, (ids, held, found, ids_sem, sems) = refs[:inner], refs[inner:]
        ids_copy = pltpu.make_async_copy(ids_ref, ids, ids_sem)
        ids_copy.start()
        copies = []
        for piece in range(pieces):
            window = pl.ds(piece * cut, cut)
            copies.append(
                pltpu.make_async_copy(embed_ref.at[window], held.at[window], sems.at[piece])
            )
            copies[-1].start()
        head_index = lax.axis_index("head")
        mine = lax.rem(head_index, inner)
        diagonal = lax.broadcasted_iota(jnp.int32, (steps, steps), 0) == (
            lax.broadcasted_iota(jnp.int32, (steps, steps), 1)
        )
        lanes = lax.broadcasted_iota(jnp.int32, (steps, vocab), 1) + head_index * vocab
        lanes = lanes.astype(F32)
        ids_copy.wait()
        selectors = []
        for block in range(inner):
            for cand in range(rows // steps):
                row = ids[pl.ds((block ^ mine) * (rows // steps) + cand, 1), :].astype(F32)
                column = jnp.sum(jnp.where(diagonal, row, 0.0), axis=1, keepdims=True)
                selectors.append((column == lanes).astype(F32).astype(BF16))
        selector = jnp.concatenate(selectors)
        for piece, copy in enumerate(copies):
            window = slice(piece * cut, (piece + 1) * cut)
            copy.wait()
            part = jnp.dot(selector[:, window], held[window, :], preferred_element_type=F32)
            if piece:
                part = part + found[...]
            if piece < pieces - 1:
                found[...] = part
        for block in range(inner):
            outs[block][...] = part[block * rows : (block + 1) * rows].astype(BF16)

    out = jax.ShapeDtypeStruct((rows, plan.features), BF16)
    return call(
        kernel,
        [out] * inner,
        [ANY_SPEC] * 2,
        [VMEM_SPEC] * inner,
        [
            pltpu.VMEM(gen_ids.shape, jnp.int32),
            pltpu.VMEM(embed_rows.shape, BF16),
            pltpu.VMEM((plan.tokens, plan.features), F32),
            pltpu.SemaphoreType.DMA,
            pltpu.SemaphoreType.DMA((pieces,)),
        ],
        16,
        in_hbm(gen_ids),
        in_hbm(embed_rows),
    )


def bring(after, source):
    def kernel(_, source_ref, out_ref, sems):
        pieces = 4
        size = source.shape[0] // pieces
        copies = [
            pltpu.make_async_copy(
                source_ref.at[pl.ds(k * size, size)], out_ref.at[pl.ds(k * size, size)], sems.at[k]
            )
            for k in range(pieces)
        ]
        for copy in copies:
            copy.start()
        for copy in copies:
            copy.wait()

    return call(
        kernel,
        jax.ShapeDtypeStruct(source.shape, source.dtype),
        [ANY_SPEC] * 2,
        ANY_SPEC,
        [pltpu.SemaphoreType.DMA((4,))],
        4,
        after,
        in_hbm(source),
    )


def gather_embedded(plan, gen_ids, embed_rows, w_key, w_value):
    picked = pick(plan, gen_ids, embed_rows)
    order = list(range(1, plan.inner))[::-1]
    total = picked[0]
    for moved in [plan.over_head(picked[step], step) for step in order]:
        total = total + moved
    w_key = bring(total, w_key)
    whole = total
    for step in range(1, plan.outer):
        whole = whole + plan.over_head(total, step * plan.inner)
    whole, w_key = lax.optimization_barrier((whole, w_key))
    w_value = bring(whole, w_value)
    return [whole] + [plan.over_head(whole, step) for step in order], w_key, w_value


def prompt_half(plan, prompt_keys, prompt_values, other, *after):
    rows, half = plan.prompt_rows, plan.half

    def kernel(keys_ref, values_ref, *refs):
        out_ref, sems = refs[-2:]
        core = lax.rem(lax.axis_index("seq"), CORES)
        window = aligned(1 - core if other else core, half)
        copies = [
            pltpu.make_async_copy(
                source.at[:, window], out_ref.at[pl.ds(place * rows, rows)], sems.at[place]
            )
            for place, source in enumerate((keys_ref, values_ref))
        ]
        for copy in copies:
            copy.start()
        for copy in copies:
            copy.wait()

    return call(
        kernel,
        jax.ShapeDtypeStruct((2 * rows, half), BF16),
        [ANY_SPEC] * (2 + len(after)),
        ANY_SPEC,
        [pltpu.SemaphoreType.DMA((2,))],
        4,
        in_hbm(prompt_keys),
        in_hbm(prompt_values),
        *after,
    )


def project_half(plan, embedded, weights, other, dtype):
    rows, half = plan.inner_rows, plan.half

    def kernel(*refs):
        blocks, sources = refs[: plan.inner], refs[plan.inner : plan.inner + 3]
        out_ref, joined = refs[plan.inner + 3 :]
        core = lax.rem(lax.axis_index("seq"), CORES)
        mine = lax.rem(lax.axis_index("head"), plan.inner)
        for place, block in enumerate(blocks):
            distance = (plan.inner - place) % plan.inner
            joined[aligned(distance ^ mine, rows), :] = block[...]
        window = aligned(1 - core if other else core, half)
        for kind in range(3):
            product = jnp.dot(
                joined[...], sources[kind][:, window], preferred_element_type=F32
            )
            out_ref[:, kind * half : (kind + 1) * half] = product.astype(dtype)

    return call(
        kernel,
        jax.ShapeDtypeStruct((plan.tokens, 3 * half), dtype),
        [VMEM_SPEC] * (plan.inner + 3),
        VMEM_SPEC,
        [pltpu.VMEM((plan.tokens, plan.features), BF16)],
        16,
        *embedded,
        *weights,
    )


def sum_cores(plan, own, received):
    tokens, half, owned = plan.tokens, plan.half, plan.owned

    def kernel(own_ref, received_ref, *refs):
        outs, total = refs[: plan.chips], refs[plan.chips]
        total[...] = own_ref[...] + received_ref[...].astype(F32)
        chip = lax.axis_index("seq") // CORES
        for dy in range(plan.chips):
            out, rows = outs[dy], aligned(chip ^ dy, owned)
            out[:tokens] = total[:, :half].astype(out.dtype)
            out[tokens : tokens + owned] = total[rows, half : 2 * half].astype(out.dtype)
            out[tokens + owned :] = total[rows, 2 * half :].astype(out.dtype)

    shape = (tokens + 2 * owned, half)
    return call(
        kernel,
        [jax.ShapeDtypeStruct(shape, BF16 if dy else F32) for dy in range(plan.chips)],
        [VMEM_SPEC] * 2,
        [VMEM_SPEC] * plan.chips,
        [pltpu.VMEM((tokens, 3 * half), F32)],
        8,
        own,
        received,
    )


def project(plan, embedded, weights):
    received = plan.over_seq(project_half(plan, embedded, weights, True, BF16), 1)
    own = project_half(plan, embedded, weights, False, F32)
    parts = sum_cores(plan, own, received)
    return [parts[0]] + [plan.over_seq(parts[dy], dy * CORES) for dy in range(1, plan.chips)]


def angle_tables(plan):
    half_size = HD // 2
    frequency = 10000.0 ** (-jnp.arange(half_size, dtype=F32) / half_size)
    positions = plan.prompt_rows * plan.seq + jnp.arange(plan.steps, dtype=jnp.int32)
    angles = positions.astype(F32)[:, None] * frequency[None, :]
    cosine, sine_part = jnp.cos(angles), jnp.sin(angles)
    return (
        jnp.concatenate([cosine, cosine], axis=-1),
        jnp.concatenate([-sine_part, sine_part], axis=-1),
    )


def attend(plan, parts, kept, swapped, tables):
    tokens, half, owned, share = plan.tokens, plan.half, plan.owned, plan.share
    rows, heads = plan.prompt_rows, plan.half // HD
    scale = 1.0 / math.sqrt(HD)
    transposed = (((1,), (1,)), ((), ()))

    def kernel(*refs):
        sums, refs = refs[: plan.chips], refs[plan.chips :]
        kept_ref, swapped_ref, cosine_ref, sine_ref = refs[:4]
        near_ref, far_ref, result = refs[4:]
        core = lax.rem(lax.axis_index("seq"), CORES)
        chip = lax.axis_index("seq") // CORES
        total = sums[0][...]
        for dy in range(1, plan.chips):
            total = total + sums[dy][...].astype(F32)
        cosine, sine_part = cosine_ref[...][None], sine_ref[...][None]

        def rotated(vectors):
            turned = pltpu.roll(vectors, HD // 2, 1)
            shaped = vectors.reshape(-1, plan.steps, HD) * cosine
            shaped = shaped + turned.reshape(-1, plan.steps, HD) * sine_part
            return shaped.reshape(vectors.shape).astype(BF16)

        row = lax.broadcasted_iota(jnp.int32, (tokens, owned), 0)
        column = lax.broadcasted_iota(jnp.int32, (tokens, owned), 1) + chip * owned
        seen = (row // plan.steps == column // plan.steps) & (column <= row)
        lane = lax.broadcasted_iota(jnp.int32, (tokens, HD), 1)
        logs = jnp.zeros((tokens, HD), F32)
        for head in range(heads):
            lanes = slice(head * HD, (head + 1) * HD)
            query = rotated(total[:tokens, lanes])
            gen_key = rotated(total[tokens : tokens + owned, lanes])
            gen_value = total[tokens + owned :, lanes].astype(BF16)

            def score(key):
                return (
                    lax.dot_general(query, key, transposed, preferred_element_type=F32) * scale
                )

            scores = [
                score(kept_ref[:rows, lanes]),
                score(swapped_ref[:rows, lanes]),
                jnp.where(seen, score(gen_key), -jnp.inf),
            ]
            held = [kept_ref[rows:, lanes], swapped_ref[rows:, lanes], gen_value]
            peak = jnp.max(scores[0], axis=1, keepdims=True)
            for part in scores[1:]:
                peak = jnp.maximum(peak, jnp.max(part, axis=1, keepdims=True))
            weight_sum, summed = 0.0, 0.0
            for part, value in zip(scores, held):
                weight = jnp.exp(part - peak)
                weight_sum = weight_sum + jnp.sum(weight, axis=1, keepdims=True)
                summed = summed + jnp.dot(
                    weight.astype(BF16), value, preferred_element_type=F32
                )
            result[:, lanes] = (summed / weight_sum).astype(BF16)
            rest = peak + jnp.log(weight_sum)
            for term in range(3):
                piece = rest.astype(BF16).astype(F32)
                rest = rest - piece
                logs = jnp.where(lane == 3 * head + term, piece, logs)
        result[:, half:] = logs.astype(BF16)
        for pair in range(plan.chips):
            place = pl.ds(pair * share, share)
            near_ref[place, :] = result[aligned(pair * CORES + core, share), :]
            far_ref[place, :] = result[aligned(pair * CORES + 1 - core, share), :]

    out = jax.ShapeDtypeStruct((tokens // CORES, half + HD), BF16)
    near, far = call(
        kernel,
        [out] * 2,
        [VMEM_SPEC] * (plan.chips + 4),
        [VMEM_SPEC] * 2,
        [pltpu.VMEM((tokens, half + HD), BF16)],
        24,
        *parts,
        kept,
        swapped,
        *tables,
    )
    got = {k: plan.over_seq(far if k % CORES else near, k) for k in range(1, plan.seq)}
    return [near] + [got[k] for k in range(1, plan.seq)]


def multiply_out(plan, attended, own, swapped):
    half, columns = plan.half, plan.columns
    rows = plan.tokens // CORES
    keys = [(dq, dx) for dq in range(CORES) for dx in range(plan.parts)]

    def kernel(*refs):
        parts, refs = refs[: plan.seq], refs[plan.seq :]
        (own_ref, swapped_ref), refs = refs[:2], refs[2:]
        outs, (joined,) = dict(zip(keys, refs)), refs[len(keys) :]
        core = lax.rem(lax.axis_index("seq"), CORES)
        head_index = lax.axis_index("head")
        part_index = lax.rem(head_index, plan.parts)
        block = lax.rem(head_index // plan.parts, CORES)
        for side in range(CORES):
            sources = [parts[step] for step in range(side, plan.seq, CORES)]
            first = (core ^ side) * half
            for head in range(half // HD):
                lanes = slice(head * HD, (head + 1) * HD)
                logs = [
                    sum(
                        source[:, half + 3 * head + term : half + 3 * head + term + 1].astype(F32)
                        for term in (2, 1, 0)
                    )
                    for source in sources
                ]
                top = logs[0]
                for one in logs[1:]:
                    top = jnp.maximum(top, one)
                scales = [jnp.exp(one - top) for one in logs]
                mixed = sum(f * source[:, lanes].astype(F32) for f, source in zip(scales, sources))
                mixed = (mixed / sum(scales)).astype(BF16)
                joined[:, pl.ds(pl.multiple_of(first + head * HD, HD), HD)] = mixed
        left = joined[...]

        def multiply(*weights):
            for dq, dx in keys[::-1]:
                weight = weights[dq][:, aligned(part_index ^ dx, columns)]
                product = jnp.dot(left, weight, preferred_element_type=F32)
                outs[dq, dx][...] = product.astype(outs[dq, dx].dtype)

        @pl.when(block == core)
        def _():
            multiply(own_ref, swapped_ref)

        @pl.when(block != core)
        def _():
            multiply(swapped_ref, own_ref)

    shape = (rows, columns)
    made = call(
        kernel,
        [jax.ShapeDtypeStruct(shape, BF16 if any(key) else F32) for key in keys],
        [VMEM_SPEC] * (plan.seq + 2),
        [VMEM_SPEC] * len(keys),
        [pltpu.VMEM((rows, plan.width), BF16)],
        24,
        *attended,
        own,
        swapped,
    )
    got = [
        plan.send(value, lambda s, h: (s, h ^ (dq * plan.parts + dx)))
        for (dq, dx), value in list(zip(keys, made))[:0:-1]
    ]
    return [made[0]] + got


def sum_parts(plan, got):
    shape = (plan.share, plan.columns)

    def kernel(*refs):
        ins, outs, held = refs[: len(got)], refs[len(got) : -1], refs[-1]
        total = ins[0][...]
        for ref in ins[1:]:
            total = total + ref[...].astype(F32)
        held[...] = total
        group = lax.axis_index("head") // (plan.parts * CORES)
        for step in range(plan.chips):
            outs[step][...] = held[aligned(group ^ step, plan.share), :].astype(BF16)

    made = call(
        kernel,
        [jax.ShapeDtypeStruct(shape, BF16)] * plan.chips,
        [VMEM_SPEC] * len(got),
        [VMEM_SPEC] * plan.chips,
        [pltpu.VMEM((plan.chips * plan.share, plan.columns), F32)],
        16,
        *got,
    )
    size = plan.parts * CORES

    def moved(step):
        def route(s, h):
            return (h // size ^ step) * CORES + s % CORES, s // CORES * size + h % size

        return plan.send(made[step], route)

    def last(own_ref, *refs):
        chip, group = lax.axis_index("seq") // CORES, lax.axis_index("head") // size
        total = jnp.zeros(shape, F32)
        for ref in refs[:-1]:
            total = total + ref[...].astype(F32)
        total = total + jnp.where(chip == group, own_ref[...].astype(F32), 0.0)
        refs[-1][...] = total.astype(BF16)

    return call(
        last,
        jax.ShapeDtypeStruct(shape, BF16),
        [VMEM_SPEC] * (plan.chips + 1),
        VMEM_SPEC,
        [],
        8,
        made[0],
        *[moved(step) for step in range(plan.chips)],
    )


def solution(mesh):
    def body(gen_ids, embed_rows, w_query, w_key, w_value, w_out, prompt_keys, prompt_values):
        plan = Plan(mesh, gen_ids, w_query, w_out, prompt_keys)
        embedded, w_key, w_value = gather_embedded(plan, gen_ids, embed_rows, w_key, w_value)
        swapped_out = plan.over_seq(w_out, 1)
        swapped = plan.over_seq(prompt_half(plan, prompt_keys, prompt_values, True), 1)
        parts = project(plan, embedded, (w_query, w_key, w_value))
        kept = prompt_half(plan, prompt_keys, prompt_values, False, parts[0])
        attended = attend(plan, parts, kept, swapped, angle_tables(plan))
        return sum_parts(plan, multiply_out(plan, attended, w_out, swapped_out))

    return jax.shard_map(
        body,
        mesh=mesh,
        in_specs=(
            P(),
            P("head", "seq"),
            P("seq", "head"),
            P("seq", "head"),
            P("seq", "head"),
            P("head", "seq"),
            P("seq", "head"),
            P("seq", "head"),
        ),
        out_specs=P("seq", "head"),
        check_vma=False,
    )
```

time: 325 us -> 57.8 us (0.18)
  waiting for transfers between devices: 265 us -> 17.3 us
  starting transfers between devices: 0.17 us -> 23.6 us
  matrix products: 21.6 us -> 0 us
  Pallas kernels: 0 us -> 16.3 us
  blocking collectives: 15.8 us -> 0 us
  between operations: 13.3 us -> 0.16 us
  local copies, waits for them, and re-layouts: 5.7 us -> 0.01 us
    all_gather x2 -> x0, waiting for transfers between devices: 107 us -> none  [the longest x1 101 us: body(): lax.all_gather(w_out, 'seq', axis=1, tiled=True)]
    reduce_scatter x2 -> x0, waiting for transfers between devices: 84.5 us -> none  [the longest x1 62 us: body(): lax.psum_scatter(partials.astype(jnp.bfloat16), 'head', scatter_dimension...]
    psum x1 -> x0, waiting for transfers between devices: 73.4 us -> none  [body(): embedded = lax.psum(picked.astype(jnp.bfloat16), 'head')]
    ppermute x0 -> x19, starting transfers between devices: none -> 23.6 us  [send(): return lax.ppermute(value, ('seq', 'head'), pairs)]
    dot_general x7 -> x0, matrix products: 21.6 us -> none  [the longest x1 8.77 us: body(): jnp.dot(attended, lax.all_gather(w_out, 'seq', axis=1, tiled=True), prefe...]
    ppermute x0 -> x19, waiting for transfers between devices: none -> 17.3 us  [send(): return lax.ppermute(value, ('seq', 'head'), pairs)]
    pallas_call x0 -> x12, Pallas kernels: none -> 16.3 us  [call(): pl.pallas_call(kernel, out_shape=out_shape, in_specs=in_specs, out_specs=...]
    all_gather x3 -> x0, blocking collectives: 15.8 us -> none  [the longest x2 10.4 us: combined_all(): gathered = jax.tree.map(lambda a: lax.all_gather(a, axis), part)]
  transfers between devices with their start and end apart: 5 -> 19, of which waited for: 5 -> 13; matrix products, arithmetic and copies ran while one was open for 2% -> 0% of each run, Pallas kernels for 0% -> 24%
where the time goes in v1:
time: 57.8 us; the launch traced here: 57.6 us
  starting transfers between devices  23.6 us (41%)
  waiting for transfers between devices  17.3 us (30%)
  Pallas kernels  16.3 us (28%)
    ppermute x19, starting transfers between devices, send(): return lax.ppermute(value, ('seq', 'head'), pairs)  23.6 us
    ppermute x19, waiting for transfers between devices, send(): return lax.ppermute(value, ('seq', 'head'), pairs)  17.3 us
    pallas_call x12, Pallas kernels, call(): pl.pallas_call(kernel, out_shape=out_shape, in_specs=in_specs, out_specs=...  16.3 us
  transfers between devices with their start and end apart: 19, of which 13 were waited for; matrix products, arithmetic and copies ran while one was open for 0% of the time, Pallas kernels for 24%

profile of v1, /device:TPU:0, one launch (start us, length us, event | category | flops | bytes accessed | tf_op | source)
XLA Modules:
  0.0 57.6 jit_solution(11037284924641233224)
XLA Ops:
  0.0 0.5 collective-permute-start.13
  0.5 2.7 %shard_map.82 = (bf16[16,2048]{1,0:T(8,128)(2,1)S(1)}, bf16[16,2048]{1,0:T(8,128)(2,1)S(1)}, bf16[16,2048]{1,0:T(8,128)(2,1)S(1)}, bf16[16,2048]{1,0:T(8,128)(2,1)S(1)}) custom-call(s32[4,16]{1,0:T(4,128)} %ids_ref.1, bf16[1024,2048]{1,0:T(8,128)(2,1)} %embed_ref.1), custom_call_target="tpu_custom_call" | custom-call | tf_op jit(solution)/shard_map/pallas_call | solution.py:63
  3.1 3.6 %collective-permute-start = (bf16[16,2048]{1,0:T(8,128)(2,1)S(1)}, bf16[16,2048]{1,0:T(8,128)(2,1)S(1)}, u32[]{:S(2)}, u32[]{:S(2)}) collective-permute-start(bf16[16,2048]{1,0:T(8,128)(2,1)S(1)} %get-tuple-element.22), channel_id=1, source_target_pairs={{0,3},{1,2},{2,1},{3,0},{4,7},{5,6},{6,5},{7,4},{8,11},{9,10},{10,... | collective-permute-start | bytes 196616 | tf_op jit(solution)/shard_map/ppermute | solution.py:41
  6.7 0.4 collective-permute-start.1
  7.1 0.2 collective-permute-start.2
  7.3 1.2 %shard_map.89 = bf16[1024,512]{1,0:T(8,128)(2,1)S(1)} custom-call(bf16[512,1024]{1,0:T(8,128)(2,1)} %keys_ref.3, bf16[512,1024]{1,0:T(8,128)(2,1)} %values_ref.3), custom_call_target="tpu_custom_call" | custom-call | tf_op jit(solution)/shard_map/pallas_call | solution.py:63
  8.5 0.1 collective-permute-start.9
  8.6 0.8 %collective-permute-done = bf16[16,2048]{1,0:T(8,128)(2,1)S(1)} collective-permute-done((bf16[16,2048]{1,0:T(8,128)(2,1)S(1)}, bf16[16,2048]{1,0:T(8,128)(2,1)S(1)}, u32[]{:S(2)}, u32[]{:S(2)}) %collective-permute-start) | collective-permute-done | bytes 65568 | tf_op jit(solution)/shard_map/ppermute | solution.py:41
  9.4 1.6 %collective-permute-done.1 = bf16[16,2048]{1,0:T(8,128)(2,1)S(1)} collective-permute-done((bf16[16,2048]{1,0:T(8,128)(2,1)S(1)}, bf16[16,2048]{1,0:T(8,128)(2,1)S(1)}, u32[]{:S(2)}, u32[]{:S(2)}) %collective-permute-start.1) | collective-permute-done | bytes 65568 | tf_op jit(solution)/shard_map/ppermute | solution.py:41
  11.0 0.4 collective-permute-done.2
  11.4 2.7 %collective-permute-start.3 = (bf16[16,2048]{1,0:T(8,128)(2,1)S(1)}, bf16[16,2048]{1,0:T(8,128)(2,1)S(1)}, u32[]{:S(2)}, u32[]{:S(2)}) collective-permute-start(bf16[16,2048]{1,0:T(8,128)(2,1)S(1)} %add_add_fusion._), channel_id=1, source_target_pairs={{0,4},{1,5},{2,6},{3,7},{4,0},{5,1},{6,2},{7,3},{8,12},{9,13},{10,... | collective-permute-start | bytes 196616 | tf_op jit(solution)/shard_map/ppermute | solution.py:41
  14.1 2.2 %shard_map.83.refs_5_ = bf16[2048,1024]{1,0:T(8,128)(2,1)S(1)} custom-call(bf16[16,2048]{1,0:T(8,128)(2,1)S(1)} %add_add_fusion._, bf16[2048,1024]{1,0:T(8,128)(2,1)} %source_ref.2), custom_call_target="tpu_custom_call" | custom-call | tf_op jit(solution)/shard_map/pallas_call | solution.py:63
  16.3 0.5 collective-permute-done.3
  16.8 0.0 copy-start
  16.8 2.2 %collective-permute-start.4 = (bf16[16,2048]{1,0:T(8,128)(2,1)S(1)}, bf16[16,2048]{1,0:T(8,128)(2,1)S(1)}, u32[]{:S(2)}, u32[]{:S(2)}) collective-permute-start(bf16[16,2048]{1,0:T(8,128)(2,1)S(1)} %add.28._.refs_0_), channel_id=1, source_target_pairs={{0,3},{1,2},{2,1},{3,0},{4,7},{5,6},{6,5},{7,4},{8,11},{9,10},{10,... | collective-permute-start | bytes 196616 | tf_op jit(solution)/shard_map/ppermute | solution.py:41
  19.0 1.6 %collective-permute-start.5 = (bf16[16,2048]{1,0:T(8,128)(2,1)S(1)}, bf16[16,2048]{1,0:T(8,128)(2,1)S(1)}, u32[]{:S(2)}, u32[]{:S(2)}) collective-permute-start(bf16[16,2048]{1,0:T(8,128)(2,1)S(1)} %add.28._.refs_0_), channel_id=1, source_target_pairs={{0,2},{1,3},{2,0},{3,1},{4,6},{5,7},{6,4},{7,5},{8,10},{9,11},{10,... | collective-permute-start | bytes 196616 | tf_op jit(solution)/shard_map/ppermute | solution.py:41
  20.6 0.0 collective-permute-start.6
  20.6 2.2 %shard_map.84.refs_6_ = bf16[2048,1024]{1,0:T(8,128)(2,1)S(1)} custom-call(bf16[16,2048]{1,0:T(8,128)(2,1)S(1)} %add.28._.refs_0_, bf16[2048,1024]{1,0:T(8,128)(2,1)} %source_ref.3), custom_call_target="tpu_custom_call" | custom-call | tf_op jit(solution)/shard_map/pallas_call | solution.py:63
  22.8 0.0 collective-permute-done.4.refs_1_
  22.8 0.7 %collective-permute-done.5.refs_2_ = bf16[16,2048]{1,0:T(8,128)(2,1)S(1)} collective-permute-done((bf16[16,2048]{1,0:T(8,128)(2,1)S(1)}, bf16[16,2048]{1,0:T(8,128)(2,1)S(1)}, u32[]{:S(2)}, u32[]{:S(2)}) %collective-permute-start.5) | collective-permute-done | bytes 65568 | tf_op jit(solution)/shard_map/ppermute | solution.py:41
  23.5 1.3 %collective-permute-done.6.refs_3_ = bf16[16,2048]{1,0:T(8,128)(2,1)S(1)} collective-permute-done((bf16[16,2048]{1,0:T(8,128)(2,1)S(1)}, bf16[16,2048]{1,0:T(8,128)(2,1)S(1)}, u32[]{:S(2)}, u32[]{:S(2)}) %collective-permute-start.6) | collective-permute-done | bytes 65568 | tf_op jit(solution)/shard_map/ppermute | solution.py:41
  24.8 0.0 copy-done
  24.8 1.2 %shard_map.86 = bf16[64,1536]{1,0:T(8,128)(2,1)S(1)} custom-call(bf16[16,2048]{1,0:T(8,128)(2,1)S(1)} %add.28._.refs_0_, bf16[16,2048]{1,0:T(8,128)(2,1)S(1)} %collective-permute-done.4.refs_1_, bf16[16,2048]{1,0:T(8,128)(2,1)S(1)} %collective-permute-done.5.refs_2_, bf16[16,2048]{1,0:T(8,128)(2,1)S(1)} %collective-permute-done.6.refs_3_, ...), custom_call_target="tpu_custom_call" | custom-call | tf_op jit(solution)/shard_map/pallas_call | solution.py:63
  26.1 0.1 collective-permute-start.7
  26.2 1.2 %shard_map.85.own_ref = f32[64,1536]{1,0:T(8,128)S(1)} custom-call(bf16[16,2048]{1,0:T(8,128)(2,1)S(1)} %add.28._.refs_0_, bf16[16,2048]{1,0:T(8,128)(2,1)S(1)} %collective-permute-done.4.refs_1_, bf16[16,2048]{1,0:T(8,128)(2,1)S(1)} %collective-permute-done.5.refs_2_, bf16[16,2048]{1,0:T(8,128)(2,1)S(1)} %collective-permute-done.6.refs_3_, ...), custom_call_target="tpu_custom_call" | custom-call | tf_op jit(solution)/shard_map/pallas_call | solution.py:63
  27.4 0.0 copy-start.1
  27.4 0.2 collective-permute-done.7.received_ref
  27.6 0.1 shard_map.87
  27.7 1.6 %collective-permute-start.8 = (bf16[128,512]{1,0:T(8,128)(2,1)S(1)}, bf16[128,512]{1,0:T(8,128)(2,1)S(1)}, u32[]{:S(2)}, u32[]{:S(2)}) collective-permute-start(bf16[128,512]{1,0:T(8,128)(2,1)S(1)} %get-tuple-element.28), channel_id=1, source_target_pairs={{0,16},{1,17},{2,18},{3,19},{4,20},{5,21},{6,22},{7,23},{8,24},{9,... | collective-permute-start | bytes 393224 | tf_op jit(solution)/shard_map/ppermute | solution.py:41
  29.3 0.1 fusion
  29.4 0.1 pad_maximum_fusion
  29.5 1.2 %shard_map.88.refs_2_ = bf16[1024,512]{1,0:T(8,128)(2,1)S(1)} custom-call(bf16[512,1024]{1,0:T(8,128)(2,1)} %keys_ref.3, bf16[512,1024]{1,0:T(8,128)(2,1)} %values_ref.3, f32[128,512]{1,0:T(8,128)S(1)} %get-tuple-element.27.refs_0_), custom_call_target="tpu_custom_call" | custom-call | tf_op jit(solution)/shard_map/pallas_call | solution.py:63
  30.7 2.8 %collective-permute-done.8.refs_1_ = bf16[128,512]{1,0:T(8,128)(2,1)S(1)} collective-permute-done((bf16[128,512]{1,0:T(8,128)(2,1)S(1)}, bf16[128,512]{1,0:T(8,128)(2,1)S(1)}, u32[]{:S(2)}, u32[]{:S(2)}) %collective-permute-start.8) | collective-permute-done | bytes 131104 | tf_op jit(solution)/shard_map/ppermute | solution.py:41
  33.5 0.0 collective-permute-done.9.refs_3_
  33.5 1.6 %shard_map.90 = (bf16[32,640]{1,0:T(8,128)(2,1)S(1)}, bf16[32,640]{1,0:T(8,128)(2,1)S(1)}) custom-call(f32[128,512]{1,0:T(8,128)S(1)} %get-tuple-element.27.refs_0_, bf16[128,512]{1,0:T(8,128)(2,1)S(1)} %collective-permute-done.8.refs_1_, bf16[1024,512]{1,0:T(8,128)(2,1)S(1)} %shard_map.88.refs_2_, bf16[1024,512]{1,0:T(8,128)(2,1)S(1)} %collective-permute-done.9.refs_3_, ...), custom_call_target="tpu_custom_call" | custom-call | tf_op jit(solution)/shard_map/pallas_call | solution.py:63
  35.1 0.1 collective-permute-start.10
  35.1 1.6 %collective-permute-start.11 = (bf16[32,640]{1,0:T(8,128)(2,1)S(1)}, bf16[32,640]{1,0:T(8,128)(2,1)S(1)}, u32[]{:S(2)}, u32[]{:S(2)}) collective-permute-start(bf16[32,640]{1,0:T(8,128)(2,1)S(1)} %get-tuple-element.29.refs_0_), channel_id=1, source_target_pairs={{0,16},{1,17},{2,18},{3,19},{4,20},{5,21},{6,22},{7,23},{8,24},{9,... | collective-permute-start | bytes 122888 | tf_op jit(solution)/shard_map/ppermute | solution.py:41
  36.7 0.3 collective-permute-start.12
  37.0 0.0 collective-permute-done.10.refs_1_
  37.0 2.2 %collective-permute-done.11.refs_2_ = bf16[32,640]{1,0:T(8,128)(2,1)S(1)} collective-permute-done((bf16[32,640]{1,0:T(8,128)(2,1)S(1)}, bf16[32,640]{1,0:T(8,128)(2,1)S(1)}, u32[]{:S(2)}, u32[]{:S(2)}) %collective-permute-start.11) | collective-permute-done | bytes 40992 | tf_op jit(solution)/shard_map/ppermute | solution.py:41
  39.2 1.0 %collective-permute-done.12.refs_3_ = bf16[32,640]{1,0:T(8,128)(2,1)S(1)} collective-permute-done((bf16[32,640]{1,0:T(8,128)(2,1)S(1)}, bf16[32,640]{1,0:T(8,128)(2,1)S(1)}, u32[]{:S(2)}, u32[]{:S(2)}) %collective-permute-start.12) | collective-permute-done | bytes 40992 | tf_op jit(solution)/shard_map/ppermute | solution.py:41
  40.3 0.0 collective-permute-done.13.refs_5_
  40.3 0.0 copy-done.1
  40.3 2.1 %shard_map.91 = (f32[32,1024]{1,0:T(8,128)S(1)}, bf16[32,1024]{1,0:T(8,128)(2,1)S(1)}, bf16[32,1024]{1,0:T(8,128)(2,1)S(1)}, bf16[32,1024]{1,0:T(8,128)(2,1)S(1)}) custom-call(bf16[32,640]{1,0:T(8,128)(2,1)S(1)} %get-tuple-element.29.refs_0_, bf16[32,640]{1,0:T(8,128)(2,1)S(1)} %collective-permute-done.10.refs_1_, ...), custom_call_target="tpu_custom_call" | custom-call | tf_op jit(solution)/shard_map/pallas_call | solution.py:63
  42.3 0.7 %collective-permute-start.14 = (bf16[32,1024]{1,0:T(8,128)(2,1)S(1)}, bf16[32,1024]{1,0:T(8,128)(2,1)S(1)}, u32[]{:S(2)}, u32[]{:S(2)}) collective-permute-start(bf16[32,1024]{1,0:T(8,128)(2,1)S(1)} %get-tuple-element.32), channel_id=1, source_target_pairs={{0,3},{1,2},{2,1},{3,0},{4,7},{5,6},{6,5},{7,4},{8,11},{9,10},{10,... | collective-permute-start | bytes 196616 | tf_op jit(solution)/shard_map/ppermute | solution.py:41
  43.0 0.9 %collective-permute-start.15 = (bf16[32,1024]{1,0:T(8,128)(2,1)S(1)}, bf16[32,1024]{1,0:T(8,128)(2,1)S(1)}, u32[]{:S(2)}, u32[]{:S(2)}) collective-permute-start(bf16[32,1024]{1,0:T(8,128)(2,1)S(1)} %get-tuple-element.33), channel_id=1, source_target_pairs={{0,2},{1,3},{2,0},{3,1},{4,6},{5,7},{6,4},{7,5},{8,10},{9,11},{10,... | collective-permute-start | bytes 196616 | tf_op jit(solution)/shard_map/ppermute | solution.py:41
  43.9 1.9 %collective-permute-start.16 = (bf16[32,1024]{1,0:T(8,128)(2,1)S(1)}, bf16[32,1024]{1,0:T(8,128)(2,1)S(1)}, u32[]{:S(2)}, u32[]{:S(2)}) collective-permute-start(bf16[32,1024]{1,0:T(8,128)(2,1)S(1)} %get-tuple-element.34), channel_id=1, source_target_pairs={{0,1},{1,0},{2,3},{3,2},{4,5},{5,4},{6,7},{7,6},{8,9},{9,8},{10,11... | collective-permute-start | bytes 196616 | tf_op jit(solution)/shard_map/ppermute | solution.py:41
  45.8 2.3 %collective-permute-done.14.refs_1_ = bf16[32,1024]{1,0:T(8,128)(2,1)S(1)} collective-permute-done((bf16[32,1024]{1,0:T(8,128)(2,1)S(1)}, bf16[32,1024]{1,0:T(8,128)(2,1)S(1)}, u32[]{:S(2)}, u32[]{:S(2)}) %collective-permute-start.14) | collective-permute-done | bytes 65568 | tf_op jit(solution)/shard_map/ppermute | solution.py:41
  48.1 0.0 collective-permute-done.15.refs_2_
  48.1 0.7 %collective-permute-done.16.refs_3_ = bf16[32,1024]{1,0:T(8,128)(2,1)S(1)} collective-permute-done((bf16[32,1024]{1,0:T(8,128)(2,1)S(1)}, bf16[32,1024]{1,0:T(8,128)(2,1)S(1)}, u32[]{:S(2)}, u32[]{:S(2)}) %collective-permute-start.16) | collective-permute-done | bytes 65568 | tf_op jit(solution)/shard_map/ppermute | solution.py:41
  48.9 0.7 %collective-permute-start.17 = (bf16[16,1024]{1,0:T(8,128)(2,1)S(1)}, bf16[16,1024]{1,0:T(8,128)(2,1)S(1)}, u32[]{:S(2)}, u32[]{:S(2)}) collective-permute-start(bf16[16,1024]{1,0:T(8,128)(2,1)S(1)} %get-tuple-element.35.own_ref), channel_id=1, source_target_pairs={{4,16},{5,17},{6,18},{7,19},{12,24},{13,25},{14,26},{15,27},{16,4}... | collective-permute-start | bytes 98312 | tf_op jit(solution)/shard_map/ppermute | solution.py:41
  49.5 4.7 %collective-permute-start.18 = (bf16[16,1024]{1,0:T(8,128)(2,1)S(1)}, bf16[16,1024]{1,0:T(8,128)(2,1)S(1)}, u32[]{:S(2)}, u32[]{:S(2)}) collective-permute-start(bf16[16,1024]{1,0:T(8,128)(2,1)S(1)} %get-tuple-element.36), channel_id=1, source_target_pairs={{0,16},{1,17},{2,18},{3,19},{4,0},{5,1},{6,2},{7,3},{8,24},{9,25},... | collective-permute-start | bytes 98312 | tf_op jit(solution)/shard_map/ppermute | solution.py:41
  54.2 0.0 collective-permute-done.17.refs_0_
  54.2 2.8 %collective-permute-done.18.refs_1_ = bf16[16,1024]{1,0:T(8,128)(2,1)S(1)} collective-permute-done((bf16[16,1024]{1,0:T(8,128)(2,1)S(1)}, bf16[16,1024]{1,0:T(8,128)(2,1)S(1)}, u32[]{:S(2)}, u32[]{:S(2)}) %collective-permute-start.18) | collective-permute-done | bytes 32800 | tf_op jit(solution)/shard_map/ppermute | solution.py:41
  57.0 0.6 %shard_map.93 = bf16[16,1024]{1,0:T(8,128)(2,1)} custom-call(bf16[16,1024]{1,0:T(8,128)(2,1)S(1)} %get-tuple-element.35.own_ref, bf16[16,1024]{1,0:T(8,128)(2,1)S(1)} %collective-permute-done.17.refs_0_, bf16[16,1024]{1,0:T(8,128)(2,1)S(1)} %collective-permute-done.18.refs_1_), custom_call_target="tpu_custom_call" | custom-call | tf_op jit(solution)/shard_map/pallas_call | solution.py:63
  (5 shorter events, 0.1 us)
Async XLA Ops:
  0.0 40.3 %collective-permute-start.13 = (bf16[1024,2048]{1,0:T(8,128)(2,1)}, bf16[1024,2048]{1,0:T(8,128)(2,1)S(1)}, u32[]{:S(2)}, u32[]{:S(2)}) collective-permute-start(bf16[1024,2048]{1,0:T(8,128)(2,1)} %refs_4_.5), channel_id=1, source_target_pairs={{0,8},{1,9},{2,10},{3,11},{4,12},{5,13},{6,14},{7,15},{8,0},{9,1},... | collective-permute-start | bytes 12582920 | tf_op jit(solution)/shard_map/ppermute | solution.py:41
  3.1 6.3 %collective-permute-start = (bf16[16,2048]{1,0:T(8,128)(2,1)S(1)}, bf16[16,2048]{1,0:T(8,128)(2,1)S(1)}, u32[]{:S(2)}, u32[]{:S(2)}) collective-permute-start(bf16[16,2048]{1,0:T(8,128)(2,1)S(1)} %get-tuple-element.22), channel_id=1, source_target_pairs={{0,3},{1,2},{2,1},{3,0},{4,7},{5,6},{6,5},{7,4},{8,11},{9,10},{10,... | collective-permute-start | bytes 196616 | tf_op jit(solution)/shard_map/ppermute | solution.py:41
  6.7 4.3 %collective-permute-start.1 = (bf16[16,2048]{1,0:T(8,128)(2,1)S(1)}, bf16[16,2048]{1,0:T(8,128)(2,1)S(1)}, u32[]{:S(2)}, u32[]{:S(2)}) collective-permute-start(bf16[16,2048]{1,0:T(8,128)(2,1)S(1)} %get-tuple-element.23), channel_id=1, source_target_pairs={{0,2},{1,3},{2,0},{3,1},{4,6},{5,7},{6,4},{7,5},{8,10},{9,11},{10,... | collective-permute-start | bytes 196616 | tf_op jit(solution)/shard_map/ppermute | solution.py:41
  7.1 4.3 %collective-permute-start.2 = (bf16[16,2048]{1,0:T(8,128)(2,1)S(1)}, bf16[16,2048]{1,0:T(8,128)(2,1)S(1)}, u32[]{:S(2)}, u32[]{:S(2)}) collective-permute-start(bf16[16,2048]{1,0:T(8,128)(2,1)S(1)} %get-tuple-element.24), channel_id=1, source_target_pairs={{0,1},{1,0},{2,3},{3,2},{4,5},{5,4},{6,7},{7,6},{8,9},{9,8},{10,11... | collective-permute-start | bytes 196616 | tf_op jit(solution)/shard_map/ppermute | solution.py:41
  8.5 24.9 %collective-permute-start.9 = (bf16[1024,512]{1,0:T(8,128)(2,1)S(1)}, bf16[1024,512]{1,0:T(8,128)(2,1)S(1)}, u32[]{:S(2)}, u32[]{:S(2)}) collective-permute-start(bf16[1024,512]{1,0:T(8,128)(2,1)S(1)} %shard_map.89), channel_id=1, source_target_pairs={{0,8},{1,9},{2,10},{3,11},{4,12},{5,13},{6,14},{7,15},{8,0},{9,1},... | collective-permute-start | bytes 3145736 | tf_op jit(solution)/shard_map/ppermute | solution.py:41
  11.4 5.3 %collective-permute-start.3 = (bf16[16,2048]{1,0:T(8,128)(2,1)S(1)}, bf16[16,2048]{1,0:T(8,128)(2,1)S(1)}, u32[]{:S(2)}, u32[]{:S(2)}) collective-permute-start(bf16[16,2048]{1,0:T(8,128)(2,1)S(1)} %add_add_fusion._), channel_id=1, source_target_pairs={{0,4},{1,5},{2,6},{3,7},{4,0},{5,1},{6,2},{7,3},{8,12},{9,13},{10,... | collective-permute-start | bytes 196616 | tf_op jit(solution)/shard_map/ppermute | solution.py:41
  16.8 8.1 %copy-start = (bf16[2048,1024]{1,0:T(8,128)(2,1)S(1)}, bf16[2048,1024]{1,0:T(8,128)(2,1)}, u32[]{:S(2)}) copy-start(bf16[2048,1024]{1,0:T(8,128)(2,1)} %refs_4_.4) | copy-start | bytes 12582916
  16.8 6.0 %collective-permute-start.4 = (bf16[16,2048]{1,0:T(8,128)(2,1)S(1)}, bf16[16,2048]{1,0:T(8,128)(2,1)S(1)}, u32[]{:S(2)}, u32[]{:S(2)}) collective-permute-start(bf16[16,2048]{1,0:T(8,128)(2,1)S(1)} %add.28._.refs_0_), channel_id=1, source_target_pairs={{0,3},{1,2},{2,1},{3,0},{4,7},{5,6},{6,5},{7,4},{8,11},{9,10},{10,... | collective-permute-start | bytes 196616 | tf_op jit(solution)/shard_map/ppermute | solution.py:41
  19.0 4.5 %collective-permute-start.5 = (bf16[16,2048]{1,0:T(8,128)(2,1)S(1)}, bf16[16,2048]{1,0:T(8,128)(2,1)S(1)}, u32[]{:S(2)}, u32[]{:S(2)}) collective-permute-start(bf16[16,2048]{1,0:T(8,128)(2,1)S(1)} %add.28._.refs_0_), channel_id=1, source_target_pairs={{0,2},{1,3},{2,0},{3,1},{4,6},{5,7},{6,4},{7,5},{8,10},{9,11},{10,... | collective-permute-start | bytes 196616 | tf_op jit(solution)/shard_map/ppermute | solution.py:41
  20.6 4.3 %collective-permute-start.6 = (bf16[16,2048]{1,0:T(8,128)(2,1)S(1)}, bf16[16,2048]{1,0:T(8,128)(2,1)S(1)}, u32[]{:S(2)}, u32[]{:S(2)}) collective-permute-start(bf16[16,2048]{1,0:T(8,128)(2,1)S(1)} %add.28._.refs_0_), channel_id=1, source_target_pairs={{0,1},{1,0},{2,3},{3,2},{4,5},{5,4},{6,7},{7,6},{8,9},{9,8},{10,11... | collective-permute-start | bytes 196616 | tf_op jit(solution)/shard_map/ppermute | solution.py:41
  26.1 1.5 %collective-permute-start.7 = (bf16[64,1536]{1,0:T(8,128)(2,1)S(1)}, bf16[64,1536]{1,0:T(8,128)(2,1)S(1)}, u32[]{:S(2)}, u32[]{:S(2)}) collective-permute-start(bf16[64,1536]{1,0:T(8,128)(2,1)S(1)} %shard_map.86), channel_id=1, source_target_pairs={{0,8},{1,9},{2,10},{3,11},{4,12},{5,13},{6,14},{7,15},{8,0},{9,1},... | collective-permute-start | bytes 589832 | tf_op jit(solution)/shard_map/ppermute | solution.py:41
  27.4 12.8 %copy-start.1 = (bf16[1024,2048]{1,0:T(8,128)(2,1)S(1)}, bf16[1024,2048]{1,0:T(8,128)(2,1)}, u32[]{:S(2)}) copy-start(bf16[1024,2048]{1,0:T(8,128)(2,1)} %refs_4_.5) | copy-start | bytes 12582916
  27.7 5.8 %collective-permute-start.8 = (bf16[128,512]{1,0:T(8,128)(2,1)S(1)}, bf16[128,512]{1,0:T(8,128)(2,1)S(1)}, u32[]{:S(2)}, u32[]{:S(2)}) collective-permute-start(bf16[128,512]{1,0:T(8,128)(2,1)S(1)} %get-tuple-element.28), channel_id=1, source_target_pairs={{0,16},{1,17},{2,18},{3,19},{4,20},{5,21},{6,22},{7,23},{8,24},{9,... | collective-permute-start | bytes 393224 | tf_op jit(solution)/shard_map/ppermute | solution.py:41
  35.1 1.9 %collective-permute-start.10 = (bf16[32,640]{1,0:T(8,128)(2,1)S(1)}, bf16[32,640]{1,0:T(8,128)(2,1)S(1)}, u32[]{:S(2)}, u32[]{:S(2)}) collective-permute-start(bf16[32,640]{1,0:T(8,128)(2,1)S(1)} %get-tuple-element.30), channel_id=1, source_target_pairs={{0,8},{1,9},{2,10},{3,11},{4,12},{5,13},{6,14},{7,15},{8,0},{9,1},... | collective-permute-start | bytes 122888 | tf_op jit(solution)/shard_map/ppermute | solution.py:41
  35.1 4.1 %collective-permute-start.11 = (bf16[32,640]{1,0:T(8,128)(2,1)S(1)}, bf16[32,640]{1,0:T(8,128)(2,1)S(1)}, u32[]{:S(2)}, u32[]{:S(2)}) collective-permute-start(bf16[32,640]{1,0:T(8,128)(2,1)S(1)} %get-tuple-element.29.refs_0_), channel_id=1, source_target_pairs={{0,16},{1,17},{2,18},{3,19},{4,20},{5,21},{6,22},{7,23},{8,24},{9,... | collective-permute-start | bytes 122888 | tf_op jit(solution)/shard_map/ppermute | solution.py:41
  36.7 3.5 %collective-permute-start.12 = (bf16[32,640]{1,0:T(8,128)(2,1)S(1)}, bf16[32,640]{1,0:T(8,128)(2,1)S(1)}, u32[]{:S(2)}, u32[]{:S(2)}) collective-permute-start(bf16[32,640]{1,0:T(8,128)(2,1)S(1)} %get-tuple-element.30), channel_id=1, source_target_pairs={{0,24},{1,25},{2,26},{3,27},{4,28},{5,29},{6,30},{7,31},{8,16},{9,... | collective-permute-start | bytes 122888 | tf_op jit(solution)/shard_map/ppermute | solution.py:41
  42.3 5.8 %collective-permute-start.14 = (bf16[32,1024]{1,0:T(8,128)(2,1)S(1)}, bf16[32,1024]{1,0:T(8,128)(2,1)S(1)}, u32[]{:S(2)}, u32[]{:S(2)}) collective-permute-start(bf16[32,1024]{1,0:T(8,128)(2,1)S(1)} %get-tuple-element.32), channel_id=1, source_target_pairs={{0,3},{1,2},{2,1},{3,0},{4,7},{5,6},{6,5},{7,4},{8,11},{9,10},{10,... | collective-permute-start | bytes 196616 | tf_op jit(solution)/shard_map/ppermute | solution.py:41
  43.0 5.1 %collective-permute-start.15 = (bf16[32,1024]{1,0:T(8,128)(2,1)S(1)}, bf16[32,1024]{1,0:T(8,128)(2,1)S(1)}, u32[]{:S(2)}, u32[]{:S(2)}) collective-permute-start(bf16[32,1024]{1,0:T(8,128)(2,1)S(1)} %get-tuple-element.33), channel_id=1, source_target_pairs={{0,2},{1,3},{2,0},{3,1},{4,6},{5,7},{6,4},{7,5},{8,10},{9,11},{10,... | collective-permute-start | bytes 196616 | tf_op jit(solution)/shard_map/ppermute | solution.py:41
  43.9 4.9 %collective-permute-start.16 = (bf16[32,1024]{1,0:T(8,128)(2,1)S(1)}, bf16[32,1024]{1,0:T(8,128)(2,1)S(1)}, u32[]{:S(2)}, u32[]{:S(2)}) collective-permute-start(bf16[32,1024]{1,0:T(8,128)(2,1)S(1)} %get-tuple-element.34), channel_id=1, source_target_pairs={{0,1},{1,0},{2,3},{3,2},{4,5},{5,4},{6,7},{7,6},{8,9},{9,8},{10,11... | collective-permute-start | bytes 196616 | tf_op jit(solution)/shard_map/ppermute | solution.py:41
  48.9 5.3 %collective-permute-start.17 = (bf16[16,1024]{1,0:T(8,128)(2,1)S(1)}, bf16[16,1024]{1,0:T(8,128)(2,1)S(1)}, u32[]{:S(2)}, u32[]{:S(2)}) collective-permute-start(bf16[16,1024]{1,0:T(8,128)(2,1)S(1)} %get-tuple-element.35.own_ref), channel_id=1, source_target_pairs={{4,16},{5,17},{6,18},{7,19},{12,24},{13,25},{14,26},{15,27},{16,4}... | collective-permute-start | bytes 98312 | tf_op jit(solution)/shard_map/ppermute | solution.py:41
  49.5 7.5 %collective-permute-start.18 = (bf16[16,1024]{1,0:T(8,128)(2,1)S(1)}, bf16[16,1024]{1,0:T(8,128)(2,1)S(1)}, u32[]{:S(2)}, u32[]{:S(2)}) collective-permute-start(bf16[16,1024]{1,0:T(8,128)(2,1)S(1)} %get-tuple-element.36), channel_id=1, source_target_pairs={{0,16},{1,17},{2,18},{3,19},{4,0},{5,1},{6,2},{7,3},{8,24},{9,25},... | collective-permute-start | bytes 98312 | tf_op jit(solution)/shard_map/ppermute | solution.py:41

commit v2 on v1

v2 whole, which is shorter than its diff:
```python
import math

import jax
import jax.numpy as jnp
from jax import lax
from jax.experimental import pallas as pl
from jax.experimental.pallas import tpu as pltpu
from jax.sharding import PartitionSpec as P

HD = 128
CORES = 2
MIB = 1 << 20
BF16 = jnp.bfloat16
F32 = jnp.float32


class Plan:
    def __init__(self, mesh, gen_ids, w_query, w_out, prompt_keys):
        self.seq, self.head = mesh.shape["seq"], mesh.shape["head"]
        self.cands, self.steps = gen_ids.shape
        self.tokens = self.cands * self.steps
        self.features, self.width = w_query.shape
        self.prompt_rows = prompt_keys.shape[0]
        self.inner = math.gcd(self.head, 4)
        self.outer = self.head // self.inner
        self.room = -(-2 * self.tokens // (self.head * 16)) * 16
        self.half = self.width // CORES
        self.chips = self.seq // CORES
        self.parts = self.head // self.seq
        self.share = self.tokens // self.seq
        self.owned = self.tokens // self.chips
        self.columns = w_out.shape[1] // self.parts

    def send(self, value, route):
        pairs = []
        for s in range(self.seq):
            for h in range(self.head):
                to_s, to_h = route(s, h)
                pairs.append((s * self.head + h, to_s * self.head + to_h))
        return lax.ppermute(value, ("seq", "head"), pairs)

    def over_seq(self, value, step):
        return self.send(value, lambda s, h: (s ^ step, h))

    def over_head(self, value, step):
        return self.send(value, lambda s, h: (s, h ^ step))


VMEM_SPEC = pl.BlockSpec(memory_space=pltpu.VMEM)
ANY_SPEC = pl.BlockSpec(memory_space=pl.ANY)


def aligned(index, size):
    return pl.ds(pl.multiple_of(index * size, size), size)


def in_hbm(value):
    return pltpu.with_memory_space_constraint(value, pltpu.HBM)


def call(kernel, out_shape, in_specs, out_specs, scratch, limit, *args, cost=None):
    return pl.pallas_call(
        kernel,
        out_shape=out_shape,
        in_specs=in_specs,
        out_specs=out_specs,
        scratch_shapes=scratch,
        cost_estimate=cost,
        compiler_params=pltpu.CompilerParams(vmem_limit_bytes=limit * MIB),
    )(*args)


def iota(shape, axis):
    return lax.broadcasted_iota(jnp.int32, shape, axis)


def id_columns(plan, ids):
    steps = plan.steps
    corner = iota((steps, steps), 0) == iota((steps, steps), 1)
    columns = []
    for cand in range(plan.cands):
        row = ids[cand : cand + 1, :].astype(F32)
        columns.append(jnp.sum(jnp.where(corner, row, 0.0), axis=1, keepdims=True))
    return jnp.concatenate(columns)


def pick(plan, gen_ids, embed_rows):
    vocab = embed_rows.shape[0]
    tokens, room = plan.tokens, plan.room
    cut = 2 * HD
    pieces = vocab // cut

    def kernel(ids_ref, embed_ref, rows_ref, ids, held, found, ids_sem, sems):
        ids_copy = pltpu.make_async_copy(ids_ref, ids, ids_sem)
        ids_copy.start()
        copies = []
        for piece in range(pieces):
            window = pl.ds(piece * cut, cut)
            copies.append(
                pltpu.make_async_copy(embed_ref.at[window], held.at[window], sems.at[piece])
            )
            copies[-1].start()
        base = (lax.axis_index("head") * vocab).astype(F32)
        first, second = iota((tokens, tokens), 0), iota((tokens, tokens), 1)
        ids_copy.wait()
        column = id_columns(plan, ids) - base
        local = (column >= 0) & (column < vocab)
        row = jnp.sum(jnp.where(first == second, column, 0.0), axis=0, keepdims=True)
        earlier = jnp.where((first < second) & local, 1.0, 0.0)
        rank = jnp.sum(earlier, axis=0, keepdims=True)
        wanted = (row >= 0) & (row < vocab) & (rank == iota((room, tokens), 0).astype(F32))
        chosen = jnp.sum(jnp.where(wanted, row + 1.0, 0.0), axis=1, keepdims=True) - 1.0
        selector = (chosen == iota((room, vocab), 1).astype(F32)).astype(F32).astype(BF16)
        for piece, copy in enumerate(copies):
            window = slice(piece * cut, (piece + 1) * cut)
            copy.wait()
            part = jnp.dot(selector[:, window], held[window, :], preferred_element_type=F32)
            if piece:
                part = part + found[...]
            if piece < pieces - 1:
                found[...] = part
        rows_ref[...] = part.astype(BF16)

    return call(
        kernel,
        jax.ShapeDtypeStruct((room, plan.features), BF16),
        [ANY_SPEC] * 2,
        VMEM_SPEC,
        [
            pltpu.VMEM(gen_ids.shape, jnp.int32),
            pltpu.VMEM(embed_rows.shape, BF16),
            pltpu.VMEM((room, plan.features), F32),
            pltpu.SemaphoreType.DMA,
            pltpu.SemaphoreType.DMA((pieces,)),
        ],
        16,
        in_hbm(gen_ids),
        in_hbm(embed_rows),
    )


def find_places(plan, after, gen_ids, vocab):
    tokens, room = plan.tokens, plan.room
    slots = plan.head * room

    def kernel(_, ids_ref, places_ref, beyond_ref, ids, ids_sem):
        ids_copy = pltpu.make_async_copy(ids_ref, ids, ids_sem)
        ids_copy.start()
        ids_copy.wait()
        owner = id_columns(plan, ids).astype(jnp.int32) // vocab
        member = (owner == iota((tokens, HD), 1)).astype(F32).astype(BF16)
        same = lax.dot_general(
            member, member, (((1,), (1,)), ((), ())), preferred_element_type=F32
        )
        earlier = iota((tokens, tokens), 1) < iota((tokens, tokens), 0)
        rank = jnp.sum(jnp.where(earlier, same, 0.0), axis=1, keepdims=True)
        beyond = jnp.sum(jnp.where(rank >= room, 1.0, 0.0), axis=0, keepdims=True)
        beyond_ref[...] = jnp.broadcast_to(beyond, beyond_ref.shape)
        slot = iota((tokens, slots), 1)
        place = slot // (plan.outer * room)
        group = lax.rem(slot // room, plan.outer)
        distance = lax.rem(plan.inner - place, plan.inner) + group * plan.inner
        filled = (owner == (lax.axis_index("head") ^ distance)) & (
            rank == lax.rem(slot, room).astype(F32)
        )
        places_ref[...] = filled.astype(F32).astype(BF16)

    return call(
        kernel,
        [
            jax.ShapeDtypeStruct((tokens, slots), BF16),
            jax.ShapeDtypeStruct((8, HD), F32),
        ],
        [ANY_SPEC] * 2,
        [VMEM_SPEC] * 2,
        [pltpu.VMEM(gen_ids.shape, jnp.int32), pltpu.SemaphoreType.DMA],
        8,
        after,
        in_hbm(gen_ids),
    )


def rows_beyond(plan, gen_ids, embed_rows):
    vocab = embed_rows.shape[0]
    ids = gen_ids.reshape(-1)
    owner = ids // vocab
    order = jnp.arange(plan.tokens)
    rank = jnp.sum((owner[:, None] == owner[None]) & (order[None] < order[:, None]), axis=1)
    shifted = jnp.where(rank >= plan.room, ids - lax.axis_index("head") * vocab, -1)
    selector = (shifted[:, None] == jnp.arange(vocab, dtype=jnp.int32)[None]).astype(BF16)

    def kernel(selector_ref, embed_ref, out_ref, held, sem):
        copy = pltpu.make_async_copy(embed_ref, held, sem)
        copy.start()
        copy.wait()
        found = jnp.dot(selector_ref[...], held[...], preferred_element_type=F32)
        out_ref[...] = found.astype(BF16)

    picked = call(
        kernel,
        jax.ShapeDtypeStruct((plan.tokens, plan.features), BF16),
        [VMEM_SPEC, ANY_SPEC],
        VMEM_SPEC,
        [pltpu.VMEM(embed_rows.shape, BF16), pltpu.SemaphoreType.DMA],
        16,
        selector,
        in_hbm(embed_rows),
    )
    step = 1
    while step < plan.head:
        picked = picked + plan.over_head(picked, step)
        step *= 2
    return picked


def bring(after, source):
    def kernel(_, source_ref, out_ref, sems):
        pieces = 4
        size = source.shape[0] // pieces
        copies = [
            pltpu.make_async_copy(
                source_ref.at[pl.ds(k * size, size)], out_ref.at[pl.ds(k * size, size)], sems.at[k]
            )
            for k in range(pieces)
        ]
        for copy in copies:
            copy.start()
        for copy in copies:
            copy.wait()

    return call(
        kernel,
        jax.ShapeDtypeStruct(source.shape, source.dtype),
        [ANY_SPEC] * 2,
        ANY_SPEC,
        [pltpu.SemaphoreType.DMA((4,))],
        4,
        after,
        in_hbm(source),
    )


def prompt_to_swap(plan, after, prompt_keys, prompt_values):
    half = plan.half

    def kernel(_, keys_ref, values_ref, given_keys_ref, given_values_ref, sems):
        window = aligned(1 - lax.rem(lax.axis_index("seq"), CORES), half)
        copies = [
            pltpu.make_async_copy(keys_ref.at[:, window], given_keys_ref, sems.at[0]),
            pltpu.make_async_copy(values_ref.at[:, window], given_values_ref, sems.at[1]),
        ]
        for copy in copies:
            copy.start()
        for copy in copies:
            copy.wait()

    return call(
        kernel,
        [jax.ShapeDtypeStruct((plan.prompt_rows, half), BF16)] * 2,
        [ANY_SPEC] * 3,
        [ANY_SPEC] * 2,
        [pltpu.SemaphoreType.DMA((2,))],
        4,
        after,
        in_hbm(prompt_keys),
        in_hbm(prompt_values),
    )


def gather_embedded(
    plan, gen_ids, embed_rows, w_key, w_value, prompt_keys, prompt_values, w_out
):
    rows = pick(plan, gen_ids, embed_rows)
    places, beyond = find_places(plan, rows, gen_ids, embed_rows.shape[0])
    rest = lax.cond(
        beyond[0, 0] > 0.5,
        lambda: rows_beyond(plan, gen_ids, embed_rows),
        lambda: jnp.zeros((plan.tokens, plan.features), BF16),
    )
    w_key = bring(rest, w_key)
    across = [plan.over_head(rows, step * plan.inner) for step in range(1, plan.outer)]
    near = jnp.concatenate([rows, *across])
    near, w_key, w_out = lax.optimization_barrier((near, w_key, w_out))
    swapped_out = plan.over_seq(w_out, 1)
    given = prompt_to_swap(plan, near, prompt_keys, prompt_values)
    w_value = bring(near, w_value)
    blocks = [near] + [plan.over_head(near, step) for step in range(1, plan.inner)[::-1]]
    size = plan.outer * plan.room

    def kernel(places_ref, beyond_ref, rest_ref, *refs):
        blocks, (out_ref, held, added, sem) = refs[: plan.inner], refs[plan.inner :]
        for block, ref in enumerate(blocks):
            held[block * size : (block + 1) * size] = ref[...]
        placed = jnp.dot(places_ref[...], held[...], preferred_element_type=F32)
        out_ref[...] = placed.astype(BF16)

        @pl.when(jnp.max(beyond_ref[...]) > 0.5)
        def _():
            copy = pltpu.make_async_copy(rest_ref, added, sem)
            copy.start()
            copy.wait()
            out_ref[...] = out_ref[...] + added[...]

    embedded = call(
        kernel,
        jax.ShapeDtypeStruct((plan.tokens, plan.features), BF16),
        [VMEM_SPEC] * 2 + [ANY_SPEC] + [VMEM_SPEC] * plan.inner,
        VMEM_SPEC,
        [
            pltpu.VMEM((plan.inner * size, plan.features), BF16),
            pltpu.VMEM((plan.tokens, plan.features), BF16),
            pltpu.SemaphoreType.DMA,
        ],
        16,
        places,
        beyond,
        rest,
        *blocks,
    )
    return embedded, w_key, w_value, given, swapped_out


def prompt_half(plan, prompt_keys, prompt_values, after):
    rows, half = plan.prompt_rows, plan.half

    def kernel(_, keys_ref, values_ref, out_ref, sems):
        window = aligned(lax.rem(lax.axis_index("seq"), CORES), half)
        copies = [
            pltpu.make_async_copy(
                source.at[:, window], out_ref.at[pl.ds(place * rows, rows)], sems.at[place]
            )
            for place, source in enumerate((keys_ref, values_ref))
        ]
        for copy in copies:
            copy.start()
        for copy in copies:
            copy.wait()

    return call(
        kernel,
        jax.ShapeDtypeStruct((2 * rows, half), BF16),
        [ANY_SPEC] * 3,
        ANY_SPEC,
        [pltpu.SemaphoreType.DMA((2,))],
        4,
        after,
        in_hbm(prompt_keys),
        in_hbm(prompt_values),
    )


def project_half(plan, embedded, weights, other, dtype):
    half = plan.half

    def kernel(rows_ref, *refs):
        sources, out_ref = refs[:3], refs[3]
        core = lax.rem(lax.axis_index("seq"), CORES)
        window = aligned(1 - core if other else core, half)
        for kind in range(3):
            product = jnp.dot(
                rows_ref[...], sources[kind][:, window], preferred_element_type=F32
            )
            out_ref[:, kind * half : (kind + 1) * half] = product.astype(dtype)

    return call(
        kernel,
        jax.ShapeDtypeStruct((plan.tokens, 3 * half), dtype),
        [VMEM_SPEC] * 4,
        VMEM_SPEC,
        [],
        16,
        embedded,
        *weights,
    )


def sum_cores(plan, own, received):
    tokens, half, owned = plan.tokens, plan.half, plan.owned

    def kernel(own_ref, received_ref, *refs):
        outs, total = refs[: plan.chips], refs[plan.chips]
        total[...] = own_ref[...] + received_ref[...].astype(F32)
        chip = lax.axis_index("seq") // CORES
        for dy in range(plan.chips):
            out, rows = outs[dy], aligned(chip ^ dy, owned)
            out[:tokens] = total[:, :half].astype(out.dtype)
            out[tokens : tokens + owned] = total[rows, half : 2 * half].astype(out.dtype)
            out[tokens + owned :] = total[rows, 2 * half :].astype(out.dtype)

    shape = (tokens + 2 * owned, half)
    return call(
        kernel,
        [jax.ShapeDtypeStruct(shape, BF16 if dy else F32) for dy in range(plan.chips)],
        [VMEM_SPEC] * 2,
        [VMEM_SPEC] * plan.chips,
        [pltpu.VMEM((tokens, 3 * half), F32)],
        8,
        own,
        received,
    )


def project(plan, embedded, weights):
    received = plan.over_seq(project_half(plan, embedded, weights, True, BF16), 1)
    own = project_half(plan, embedded, weights, False, F32)
    parts = sum_cores(plan, own, received)
    return [parts[0]] + [plan.over_seq(parts[dy], dy * CORES) for dy in range(1, plan.chips)]


def angle_tables(plan):
    half_size = HD // 2
    frequency = 10000.0 ** (-jnp.arange(half_size, dtype=F32) / half_size)
    positions = plan.prompt_rows * plan.seq + jnp.arange(plan.steps, dtype=jnp.int32)
    angles = positions.astype(F32)[:, None] * frequency[None, :]
    cosine, sine_part = jnp.cos(angles), jnp.sin(angles)
    return (
        jnp.concatenate([cosine, cosine], axis=-1),
        jnp.concatenate([-sine_part, sine_part], axis=-1),
    )


def attend(plan, parts, kept, swapped, tables):
    tokens, half, owned, share = plan.tokens, plan.half, plan.owned, plan.share
    rows = plan.prompt_rows
    scale = 1.0 / math.sqrt(HD)
    transposed = (((1,), (1,)), ((), ()))

    def kernel(*refs):
        sums, refs = refs[: plan.chips], refs[plan.chips :]
        kept_ref, keys_ref, values_ref, cosine_ref, sine_ref = refs[:5]
        near_ref, far_ref, result = refs[5:]
        core = lax.rem(lax.axis_index("seq"), CORES)
        chip = lax.axis_index("seq") // CORES
        total = sums[0][...]
        for dy in range(1, plan.chips):
            total = total + sums[dy][...].astype(F32)
        cosine, sine_part = cosine_ref[...][None], sine_ref[...][None]

        def rotated(vectors):
            turned = pltpu.roll(vectors, HD // 2, 1)
            shaped = vectors.reshape(-1, plan.steps, HD) * cosine
            shaped = shaped + turned.reshape(-1, plan.steps, HD) * sine_part
            return shaped.reshape(vectors.shape).astype(BF16)

        pair = 2 * HD
        row = lax.broadcasted_iota(jnp.int32, (2 * tokens, 2 * owned), 0)
        column = lax.broadcasted_iota(jnp.int32, (2 * tokens, 2 * owned), 1)
        same_head = row // tokens == column // owned
        row, column = lax.rem(row, tokens), lax.rem(column, owned) + chip * owned
        seen = same_head & (row // plan.steps == column // plan.steps) & (column <= row)
        lane = lax.broadcasted_iota(jnp.int32, (tokens, HD), 1)
        logs = jnp.zeros((tokens, HD), F32)
        nothing = jnp.zeros((tokens, HD), BF16)
        for start in range(0, half, pair):
            lanes = slice(start, start + pair)
            near, far = slice(start, start + HD), slice(start + HD, start + pair)
            query = jnp.concatenate(
                [
                    jnp.concatenate([rotated(total[:tokens, near]), nothing], axis=1),
                    jnp.concatenate([nothing, rotated(total[:tokens, far])], axis=1),
                ]
            )
            keys, values = slice(tokens, tokens + owned), slice(tokens + owned, None)
            gen_key = jnp.concatenate([rotated(total[keys, near]), rotated(total[keys, far])])
            gen_value = jnp.concatenate([total[values, near], total[values, far]]).astype(BF16)

            def score(vectors, key):
                return (
                    lax.dot_general(vectors, key, transposed, preferred_element_type=F32) * scale
                )

            own = score(jnp.concatenate([query[:tokens, :HD], query[tokens:, HD:]]), gen_key)
            scores = [
                score(query, kept_ref[:rows, lanes]),
                score(query, keys_ref[:, lanes]),
                jnp.where(seen, own, -jnp.inf),
            ]
            peak = jnp.max(scores[0], axis=1, keepdims=True)
            for part in scores[1:]:
                peak = jnp.maximum(peak, jnp.max(part, axis=1, keepdims=True))
            weights = [jnp.exp(part - peak) for part in scores]
            weight_sum = sum(jnp.sum(weight, axis=1, keepdims=True) for weight in weights)
            weights = [weight.astype(BF16) for weight in weights]
            summed = jnp.dot(
                weights[0], kept_ref[rows:, lanes], preferred_element_type=F32
            ) + jnp.dot(weights[1], values_ref[:, lanes], preferred_element_type=F32)
            summed = jnp.concatenate([summed[:tokens, :HD], summed[tokens:, HD:]])
            summed = summed + jnp.dot(weights[2], gen_value, preferred_element_type=F32)
            mixed = (summed / weight_sum).astype(BF16)
            result[:, near] = mixed[:tokens]
            result[:, far] = mixed[tokens:]
            both = peak + jnp.log(weight_sum)
            for place, rest in enumerate((both[:tokens], both[tokens:])):
                first = 3 * (start // HD + place)
                for term in range(3):
                    piece = rest.astype(BF16).astype(F32)
                    rest = rest - piece
                    logs = jnp.where(lane == first + term, piece, logs)
        result[:, half:] = logs.astype(BF16)
        for pair in range(plan.chips):
            place = pl.ds(pair * share, share)
            near_ref[place, :] = result[aligned(pair * CORES + core, share), :]
            far_ref[place, :] = result[aligned(pair * CORES + 1 - core, share), :]

    out = jax.ShapeDtypeStruct((tokens // CORES, half + HD), BF16)
    near, far = call(
        kernel,
        [out] * 2,
        [VMEM_SPEC] * (plan.chips + 5),
        [VMEM_SPEC] * 2,
        [pltpu.VMEM((tokens, half + HD), BF16)],
        24,
        *parts,
        kept,
        *swapped,
        *tables,
    )
    got = {k: plan.over_seq(far if k % CORES else near, k) for k in range(1, plan.seq)}
    return [near] + [got[k] for k in range(1, plan.seq)]


def multiply_out(plan, attended, own, swapped):
    share, half, columns = plan.share, plan.half, plan.columns
    rows = plan.tokens // CORES
    keys = [(dy, dx) for dx in range(plan.parts) for dy in range(plan.chips)]

    def kernel(*refs):
        parts, refs = refs[: plan.seq], refs[plan.seq :]
        (own_ref, swapped_ref), refs = refs[:2], refs[2:]
        outs, (joined, held) = refs[: len(keys)], refs[len(keys) :]
        seq_index = lax.axis_index("seq")
        chip, core = seq_index // CORES, lax.rem(seq_index, CORES)
        part_index = lax.rem(lax.axis_index("head"), plan.parts)
        for side in range(CORES):
            sources = [parts[step] for step in range(side, plan.seq, CORES)]
            first = (core ^ side) * half
            for head in range(half // HD):
                lanes = slice(head * HD, (head + 1) * HD)
                logs = [
                    sum(
                        source[:, half + 3 * head + term : half + 3 * head + term + 1].astype(F32)
                        for term in (2, 1, 0)
                    )
                    for source in sources
                ]
                top = logs[0]
                for one in logs[1:]:
                    top = jnp.maximum(top, one)
                scales = [jnp.exp(one - top) for one in logs]
                mixed = sum(f * source[:, lanes].astype(F32) for f, source in zip(scales, sources))
                mixed = (mixed / sum(scales)).astype(BF16)
                joined[:, pl.ds(pl.multiple_of(first + head * HD, HD), HD)] = mixed
        left = joined[...]
        for dx in list(range(plan.parts))[::-1]:
            lanes = aligned(part_index ^ dx, columns)
            for weight, block in ((own_ref, core), (swapped_ref, 1 - core)):
                product = jnp.dot(left, weight[:, lanes], preferred_element_type=F32)
                held[...] = product
                for dy in range(plan.chips):
                    out = outs[keys.index((dy, dx))]
                    out[block] = held[aligned(chip ^ dy, share), :].astype(out.dtype)

    shape = (CORES, share, columns)
    outs = [jax.ShapeDtypeStruct(shape, BF16 if any(key) else F32) for key in keys]
    made = call(
        kernel,
        outs,
        [VMEM_SPEC] * (plan.seq + 2),
        [VMEM_SPEC] * len(keys),
        [pltpu.VMEM((rows, plan.width), BF16), pltpu.VMEM((rows, columns), F32)],
        24,
        *attended,
        own,
        swapped,
    )
    got = {}
    for key, value in list(zip(keys, made))[::-1]:
        dy, dx = key
        if any(key):
            value = plan.send(value, lambda s, h: (s ^ (dy * CORES), h ^ dx))
        got[key] = value
    return got


def sum_parts(plan, got):
    keys = list(got)
    shape = (plan.share, plan.columns)

    def kernel(*refs):
        ins, refs = dict(zip(keys, refs)), refs[len(keys) :]
        outs, (held,) = refs[: plan.seq], refs[plan.seq :]
        chip = lax.axis_index("seq") // CORES
        place = lax.axis_index("head") // plan.parts
        for dy in range(plan.chips):
            total = ins[dy, 0][...].astype(F32)
            for dx in range(1, plan.parts):
                total = total + ins[dy, dx][...].astype(F32)
            for core in range(CORES):
                held[(chip ^ dy) * CORES + core] = total[core]
        for step in range(plan.seq):
            outs[step][...] = held[place ^ step].astype(outs[step].dtype)

    outs = [jax.ShapeDtypeStruct(shape, BF16 if step else F32) for step in range(plan.seq)]
    made = call(
        kernel,
        outs,
        [VMEM_SPEC] * len(keys),
        [VMEM_SPEC] * plan.seq,
        [pltpu.VMEM((plan.seq,) + shape, F32)],
        16,
        *got.values(),
    )
    got = [
        plan.send(made[step], lambda s, h: (s, h ^ (step * plan.parts)))
        for step in list(range(1, plan.seq))[::-1]
    ]

    def last(*refs):
        total = refs[0][...]
        for ref in refs[1:-1]:
            total = total + ref[...].astype(F32)
        refs[-1][...] = total.astype(BF16)

    return call(
        last,
        jax.ShapeDtypeStruct(shape, BF16),
        [VMEM_SPEC] * plan.seq,
        VMEM_SPEC,
        [],
        8,
        made[0],
        *got,
    )


def solution(mesh):
    def body(gen_ids, embed_rows, w_query, w_key, w_value, w_out, prompt_keys, prompt_values):
        plan = Plan(mesh, gen_ids, w_query, w_out, prompt_keys)
        embedded, w_key, w_value, given, swapped_out = gather_embedded(
            plan, gen_ids, embed_rows, w_key, w_value, prompt_keys, prompt_values, w_out
        )
        swapped = [plan.over_seq(part, 1) for part in given]
        parts = project(plan, embedded, (w_query, w_key, w_value))
        kept = prompt_half(plan, prompt_keys, prompt_values, parts[0])
        attended = attend(plan, parts, kept, swapped, angle_tables(plan))
        return sum_parts(plan, multiply_out(plan, attended, w_out, swapped_out))

    return jax.shard_map(
        body,
        mesh=mesh,
        in_specs=(
            P(),
            P("head", "seq"),
            P("seq", "head"),
            P("seq", "head"),
            P("seq", "head"),
            P("head", "seq"),
            P("seq", "head"),
            P("seq", "head"),
        ),
        out_specs=P("seq", "head"),
        check_vma=False,
    )
```

time: 57.8 us -> 54.2 us (0.938)
  starting transfers between devices: 23.6 us -> 19.6 us
  waiting for transfers between devices: 17.3 us -> 14.2 us
  local copies, waits for them, and re-layouts: 0.01 us -> 1.59 us
  Pallas kernels: 16.3 us -> 17.5 us
  between operations: 0.16 us -> 0.85 us
    ppermute x19 -> x18, starting transfers between devices: 23.6 us -> 19.6 us  [send(): return lax.ppermute(value, ('seq', 'head'), pairs)]
    ppermute x19 -> x18, waiting for transfers between devices: 17.3 us -> 14.2 us  [send(): return lax.ppermute(value, ('seq', 'head'), pairs)]
    pallas_call x12 -> x14, Pallas kernels: 16.3 us -> 17.5 us  [call(): pl.pallas_call(kernel, out_shape=out_shape, in_specs=in_specs, out_specs=...]
    unnamed x4 -> x6, local copies, waits for them, and re-layouts: 0.01 us -> 1.05 us
  transfers between devices with their start and end apart: 19 -> 18, of which waited for: 13 -> 12; matrix products, arithmetic and copies ran while one was open for 0% -> 1% of each run, Pallas kernels for 24% -> 22%
where the time goes in v2:
time: 54.2 us; the launch traced here: 54 us
  starting transfers between devices  19.6 us (36%)
  Pallas kernels  17.5 us (32%)
  waiting for transfers between devices  14.2 us (26%)
  local copies, waits for them, and re-layouts  1.59 us (3%)
  between operations  0.85 us (2%)
    ppermute x18, starting transfers between devices, send(): return lax.ppermute(value, ('seq', 'head'), pairs)  19.6 us
    pallas_call x14, Pallas kernels, call(): pl.pallas_call(kernel, out_shape=out_shape, in_specs=in_specs, out_specs=...  17.5 us
    ppermute x18, waiting for transfers between devices, send(): return lax.ppermute(value, ('seq', 'head'), pairs)  14.2 us
  transfers between devices with their start and end apart: 18, of which 12 were waited for; matrix products, arithmetic and copies ran while one was open for 1% of the time, Pallas kernels for 22%

profile of v2, /device:TPU:0, one launch (start us, length us, event | category | flops | bytes accessed | tf_op | source)
XLA Modules:
  0.0 54.0 jit_solution(13690978628016246804)
XLA Ops:
  0.0 0.0 copy-start.2
  0.0 2.9 %shard_map.82._ = bf16[16,2048]{1,0:T(8,128)(2,1)S(1)} custom-call(s32[4,16]{1,0:T(4,128)} %ids_ref.3, bf16[1024,2048]{1,0:T(8,128)(2,1)} %embed_ref.1), custom_call_target="tpu_custom_call" | custom-call | tf_op jit(solution)/shard_map/pallas_call | solution.py:62
  2.9 4.1 %collective-permute-start.3 = (bf16[16,2048]{1,0:T(8,128)(2,1)S(1)}, bf16[16,2048]{1,0:T(8,128)(2,1)S(1)}, u32[]{:S(2)}, u32[]{:S(2)}) collective-permute-start(bf16[16,2048]{1,0:T(8,128)(2,1)S(1)} %shard_map.82._), channel_id=1, source_target_pairs={{0,4},{1,5},{2,6},{3,7},{4,0},{5,1},{6,2},{7,3},{8,12},{9,13},{10,... | collective-permute-start | bytes 196616 | tf_op jit(solution)/shard_map/ppermute | solution.py:40
  7.0 1.1 %shard_map.83 = (bf16[64,128]{1,0:T(8,128)(2,1)S(1)}, f32[8,128]{1,0:T(8,128)S(1)}) custom-call(bf16[16,2048]{1,0:T(8,128)(2,1)S(1)} %shard_map.82._, s32[4,16]{1,0:T(4,128)} %ids_ref.3), custom_call_target="tpu_custom_call" | custom-call | tf_op jit(solution)/shard_map/pallas_call | solution.py:62
  8.1 0.5 slice.3
  9.3 0.0 copy-done.2
  9.3 0.0 copy-start.1
  9.4 2.4 %shard_map.84.refs_1_ = bf16[2048,1024]{1,0:T(8,128)(2,1)S(1)} custom-call(bf16[64,2048]{1,0:T(8,128)(2,1)S(1)} %get-tuple-element.57._.rest_ref, bf16[2048,1024]{1,0:T(8,128)(2,1)} %source_ref.2), custom_call_target="tpu_custom_call" | custom-call | tf_op jit(solution)/shard_map/pallas_call | solution.py:62
  11.7 0.0 collective-permute-done.3
  11.8 1.0 %copy-done.1 = bf16[1024,2048]{1,0:T(8,128)(2,1)S(1)} copy-done((bf16[1024,2048]{1,0:T(8,128)(2,1)S(1)}, bf16[1024,2048]{1,0:T(8,128)(2,1)}, u32[]{:S(2)}) %copy-start.1) | copy-done | bytes 4194328
  12.8 0.0 copy-start
  12.8 0.0 collective-permute-start.14
  12.8 2.5 %collective-permute-start.4 = (bf16[32,2048]{1,0:T(8,128)(2,1)S(1)}, bf16[32,2048]{1,0:T(8,128)(2,1)S(1)}, u32[]{:S(2)}, u32[]{:S(2)}) collective-permute-start(bf16[32,2048]{1,0:T(8,128)(2,1)S(1)} %pad_maximum_fusion.refs_0_._), channel_id=1, source_target_pairs={{0,3},{1,2},{2,1},{3,0},{4,7},{5,6},{6,5},{7,4},{8,11},{9,10},{10,... | collective-permute-start | bytes 393224 | tf_op jit(solution)/shard_map/ppermute | solution.py:40
  15.3 0.4 collective-permute-start.5
  15.8 0.5 collective-permute-start.6
  16.3 2.2 %shard_map.86.refs_2_ = bf16[2048,1024]{1,0:T(8,128)(2,1)S(1)} custom-call(bf16[32,2048]{1,0:T(8,128)(2,1)S(1)} %pad_maximum_fusion.refs_0_._, bf16[2048,1024]{1,0:T(8,128)(2,1)} %source_ref.3), custom_call_target="tpu_custom_call" | custom-call | tf_op jit(solution)/shard_map/pallas_call | solution.py:62
  18.5 1.2 %shard_map.91 = (bf16[512,512]{1,0:T(8,128)(2,1)S(1)}, bf16[512,512]{1,0:T(8,128)(2,1)S(1)}) custom-call(bf16[32,2048]{1,0:T(8,128)(2,1)S(1)} %pad_maximum_fusion.refs_0_._, bf16[512,1024]{1,0:T(8,128)(2,1)} %keys_ref.3, bf16[512,1024]{1,0:T(8,128)(2,1)} %values_ref.3), custom_call_target="tpu_custom_call" | custom-call | tf_op jit(solution)/shard_map/pallas_call | solution.py:62
  19.7 0.1 collective-permute-start.10
  19.8 0.2 collective-permute-done.4.refs_1_
  20.0 0.3 collective-permute-start.9
  20.3 2.2 %collective-permute-done.5.refs_2_ = bf16[32,2048]{1,0:T(8,128)(2,1)S(1)} collective-permute-done((bf16[32,2048]{1,0:T(8,128)(2,1)S(1)}, bf16[32,2048]{1,0:T(8,128)(2,1)S(1)}, u32[]{:S(2)}, u32[]{:S(2)}) %collective-permute-start.5) | collective-permute-done | bytes 131104 | tf_op jit(solution)/shard_map/ppermute | solution.py:40
  22.5 0.0 collective-permute-done.6.refs_3_
  22.5 0.2 shard_map.85.rows_ref
  22.7 0.0 copy-done
  22.7 1.2 %shard_map.88 = bf16[64,1536]{1,0:T(8,128)(2,1)S(1)} custom-call(bf16[64,2048]{1,0:T(8,128)(2,1)S(1)} %shard_map.85.rows_ref, bf16[2048,1024]{1,0:T(8,128)(2,1)S(1)} %copy-done, bf16[2048,1024]{1,0:T(8,128)(2,1)S(1)} %shard_map.84.refs_1_, bf16[2048,1024]{1,0:T(8,128)(2,1)S(1)} %shard_map.86.refs_2_), custom_call_target="tpu_custom_call" | custom-call | tf_op jit(solution)/shard_map/pallas_call | solution.py:62
  24.0 0.1 collective-permute-start.7
  24.1 1.2 %shard_map.87.own_ref = f32[64,1536]{1,0:T(8,128)S(1)} custom-call(bf16[64,2048]{1,0:T(8,128)(2,1)S(1)} %shard_map.85.rows_ref, bf16[2048,1024]{1,0:T(8,128)(2,1)S(1)} %copy-done, bf16[2048,1024]{1,0:T(8,128)(2,1)S(1)} %shard_map.84.refs_1_, bf16[2048,1024]{1,0:T(8,128)(2,1)S(1)} %shard_map.86.refs_2_), custom_call_target="tpu_custom_call" | custom-call | tf_op jit(solution)/shard_map/pallas_call | solution.py:62
  25.3 0.2 collective-permute-done.7.received_ref
  25.5 0.1 shard_map.89
  25.6 1.6 %collective-permute-start.8 = (bf16[128,512]{1,0:T(8,128)(2,1)S(1)}, bf16[128,512]{1,0:T(8,128)(2,1)S(1)}, u32[]{:S(2)}, u32[]{:S(2)}) collective-permute-start(bf16[128,512]{1,0:T(8,128)(2,1)S(1)} %get-tuple-element.38), channel_id=1, source_target_pairs={{0,16},{1,17},{2,18},{3,19},{4,20},{5,21},{6,22},{7,23},{8,24},{9,... | collective-permute-start | bytes 393224 | tf_op jit(solution)/shard_map/ppermute | solution.py:40
  27.1 0.1 fusion.2
  27.3 0.1 pad_maximum_fusion.1
  27.3 1.2 %shard_map.90.refs_2_ = bf16[1024,512]{1,0:T(8,128)(2,1)S(1)} custom-call(f32[128,512]{1,0:T(8,128)S(1)} %get-tuple-element.37._.refs_0_, bf16[512,1024]{1,0:T(8,128)(2,1)} %keys_ref.3, bf16[512,1024]{1,0:T(8,128)(2,1)} %values_ref.3), custom_call_target="tpu_custom_call" | custom-call | tf_op jit(solution)/shard_map/pallas_call | solution.py:62
  28.6 2.8 %collective-permute-done.8.refs_1_ = bf16[128,512]{1,0:T(8,128)(2,1)S(1)} collective-permute-done((bf16[128,512]{1,0:T(8,128)(2,1)S(1)}, bf16[128,512]{1,0:T(8,128)(2,1)S(1)}, u32[]{:S(2)}, u32[]{:S(2)}) %collective-permute-start.8) | collective-permute-done | bytes 131104 | tf_op jit(solution)/shard_map/ppermute | solution.py:40
  31.4 0.0 collective-permute-done.10.refs_4_
  31.4 0.0 collective-permute-done.9.refs_3_
  31.4 1.2 %shard_map.92 = (bf16[32,640]{1,0:T(8,128)(2,1)S(1)}, bf16[32,640]{1,0:T(8,128)(2,1)S(1)}) custom-call(f32[128,512]{1,0:T(8,128)S(1)} %get-tuple-element.37._.refs_0_, bf16[128,512]{1,0:T(8,128)(2,1)S(1)} %collective-permute-done.8.refs_1_, bf16[1024,512]{1,0:T(8,128)(2,1)S(1)} %shard_map.90.refs_2_, bf16[512,512]{1,0:T(8,128)(2,1)S(1)} %collective-permute-done.9.refs_3_, ...), custom_call_target="tpu_custom_call" | custom-call | tf_op jit(solution)/shard_map/pallas_call | solution.py:62
  32.6 0.1 collective-permute-start.11
  32.7 1.6 %collective-permute-start.12 = (bf16[32,640]{1,0:T(8,128)(2,1)S(1)}, bf16[32,640]{1,0:T(8,128)(2,1)S(1)}, u32[]{:S(2)}, u32[]{:S(2)}) collective-permute-start(bf16[32,640]{1,0:T(8,128)(2,1)S(1)} %get-tuple-element.41.refs_0_), channel_id=1, source_target_pairs={{0,16},{1,17},{2,18},{3,19},{4,20},{5,21},{6,22},{7,23},{8,24},{9,... | collective-permute-start | bytes 122888 | tf_op jit(solution)/shard_map/ppermute | solution.py:40
  34.3 0.3 collective-permute-start.13
  34.5 0.0 collective-permute-done.11.refs_1_
  34.5 2.2 %collective-permute-done.12.refs_2_ = bf16[32,640]{1,0:T(8,128)(2,1)S(1)} collective-permute-done((bf16[32,640]{1,0:T(8,128)(2,1)S(1)}, bf16[32,640]{1,0:T(8,128)(2,1)S(1)}, u32[]{:S(2)}, u32[]{:S(2)}) %collective-permute-start.12) | collective-permute-done | bytes 40992 | tf_op jit(solution)/shard_map/ppermute | solution.py:40
  36.7 1.0 %collective-permute-done.13.refs_3_ = bf16[32,640]{1,0:T(8,128)(2,1)S(1)} collective-permute-done((bf16[32,640]{1,0:T(8,128)(2,1)S(1)}, bf16[32,640]{1,0:T(8,128)(2,1)S(1)}, u32[]{:S(2)}, u32[]{:S(2)}) %collective-permute-start.13) | collective-permute-done | bytes 40992 | tf_op jit(solution)/shard_map/ppermute | solution.py:40
  37.8 0.0 collective-permute-done.14.refs_5_
  37.8 1.9 %shard_map.93 = (f32[2,16,1024]{2,1,0:T(8,128)S(1)}, bf16[2,16,1024]{2,1,0:T(8,128)(2,1)S(1)}, bf16[2,16,1024]{2,1,0:T(8,128)(2,1)S(1)}, bf16[2,16,1024]{2,1,0:T(8,128)(2,1)S(1)}) custom-call(bf16[32,640]{1,0:T(8,128)(2,1)S(1)} %get-tuple-element.41.refs_0_, bf16[32,640]{1,0:T(8,128)(2,1)S(1)} %collective-permute-done.11.refs_1_, ...), custom_call_target="tpu_custom_call" | custom-call | tf_op jit(solution)/shard_map/pallas_call | solution.py:62
  39.7 1.8 %collective-permute-start.15 = (bf16[2,16,1024]{2,1,0:T(8,128)(2,1)S(1)}, bf16[2,16,1024]{2,1,0:T(8,128)(2,1)S(1)}, u32[]{:S(2)}, u32[]{:S(2)}) collective-permute-start(bf16[2,16,1024]{2,1,0:T(8,128)(2,1)S(1)} %get-tuple-element.44), channel_id=1, source_target_pairs={{0,17},{1,16},{2,19},{3,18},{4,21},{5,20},{6,23},{7,22},{8,25},{9,... | collective-permute-start | bytes 196616 | tf_op jit(solution)/shard_map/ppermute | solution.py:40
  41.4 0.6 %collective-permute-start.16 = (bf16[2,16,1024]{2,1,0:T(8,128)(2,1)S(1)}, bf16[2,16,1024]{2,1,0:T(8,128)(2,1)S(1)}, u32[]{:S(2)}, u32[]{:S(2)}) collective-permute-start(bf16[2,16,1024]{2,1,0:T(8,128)(2,1)S(1)} %get-tuple-element.45), channel_id=1, source_target_pairs={{0,1},{1,0},{2,3},{3,2},{4,5},{5,4},{6,7},{7,6},{8,9},{9,8},{10,11... | collective-permute-start | bytes 196616 | tf_op jit(solution)/shard_map/ppermute | solution.py:40
  42.0 1.2 %collective-permute-start.17 = (bf16[2,16,1024]{2,1,0:T(8,128)(2,1)S(1)}, bf16[2,16,1024]{2,1,0:T(8,128)(2,1)S(1)}, u32[]{:S(2)}, u32[]{:S(2)}) collective-permute-start(bf16[2,16,1024]{2,1,0:T(8,128)(2,1)S(1)} %get-tuple-element.46), channel_id=1, source_target_pairs={{0,16},{1,17},{2,18},{3,19},{4,20},{5,21},{6,22},{7,23},{8,24},{9,... | collective-permute-start | bytes 196616 | tf_op jit(solution)/shard_map/ppermute | solution.py:40
  43.2 2.0 %collective-permute-done.15.refs_0_ = bf16[2,16,1024]{2,1,0:T(8,128)(2,1)S(1)} collective-permute-done((bf16[2,16,1024]{2,1,0:T(8,128)(2,1)S(1)}, bf16[2,16,1024]{2,1,0:T(8,128)(2,1)S(1)}, u32[]{:S(2)}, u32[]{:S(2)}) %collective-permute-start.15) | collective-permute-done | bytes 65568 | tf_op jit(solution)/shard_map/ppermute | solution.py:40
  45.2 0.5 collective-permute-done.16.refs_1_
  45.7 0.6 %collective-permute-done.17.refs_2_ = bf16[2,16,1024]{2,1,0:T(8,128)(2,1)S(1)} collective-permute-done((bf16[2,16,1024]{2,1,0:T(8,128)(2,1)S(1)}, bf16[2,16,1024]{2,1,0:T(8,128)(2,1)S(1)}, u32[]{:S(2)}, u32[]{:S(2)}) %collective-permute-start.17) | collective-permute-done | bytes 65568 | tf_op jit(solution)/shard_map/ppermute | solution.py:40
  46.4 1.4 %collective-permute-start.18 = (bf16[16,1024]{1,0:T(8,128)(2,1)S(1)}, bf16[16,1024]{1,0:T(8,128)(2,1)S(1)}, u32[]{:S(2)}, u32[]{:S(2)}) collective-permute-start(bf16[16,1024]{1,0:T(8,128)(2,1)S(1)} %get-tuple-element.49), channel_id=1, source_target_pairs={{0,6},{1,7},{2,4},{3,5},{4,2},{5,3},{6,0},{7,1},{8,14},{9,15},{10,... | collective-permute-start | bytes 98312 | tf_op jit(solution)/shard_map/ppermute | solution.py:40
  47.8 1.7 %collective-permute-start.19 = (bf16[16,1024]{1,0:T(8,128)(2,1)S(1)}, bf16[16,1024]{1,0:T(8,128)(2,1)S(1)}, u32[]{:S(2)}, u32[]{:S(2)}) collective-permute-start(bf16[16,1024]{1,0:T(8,128)(2,1)S(1)} %get-tuple-element.50), channel_id=1, source_target_pairs={{0,4},{1,5},{2,6},{3,7},{4,0},{5,1},{6,2},{7,3},{8,12},{9,13},{10,... | collective-permute-start | bytes 98312 | tf_op jit(solution)/shard_map/ppermute | solution.py:40
  49.5 1.3 %collective-permute-start.20 = (bf16[16,1024]{1,0:T(8,128)(2,1)S(1)}, bf16[16,1024]{1,0:T(8,128)(2,1)S(1)}, u32[]{:S(2)}, u32[]{:S(2)}) collective-permute-start(bf16[16,1024]{1,0:T(8,128)(2,1)S(1)} %get-tuple-element.51), channel_id=1, source_target_pairs={{0,2},{1,3},{2,0},{3,1},{4,6},{5,7},{6,4},{7,5},{8,10},{9,11},{10,... | collective-permute-start | bytes 98312 | tf_op jit(solution)/shard_map/ppermute | solution.py:40
  50.8 1.5 %collective-permute-done.18.refs_1_ = bf16[16,1024]{1,0:T(8,128)(2,1)S(1)} collective-permute-done((bf16[16,1024]{1,0:T(8,128)(2,1)S(1)}, bf16[16,1024]{1,0:T(8,128)(2,1)S(1)}, u32[]{:S(2)}, u32[]{:S(2)}) %collective-permute-start.18) | collective-permute-done | bytes 32800 | tf_op jit(solution)/shard_map/ppermute | solution.py:40
  52.3 0.7 %collective-permute-done.19.refs_2_ = bf16[16,1024]{1,0:T(8,128)(2,1)S(1)} collective-permute-done((bf16[16,1024]{1,0:T(8,128)(2,1)S(1)}, bf16[16,1024]{1,0:T(8,128)(2,1)S(1)}, u32[]{:S(2)}, u32[]{:S(2)}) %collective-permute-start.19) | collective-permute-done | bytes 32800 | tf_op jit(solution)/shard_map/ppermute | solution.py:40
  53.0 0.4 collective-permute-done.20.refs_3_
  53.4 0.6 %shard_map.95 = bf16[16,1024]{1,0:T(8,128)(2,1)} custom-call(f32[16,1024]{1,0:T(8,128)S(1)} %get-tuple-element.48.refs_0_, bf16[16,1024]{1,0:T(8,128)(2,1)S(1)} %collective-permute-done.18.refs_1_, bf16[16,1024]{1,0:T(8,128)(2,1)S(1)} %collective-permute-done.19.refs_2_, bf16[16,1024]{1,0:T(8,128)(2,1)S(1)} %collective-permute-done.20.refs_3_), custom_call_target="tpu_custom_call" | custom-call | tf_op jit(solution)/shard_map/pallas_call | solution.py:62
  (6 shorter events, 0.1 us)
Async XLA Ops:
  0.0 9.3 %copy-start.2 = (s32[4,16]{1,0:T(4,128)S(1)}, s32[4,16]{1,0:T(4,128)}, u32[]{:S(2)}) copy-start(s32[4,16]{1,0:T(4,128)} %ids_ref.3) | copy-start | bytes 772
  2.9 8.8 %collective-permute-start.3 = (bf16[16,2048]{1,0:T(8,128)(2,1)S(1)}, bf16[16,2048]{1,0:T(8,128)(2,1)S(1)}, u32[]{:S(2)}, u32[]{:S(2)}) collective-permute-start(bf16[16,2048]{1,0:T(8,128)(2,1)S(1)} %shard_map.82._), channel_id=1, source_target_pairs={{0,4},{1,5},{2,6},{3,7},{4,0},{5,1},{6,2},{7,3},{8,12},{9,13},{10,... | collective-permute-start | bytes 196616 | tf_op jit(solution)/shard_map/ppermute | solution.py:40
  9.3 3.5 %copy-start.1 = (bf16[1024,2048]{1,0:T(8,128)(2,1)S(1)}, bf16[1024,2048]{1,0:T(8,128)(2,1)}, u32[]{:S(2)}) copy-start(bf16[1024,2048]{1,0:T(8,128)(2,1)} %refs_4_.1) | copy-start | bytes 12582916
  12.8 9.9 %copy-start = (bf16[2048,1024]{1,0:T(8,128)(2,1)S(1)}, bf16[2048,1024]{1,0:T(8,128)(2,1)}, u32[]{:S(2)}) copy-start(bf16[2048,1024]{1,0:T(8,128)(2,1)} %refs_0_.3) | copy-start | bytes 12582916
  12.8 25.0 %collective-permute-start.14 = (bf16[1024,2048]{1,0:T(8,128)(2,1)S(1)}, bf16[1024,2048]{1,0:T(8,128)(2,1)S(1)}, u32[]{:S(2)}, u32[]{:S(2)}) collective-permute-start(bf16[1024,2048]{1,0:T(8,128)(2,1)S(1)} %copy-done.1), channel_id=1, source_target_pairs={{0,8},{1,9},{2,10},{3,11},{4,12},{5,13},{6,14},{7,15},{8,0},{9,1},... | collective-permute-start | bytes 12582920 | tf_op jit(solution)/shard_map/ppermute | solution.py:40
  12.8 7.2 %collective-permute-start.4 = (bf16[32,2048]{1,0:T(8,128)(2,1)S(1)}, bf16[32,2048]{1,0:T(8,128)(2,1)S(1)}, u32[]{:S(2)}, u32[]{:S(2)}) collective-permute-start(bf16[32,2048]{1,0:T(8,128)(2,1)S(1)} %pad_maximum_fusion.refs_0_._), channel_id=1, source_target_pairs={{0,3},{1,2},{2,1},{3,0},{4,7},{5,6},{6,5},{7,4},{8,11},{9,10},{10,... | collective-permute-start | bytes 393224 | tf_op jit(solution)/shard_map/ppermute | solution.py:40
  15.3 7.2 %collective-permute-start.5 = (bf16[32,2048]{1,0:T(8,128)(2,1)S(1)}, bf16[32,2048]{1,0:T(8,128)(2,1)S(1)}, u32[]{:S(2)}, u32[]{:S(2)}) collective-permute-start(bf16[32,2048]{1,0:T(8,128)(2,1)S(1)} %pad_maximum_fusion.refs_0_._), channel_id=1, source_target_pairs={{0,2},{1,3},{2,0},{3,1},{4,6},{5,7},{6,4},{7,5},{8,10},{9,11},{10,... | collective-permute-start | bytes 393224 | tf_op jit(solution)/shard_map/ppermute | solution.py:40
  15.8 6.7 %collective-permute-start.6 = (bf16[32,2048]{1,0:T(8,128)(2,1)S(1)}, bf16[32,2048]{1,0:T(8,128)(2,1)S(1)}, u32[]{:S(2)}, u32[]{:S(2)}) collective-permute-start(bf16[32,2048]{1,0:T(8,128)(2,1)S(1)} %pad_maximum_fusion.refs_0_._), channel_id=1, source_target_pairs={{0,1},{1,0},{2,3},{3,2},{4,5},{5,4},{6,7},{7,6},{8,9},{9,8},{10,11... | collective-permute-start | bytes 393224 | tf_op jit(solution)/shard_map/ppermute | solution.py:40
  19.7 11.6 %collective-permute-start.10 = (bf16[512,512]{1,0:T(8,128)(2,1)S(1)}, bf16[512,512]{1,0:T(8,128)(2,1)S(1)}, u32[]{:S(2)}, u32[]{:S(2)}) collective-permute-start(bf16[512,512]{1,0:T(8,128)(2,1)S(1)} %get-tuple-element.40), channel_id=1, source_target_pairs={{0,8},{1,9},{2,10},{3,11},{4,12},{5,13},{6,14},{7,15},{8,0},{9,1},... | collective-permute-start | bytes 1572872 | tf_op jit(solution)/shard_map/ppermute | solution.py:40
  20.0 11.4 %collective-permute-start.9 = (bf16[512,512]{1,0:T(8,128)(2,1)S(1)}, bf16[512,512]{1,0:T(8,128)(2,1)S(1)}, u32[]{:S(2)}, u32[]{:S(2)}) collective-permute-start(bf16[512,512]{1,0:T(8,128)(2,1)S(1)} %get-tuple-element.39), channel_id=1, source_target_pairs={{0,8},{1,9},{2,10},{3,11},{4,12},{5,13},{6,14},{7,15},{8,0},{9,1},... | collective-permute-start | bytes 1572872 | tf_op jit(solution)/shard_map/ppermute | solution.py:40
  24.0 1.5 %collective-permute-start.7 = (bf16[64,1536]{1,0:T(8,128)(2,1)S(1)}, bf16[64,1536]{1,0:T(8,128)(2,1)S(1)}, u32[]{:S(2)}, u32[]{:S(2)}) collective-permute-start(bf16[64,1536]{1,0:T(8,128)(2,1)S(1)} %shard_map.88), channel_id=1, source_target_pairs={{0,8},{1,9},{2,10},{3,11},{4,12},{5,13},{6,14},{7,15},{8,0},{9,1},... | collective-permute-start | bytes 589832 | tf_op jit(solution)/shard_map/ppermute | solution.py:40
  25.6 5.8 %collective-permute-start.8 = (bf16[128,512]{1,0:T(8,128)(2,1)S(1)}, bf16[128,512]{1,0:T(8,128)(2,1)S(1)}, u32[]{:S(2)}, u32[]{:S(2)}) collective-permute-start(bf16[128,512]{1,0:T(8,128)(2,1)S(1)} %get-tuple-element.38), channel_id=1, source_target_pairs={{0,16},{1,17},{2,18},{3,19},{4,20},{5,21},{6,22},{7,23},{8,24},{9,... | collective-permute-start | bytes 393224 | tf_op jit(solution)/shard_map/ppermute | solution.py:40
  32.6 1.9 %collective-permute-start.11 = (bf16[32,640]{1,0:T(8,128)(2,1)S(1)}, bf16[32,640]{1,0:T(8,128)(2,1)S(1)}, u32[]{:S(2)}, u32[]{:S(2)}) collective-permute-start(bf16[32,640]{1,0:T(8,128)(2,1)S(1)} %get-tuple-element.42), channel_id=1, source_target_pairs={{0,8},{1,9},{2,10},{3,11},{4,12},{5,13},{6,14},{7,15},{8,0},{9,1},... | collective-permute-start | bytes 122888 | tf_op jit(solution)/shard_map/ppermute | solution.py:40
  32.7 4.1 %collective-permute-start.12 = (bf16[32,640]{1,0:T(8,128)(2,1)S(1)}, bf16[32,640]{1,0:T(8,128)(2,1)S(1)}, u32[]{:S(2)}, u32[]{:S(2)}) collective-permute-start(bf16[32,640]{1,0:T(8,128)(2,1)S(1)} %get-tuple-element.41.refs_0_), channel_id=1, source_target_pairs={{0,16},{1,17},{2,18},{3,19},{4,20},{5,21},{6,22},{7,23},{8,24},{9,... | collective-permute-start | bytes 122888 | tf_op jit(solution)/shard_map/ppermute | solution.py:40
  34.3 3.5 %collective-permute-start.13 = (bf16[32,640]{1,0:T(8,128)(2,1)S(1)}, bf16[32,640]{1,0:T(8,128)(2,1)S(1)}, u32[]{:S(2)}, u32[]{:S(2)}) collective-permute-start(bf16[32,640]{1,0:T(8,128)(2,1)S(1)} %get-tuple-element.42), channel_id=1, source_target_pairs={{0,24},{1,25},{2,26},{3,27},{4,28},{5,29},{6,30},{7,31},{8,16},{9,... | collective-permute-start | bytes 122888 | tf_op jit(solution)/shard_map/ppermute | solution.py:40
  39.7 5.6 %collective-permute-start.15 = (bf16[2,16,1024]{2,1,0:T(8,128)(2,1)S(1)}, bf16[2,16,1024]{2,1,0:T(8,128)(2,1)S(1)}, u32[]{:S(2)}, u32[]{:S(2)}) collective-permute-start(bf16[2,16,1024]{2,1,0:T(8,128)(2,1)S(1)} %get-tuple-element.44), channel_id=1, source_target_pairs={{0,17},{1,16},{2,19},{3,18},{4,21},{5,20},{6,23},{7,22},{8,25},{9,... | collective-permute-start | bytes 196616 | tf_op jit(solution)/shard_map/ppermute | solution.py:40
  41.4 4.3 %collective-permute-start.16 = (bf16[2,16,1024]{2,1,0:T(8,128)(2,1)S(1)}, bf16[2,16,1024]{2,1,0:T(8,128)(2,1)S(1)}, u32[]{:S(2)}, u32[]{:S(2)}) collective-permute-start(bf16[2,16,1024]{2,1,0:T(8,128)(2,1)S(1)} %get-tuple-element.45), channel_id=1, source_target_pairs={{0,1},{1,0},{2,3},{3,2},{4,5},{5,4},{6,7},{7,6},{8,9},{9,8},{10,11... | collective-permute-start | bytes 196616 | tf_op jit(solution)/shard_map/ppermute | solution.py:40
  42.0 4.3 %collective-permute-start.17 = (bf16[2,16,1024]{2,1,0:T(8,128)(2,1)S(1)}, bf16[2,16,1024]{2,1,0:T(8,128)(2,1)S(1)}, u32[]{:S(2)}, u32[]{:S(2)}) collective-permute-start(bf16[2,16,1024]{2,1,0:T(8,128)(2,1)S(1)} %get-tuple-element.46), channel_id=1, source_target_pairs={{0,16},{1,17},{2,18},{3,19},{4,20},{5,21},{6,22},{7,23},{8,24},{9,... | collective-permute-start | bytes 196616 | tf_op jit(solution)/shard_map/ppermute | solution.py:40
  46.4 5.9 %collective-permute-start.18 = (bf16[16,1024]{1,0:T(8,128)(2,1)S(1)}, bf16[16,1024]{1,0:T(8,128)(2,1)S(1)}, u32[]{:S(2)}, u32[]{:S(2)}) collective-permute-start(bf16[16,1024]{1,0:T(8,128)(2,1)S(1)} %get-tuple-element.49), channel_id=1, source_target_pairs={{0,6},{1,7},{2,4},{3,5},{4,2},{5,3},{6,0},{7,1},{8,14},{9,15},{10,... | collective-permute-start | bytes 98312 | tf_op jit(solution)/shard_map/ppermute | solution.py:40
  47.8 5.2 %collective-permute-start.19 = (bf16[16,1024]{1,0:T(8,128)(2,1)S(1)}, bf16[16,1024]{1,0:T(8,128)(2,1)S(1)}, u32[]{:S(2)}, u32[]{:S(2)}) collective-permute-start(bf16[16,1024]{1,0:T(8,128)(2,1)S(1)} %get-tuple-element.50), channel_id=1, source_target_pairs={{0,4},{1,5},{2,6},{3,7},{4,0},{5,1},{6,2},{7,3},{8,12},{9,13},{10,... | collective-permute-start | bytes 98312 | tf_op jit(solution)/shard_map/ppermute | solution.py:40
  49.5 3.9 %collective-permute-start.20 = (bf16[16,1024]{1,0:T(8,128)(2,1)S(1)}, bf16[16,1024]{1,0:T(8,128)(2,1)S(1)}, u32[]{:S(2)}, u32[]{:S(2)}) collective-permute-start(bf16[16,1024]{1,0:T(8,128)(2,1)S(1)} %get-tuple-element.51), channel_id=1, source_target_pairs={{0,2},{1,3},{2,0},{3,1},{4,6},{5,7},{6,4},{7,5},{8,10},{9,11},{10,... | collective-permute-start | bytes 98312 | tf_op jit(solution)/shard_map/ppermute | solution.py:40

commit v3 on v2

--- a/solution.py
+++ b/solution.py
@@ -70,27 +70,18 @@
     )(*args)
 
 
-def iota(shape, axis):
-    return lax.broadcasted_iota(jnp.int32, shape, axis)
-
-
-def id_columns(plan, ids):
-    steps = plan.steps
-    corner = iota((steps, steps), 0) == iota((steps, steps), 1)
-    columns = []
-    for cand in range(plan.cands):
-        row = ids[cand : cand + 1, :].astype(F32)
-        columns.append(jnp.sum(jnp.where(corner, row, 0.0), axis=1, keepdims=True))
-    return jnp.concatenate(columns)
-
-
 def pick(plan, gen_ids, embed_rows):
     vocab = embed_rows.shape[0]
-    tokens, room = plan.tokens, plan.room
+    tokens, steps, room = plan.tokens, plan.steps, plan.room
     cut = 2 * HD
     pieces = vocab // cut
-
-    def kernel(ids_ref, embed_ref, rows_ref, ids, held, found, ids_sem, sems):
+    slots = plan.head * room
+
+    def iota(shape, axis):
+        return lax.broadcasted_iota(jnp.int32, shape, axis)
+
+    def kernel(ids_ref, embed_ref, rows_ref, places_ref, beyond_ref, *scratch):
+        ids, held, found, ids_sem, sems = scratch
         ids_copy = pltpu.make_async_copy(ids_ref, ids, ids_sem)
         ids_copy.start()
         copies = []
@@ -99,17 +90,41 @@
             copies.append(
                 pltpu.make_async_copy(embed_ref.at[window], held.at[window], sems.at[piece])
             )
-            copies[-1].start()
-        base = (lax.axis_index("head") * vocab).astype(F32)
+            copies[-1].start(priority=piece % 2)
+        me = lax.axis_index("head")
+        ids_copy.wait()
+        corner = iota((steps, steps), 0) == iota((steps, steps), 1)
+        columns = []
+        for cand in range(plan.cands):
+            row = ids[cand : cand + 1, :].astype(F32)
+            columns.append(jnp.sum(jnp.where(corner, row, 0.0), axis=1, keepdims=True))
+        id_column = jnp.concatenate(columns)
+        owner_column = id_column.astype(jnp.int32) // vocab
+
+        member = (owner_column == iota((tokens, HD), 1)).astype(F32).astype(BF16)
+        same = lax.dot_general(
+            member, member, (((1,), (1,)), ((), ())), preferred_element_type=F32
+        )
         first, second = iota((tokens, tokens), 0), iota((tokens, tokens), 1)
-        ids_copy.wait()
-        column = id_columns(plan, ids) - base
-        local = (column >= 0) & (column < vocab)
-        row = jnp.sum(jnp.where(first == second, column, 0.0), axis=0, keepdims=True)
-        earlier = jnp.where((first < second) & local, 1.0, 0.0)
-        rank = jnp.sum(earlier, axis=0, keepdims=True)
-        wanted = (row >= 0) & (row < vocab) & (rank == iota((room, tokens), 0).astype(F32))
-        chosen = jnp.sum(jnp.where(wanted, row + 1.0, 0.0), axis=1, keepdims=True) - 1.0
+        rank_column = jnp.sum(jnp.where(second < first, same, 0.0), axis=1, keepdims=True)
+        rank_row = jnp.sum(jnp.where(first < second, same, 0.0), axis=0, keepdims=True)
+        id_row = jnp.sum(jnp.where(first == second, id_column, 0.0), axis=0, keepdims=True)
+        beyond = jnp.sum(jnp.where(rank_column >= room, 1.0, 0.0), axis=0, keepdims=True)
+        beyond_ref[...] = jnp.broadcast_to(beyond, beyond_ref.shape)
+
+        slot = iota((tokens, slots), 1)
+        place = slot // (plan.outer * room)
+        group = lax.rem(slot // room, plan.outer)
+        distance = lax.rem(plan.inner - place, plan.inner) + group * plan.inner
+        filled = (owner_column == (me ^ distance)) & (
+            rank_column == lax.rem(slot, room).astype(F32)
+        )
+        places_ref[...] = filled.astype(F32).astype(BF16)
+
+        local = id_row - (me * vocab).astype(F32)
+        wanted = (local >= 0) & (local < vocab)
+        wanted = wanted & (rank_row == iota((room, tokens), 0).astype(F32))
+        chosen = jnp.sum(jnp.where(wanted, local + 1.0, 0.0), axis=1, keepdims=True) - 1.0
         selector = (chosen == iota((room, vocab), 1).astype(F32)).astype(F32).astype(BF16)
         for piece, copy in enumerate(copies):
             window = slice(piece * cut, (piece + 1) * cut)
@@ -123,9 +138,13 @@
 
     return call(
         kernel,
-        jax.ShapeDtypeStruct((room, plan.features), BF16),
+        [
+            jax.ShapeDtypeStruct((room, plan.features), BF16),
+            jax.ShapeDtypeStruct((tokens, slots), BF16),
+            jax.ShapeDtypeStruct((8, HD), F32),
+        ],
         [ANY_SPEC] * 2,
-        VMEM_SPEC,
+        [VMEM_SPEC] * 3,
         [
             pltpu.VMEM(gen_ids.shape, jnp.int32),
             pltpu.VMEM(embed_rows.shape, BF16),
@@ -139,47 +158,6 @@
     )
 
 
-def find_places(plan, after, gen_ids, vocab):
-    tokens, room = plan.tokens, plan.room
-    slots = plan.head * room
-
-    def kernel(_, ids_ref, places_ref, beyond_ref, ids, ids_sem):
-        ids_copy = pltpu.make_async_copy(ids_ref, ids, ids_sem)
-        ids_copy.start()
-        ids_copy.wait()
-        owner = id_columns(plan, ids).astype(jnp.int32) // vocab
-        member = (owner == iota((tokens, HD), 1)).astype(F32).astype(BF16)
-        same = lax.dot_general(
-            member, member, (((1,), (1,)), ((), ())), preferred_element_type=F32
-        )
-        earlier = iota((tokens, tokens), 1) < iota((tokens, tokens), 0)
-        rank = jnp.sum(jnp.where(earlier, same, 0.0), axis=1, keepdims=True)
-        beyond = jnp.sum(jnp.where(rank >= room, 1.0, 0.0), axis=0, keepdims=True)
-        beyond_ref[...] = jnp.broadcast_to(beyond, beyond_ref.shape)
-        slot = iota((tokens, slots), 1)
-        place = slot // (plan.outer * room)
-        group = lax.rem(slot // room, plan.outer)
-        distance = lax.rem(plan.inner - place, plan.inner) + group * plan.inner
-        filled = (owner == (lax.axis_index("head") ^ distance)) & (
-            rank == lax.rem(slot, room).astype(F32)
-        )
-        places_ref[...] = filled.astype(F32).astype(BF16)
-
-    return call(
-        kernel,
-        [
-            jax.ShapeDtypeStruct((tokens, slots), BF16),
-            jax.ShapeDtypeStruct((8, HD), F32),
-        ],
-        [ANY_SPEC] * 2,
-        [VMEM_SPEC] * 2,
-        [pltpu.VMEM(gen_ids.shape, jnp.int32), pltpu.SemaphoreType.DMA],
-        8,
-        after,
-        in_hbm(gen_ids),
-    )
-
-
 def rows_beyond(plan, gen_ids, embed_rows):
     vocab = embed_rows.shape[0]
     ids = gen_ids.reshape(-1)
@@ -223,8 +201,8 @@
             )
             for k in range(pieces)
         ]
-        for copy in copies:
-            copy.start()
+        for k, copy in enumerate(copies):
+            copy.start(priority=k % 2)
         for copy in copies:
             copy.wait()
 
@@ -270,8 +248,7 @@
 def gather_embedded(
     plan, gen_ids, embed_rows, w_key, w_value, prompt_keys, prompt_values, w_out
 ):
-    rows = pick(plan, gen_ids, embed_rows)
-    places, beyond = find_places(plan, rows, gen_ids, embed_rows.shape[0])
+    rows, places, beyond = pick(plan, gen_ids, embed_rows)
     rest = lax.cond(
         beyond[0, 0] > 0.5,
         lambda: rows_beyond(plan, gen_ids, embed_rows),

time: 54.2 us -> 53.3 us (0.983)
  Pallas kernels: 17.5 us -> 16.3 us
    pallas_call x14 -> x13, Pallas kernels: 17.5 us -> 16.3 us  [call(): pl.pallas_call(kernel, out_shape=out_shape, in_specs=in_specs, out_specs=...]
  transfers between devices with their start and end apart: 18 -> 18, of which waited for: 12 -> 11; matrix products, arithmetic and copies ran while one was open for 1% -> 1% of each run, Pallas kernels for 22% -> 21%
where the time goes in v3:
time: 53.3 us; the launch traced here: 53.1 us
  starting transfers between devices  19.6 us (37%)
  Pallas kernels  16.3 us (31%)
  waiting for transfers between devices  14.6 us (27%)
  local copies, waits for them, and re-layouts  1.55 us (3%)
  between operations  0.83 us (2%)
    ppermute x18, starting transfers between devices, send(): return lax.ppermute(value, ('seq', 'head'), pairs)  19.6 us
    pallas_call x13, Pallas kernels, call(): pl.pallas_call(kernel, out_shape=out_shape, in_specs=in_specs, out_specs=...  16.3 us
    ppermute x18, waiting for transfers between devices, send(): return lax.ppermute(value, ('seq', 'head'), pairs)  14.6 us
  transfers between devices with their start and end apart: 18, of which 11 were waited for; matrix products, arithmetic and copies ran while one was open for 1% of the time, Pallas kernels for 21%

profile of v3, /device:TPU:0, one launch (start us, length us, event | category | flops | bytes accessed | tf_op | source)
XLA Modules:
  0.0 53.1 jit_solution(12435860371074461211)
XLA Ops:
  0.0 0.0 copy-start.2
  0.0 2.7 %shard_map.82 = (bf16[16,2048]{1,0:T(8,128)(2,1)S(1)}, bf16[64,128]{1,0:T(8,128)(2,1)S(1)}, f32[8,128]{1,0:T(8,128)S(1)}) custom-call(s32[4,16]{1,0:T(4,128)} %ids_ref.1, bf16[1024,2048]{1,0:T(8,128)(2,1)} %embed_ref.1), custom_call_target="tpu_custom_call" | custom-call | tf_op jit(solution)/shard_map/pallas_call | solution.py:62
  2.8 4.1 %collective-permute-start.3 = (bf16[16,2048]{1,0:T(8,128)(2,1)S(1)}, bf16[16,2048]{1,0:T(8,128)(2,1)S(1)}, u32[]{:S(2)}, u32[]{:S(2)}) collective-permute-start(bf16[16,2048]{1,0:T(8,128)(2,1)S(1)} %get-tuple-element.36), channel_id=1, source_target_pairs={{0,4},{1,5},{2,6},{3,7},{4,0},{5,1},{6,2},{7,3},{8,12},{9,13},{10,... | collective-permute-start | bytes 196616 | tf_op jit(solution)/shard_map/ppermute | solution.py:40
  6.9 0.5 slice.3
  8.0 0.0 copy-done.2
  8.1 0.0 copy-start.1
  8.1 2.4 %shard_map.83.refs_1_ = bf16[2048,1024]{1,0:T(8,128)(2,1)S(1)} custom-call(bf16[64,2048]{1,0:T(8,128)(2,1)S(1)} %get-tuple-element.59._.rest_ref, bf16[2048,1024]{1,0:T(8,128)(2,1)} %source_ref.2), custom_call_target="tpu_custom_call" | custom-call | tf_op jit(solution)/shard_map/pallas_call | solution.py:62
  10.5 0.0 collective-permute-done.3
  10.5 1.0 %copy-done.1 = bf16[1024,2048]{1,0:T(8,128)(2,1)S(1)} copy-done((bf16[1024,2048]{1,0:T(8,128)(2,1)S(1)}, bf16[1024,2048]{1,0:T(8,128)(2,1)}, u32[]{:S(2)}) %copy-start.1) | copy-done | bytes 4194328
  11.5 0.0 copy-start
  11.5 0.0 collective-permute-start.14
  11.5 2.5 %collective-permute-start.4 = (bf16[32,2048]{1,0:T(8,128)(2,1)S(1)}, bf16[32,2048]{1,0:T(8,128)(2,1)S(1)}, u32[]{:S(2)}, u32[]{:S(2)}) collective-permute-start(bf16[32,2048]{1,0:T(8,128)(2,1)S(1)} %pad_maximum_fusion.refs_0_._), channel_id=1, source_target_pairs={{0,3},{1,2},{2,1},{3,0},{4,7},{5,6},{6,5},{7,4},{8,11},{9,10},{10,... | collective-permute-start | bytes 393224 | tf_op jit(solution)/shard_map/ppermute | solution.py:40
  14.0 0.4 collective-permute-start.5
  14.5 0.5 %collective-permute-start.6 = (bf16[32,2048]{1,0:T(8,128)(2,1)S(1)}, bf16[32,2048]{1,0:T(8,128)(2,1)S(1)}, u32[]{:S(2)}, u32[]{:S(2)}) collective-permute-start(bf16[32,2048]{1,0:T(8,128)(2,1)S(1)} %pad_maximum_fusion.refs_0_._), channel_id=1, source_target_pairs={{0,1},{1,0},{2,3},{3,2},{4,5},{5,4},{6,7},{7,6},{8,9},{9,8},{10,11... | collective-permute-start | bytes 393224 | tf_op jit(solution)/shard_map/ppermute | solution.py:40
  15.0 2.2 %shard_map.85.refs_2_ = bf16[2048,1024]{1,0:T(8,128)(2,1)S(1)} custom-call(bf16[32,2048]{1,0:T(8,128)(2,1)S(1)} %pad_maximum_fusion.refs_0_._, bf16[2048,1024]{1,0:T(8,128)(2,1)} %source_ref.3), custom_call_target="tpu_custom_call" | custom-call | tf_op jit(solution)/shard_map/pallas_call | solution.py:62
  17.2 1.2 %shard_map.90 = (bf16[512,512]{1,0:T(8,128)(2,1)S(1)}, bf16[512,512]{1,0:T(8,128)(2,1)S(1)}) custom-call(bf16[32,2048]{1,0:T(8,128)(2,1)S(1)} %pad_maximum_fusion.refs_0_._, bf16[512,1024]{1,0:T(8,128)(2,1)} %keys_ref.3, bf16[512,1024]{1,0:T(8,128)(2,1)} %values_ref.3), custom_call_target="tpu_custom_call" | custom-call | tf_op jit(solution)/shard_map/pallas_call | solution.py:62
  18.5 0.1 collective-permute-start.10
  18.6 0.2 collective-permute-done.4.refs_1_
  18.7 0.3 collective-permute-start.9
  19.1 2.2 %collective-permute-done.5.refs_2_ = bf16[32,2048]{1,0:T(8,128)(2,1)S(1)} collective-permute-done((bf16[32,2048]{1,0:T(8,128)(2,1)S(1)}, bf16[32,2048]{1,0:T(8,128)(2,1)S(1)}, u32[]{:S(2)}, u32[]{:S(2)}) %collective-permute-start.5) | collective-permute-done | bytes 131104 | tf_op jit(solution)/shard_map/ppermute | solution.py:40
  21.2 0.0 collective-permute-done.6.refs_3_
  21.2 0.2 shard_map.84.rows_ref
  21.5 0.0 copy-done
  21.5 1.2 %shard_map.87 = bf16[64,1536]{1,0:T(8,128)(2,1)S(1)} custom-call(bf16[64,2048]{1,0:T(8,128)(2,1)S(1)} %shard_map.84.rows_ref, bf16[2048,1024]{1,0:T(8,128)(2,1)S(1)} %copy-done, bf16[2048,1024]{1,0:T(8,128)(2,1)S(1)} %shard_map.83.refs_1_, bf16[2048,1024]{1,0:T(8,128)(2,1)S(1)} %shard_map.85.refs_2_), custom_call_target="tpu_custom_call" | custom-call | tf_op jit(solution)/shard_map/pallas_call | solution.py:62
  22.7 0.1 collective-permute-start.7
  22.8 1.2 %shard_map.86.own_ref = f32[64,1536]{1,0:T(8,128)S(1)} custom-call(bf16[64,2048]{1,0:T(8,128)(2,1)S(1)} %shard_map.84.rows_ref, bf16[2048,1024]{1,0:T(8,128)(2,1)S(1)} %copy-done, bf16[2048,1024]{1,0:T(8,128)(2,1)S(1)} %shard_map.83.refs_1_, bf16[2048,1024]{1,0:T(8,128)(2,1)S(1)} %shard_map.85.refs_2_), custom_call_target="tpu_custom_call" | custom-call | tf_op jit(solution)/shard_map/pallas_call | solution.py:62
  24.1 0.2 collective-permute-done.7.received_ref
  24.2 0.1 shard_map.88
  24.3 1.6 %collective-permute-start.8 = (bf16[128,512]{1,0:T(8,128)(2,1)S(1)}, bf16[128,512]{1,0:T(8,128)(2,1)S(1)}, u32[]{:S(2)}, u32[]{:S(2)}) collective-permute-start(bf16[128,512]{1,0:T(8,128)(2,1)S(1)} %get-tuple-element.40), channel_id=1, source_target_pairs={{0,16},{1,17},{2,18},{3,19},{4,20},{5,21},{6,22},{7,23},{8,24},{9,... | collective-permute-start | bytes 393224 | tf_op jit(solution)/shard_map/ppermute | solution.py:40
  25.9 0.1 fusion.2
  26.0 0.1 pad_maximum_fusion.1
  26.1 1.2 %shard_map.89.refs_2_ = bf16[1024,512]{1,0:T(8,128)(2,1)S(1)} custom-call(f32[128,512]{1,0:T(8,128)S(1)} %get-tuple-element.39._.refs_0_, bf16[512,1024]{1,0:T(8,128)(2,1)} %keys_ref.3, bf16[512,1024]{1,0:T(8,128)(2,1)} %values_ref.3), custom_call_target="tpu_custom_call" | custom-call | tf_op jit(solution)/shard_map/pallas_call | solution.py:62
  27.3 2.8 %collective-permute-done.8.refs_1_ = bf16[128,512]{1,0:T(8,128)(2,1)S(1)} collective-permute-done((bf16[128,512]{1,0:T(8,128)(2,1)S(1)}, bf16[128,512]{1,0:T(8,128)(2,1)S(1)}, u32[]{:S(2)}, u32[]{:S(2)}) %collective-permute-start.8) | collective-permute-done | bytes 131104 | tf_op jit(solution)/shard_map/ppermute | solution.py:40
  30.1 0.0 collective-permute-done.10.refs_4_
  30.1 0.0 collective-permute-done.9.refs_3_
  30.1 1.2 %shard_map.91 = (bf16[32,640]{1,0:T(8,128)(2,1)S(1)}, bf16[32,640]{1,0:T(8,128)(2,1)S(1)}) custom-call(f32[128,512]{1,0:T(8,128)S(1)} %get-tuple-element.39._.refs_0_, bf16[128,512]{1,0:T(8,128)(2,1)S(1)} %collective-permute-done.8.refs_1_, bf16[1024,512]{1,0:T(8,128)(2,1)S(1)} %shard_map.89.refs_2_, bf16[512,512]{1,0:T(8,128)(2,1)S(1)} %collective-permute-done.9.refs_3_, ...), custom_call_target="tpu_custom_call" | custom-call | tf_op jit(solution)/shard_map/pallas_call | solution.py:62
  31.3 0.1 collective-permute-start.11
  31.4 1.6 %collective-permute-start.12 = (bf16[32,640]{1,0:T(8,128)(2,1)S(1)}, bf16[32,640]{1,0:T(8,128)(2,1)S(1)}, u32[]{:S(2)}, u32[]{:S(2)}) collective-permute-start(bf16[32,640]{1,0:T(8,128)(2,1)S(1)} %get-tuple-element.43.refs_0_), channel_id=1, source_target_pairs={{0,16},{1,17},{2,18},{3,19},{4,20},{5,21},{6,22},{7,23},{8,24},{9,... | collective-permute-start | bytes 122888 | tf_op jit(solution)/shard_map/ppermute | solution.py:40
  33.0 0.3 collective-permute-start.13
  33.3 0.0 collective-permute-done.11.refs_1_
  33.3 2.2 %collective-permute-done.12.refs_2_ = bf16[32,640]{1,0:T(8,128)(2,1)S(1)} collective-permute-done((bf16[32,640]{1,0:T(8,128)(2,1)S(1)}, bf16[32,640]{1,0:T(8,128)(2,1)S(1)}, u32[]{:S(2)}, u32[]{:S(2)}) %collective-permute-start.12) | collective-permute-done | bytes 40992 | tf_op jit(solution)/shard_map/ppermute | solution.py:40
  35.5 1.0 %collective-permute-done.13.refs_3_ = bf16[32,640]{1,0:T(8,128)(2,1)S(1)} collective-permute-done((bf16[32,640]{1,0:T(8,128)(2,1)S(1)}, bf16[32,640]{1,0:T(8,128)(2,1)S(1)}, u32[]{:S(2)}, u32[]{:S(2)}) %collective-permute-start.13) | collective-permute-done | bytes 40992 | tf_op jit(solution)/shard_map/ppermute | solution.py:40
  36.5 0.0 collective-permute-done.14.refs_5_
  36.5 1.9 %shard_map.92 = (f32[2,16,1024]{2,1,0:T(8,128)S(1)}, bf16[2,16,1024]{2,1,0:T(8,128)(2,1)S(1)}, bf16[2,16,1024]{2,1,0:T(8,128)(2,1)S(1)}, bf16[2,16,1024]{2,1,0:T(8,128)(2,1)S(1)}) custom-call(bf16[32,640]{1,0:T(8,128)(2,1)S(1)} %get-tuple-element.43.refs_0_, bf16[32,640]{1,0:T(8,128)(2,1)S(1)} %collective-permute-done.11.refs_1_, ...), custom_call_target="tpu_custom_call" | custom-call | tf_op jit(solution)/shard_map/pallas_call | solution.py:62
  38.4 1.8 %collective-permute-start.15 = (bf16[2,16,1024]{2,1,0:T(8,128)(2,1)S(1)}, bf16[2,16,1024]{2,1,0:T(8,128)(2,1)S(1)}, u32[]{:S(2)}, u32[]{:S(2)}) collective-permute-start(bf16[2,16,1024]{2,1,0:T(8,128)(2,1)S(1)} %get-tuple-element.46), channel_id=1, source_target_pairs={{0,17},{1,16},{2,19},{3,18},{4,21},{5,20},{6,23},{7,22},{8,25},{9,... | collective-permute-start | bytes 196616 | tf_op jit(solution)/shard_map/ppermute | solution.py:40
  40.2 0.6 %collective-permute-start.16 = (bf16[2,16,1024]{2,1,0:T(8,128)(2,1)S(1)}, bf16[2,16,1024]{2,1,0:T(8,128)(2,1)S(1)}, u32[]{:S(2)}, u32[]{:S(2)}) collective-permute-start(bf16[2,16,1024]{2,1,0:T(8,128)(2,1)S(1)} %get-tuple-element.47), channel_id=1, source_target_pairs={{0,1},{1,0},{2,3},{3,2},{4,5},{5,4},{6,7},{7,6},{8,9},{9,8},{10,11... | collective-permute-start | bytes 196616 | tf_op jit(solution)/shard_map/ppermute | solution.py:40
  40.8 1.2 %collective-permute-start.17 = (bf16[2,16,1024]{2,1,0:T(8,128)(2,1)S(1)}, bf16[2,16,1024]{2,1,0:T(8,128)(2,1)S(1)}, u32[]{:S(2)}, u32[]{:S(2)}) collective-permute-start(bf16[2,16,1024]{2,1,0:T(8,128)(2,1)S(1)} %get-tuple-element.48), channel_id=1, source_target_pairs={{0,16},{1,17},{2,18},{3,19},{4,20},{5,21},{6,22},{7,23},{8,24},{9,... | collective-permute-start | bytes 196616 | tf_op jit(solution)/shard_map/ppermute | solution.py:40
  41.9 2.0 %collective-permute-done.15.refs_0_ = bf16[2,16,1024]{2,1,0:T(8,128)(2,1)S(1)} collective-permute-done((bf16[2,16,1024]{2,1,0:T(8,128)(2,1)S(1)}, bf16[2,16,1024]{2,1,0:T(8,128)(2,1)S(1)}, u32[]{:S(2)}, u32[]{:S(2)}) %collective-permute-start.15) | collective-permute-done | bytes 65568 | tf_op jit(solution)/shard_map/ppermute | solution.py:40
  44.0 0.4 collective-permute-done.16.refs_1_
  44.4 0.6 %collective-permute-done.17.refs_2_ = bf16[2,16,1024]{2,1,0:T(8,128)(2,1)S(1)} collective-permute-done((bf16[2,16,1024]{2,1,0:T(8,128)(2,1)S(1)}, bf16[2,16,1024]{2,1,0:T(8,128)(2,1)S(1)}, u32[]{:S(2)}, u32[]{:S(2)}) %collective-permute-start.17) | collective-permute-done | bytes 65568 | tf_op jit(solution)/shard_map/ppermute | solution.py:40
  45.1 2.5 %collective-permute-start.18 = (bf16[16,1024]{1,0:T(8,128)(2,1)S(1)}, bf16[16,1024]{1,0:T(8,128)(2,1)S(1)}, u32[]{:S(2)}, u32[]{:S(2)}) collective-permute-start(bf16[16,1024]{1,0:T(8,128)(2,1)S(1)} %get-tuple-element.51), channel_id=1, source_target_pairs={{0,6},{1,7},{2,4},{3,5},{4,2},{5,3},{6,0},{7,1},{8,14},{9,15},{10,... | collective-permute-start | bytes 98312 | tf_op jit(solution)/shard_map/ppermute | solution.py:40
  47.6 0.6 %collective-permute-start.19 = (bf16[16,1024]{1,0:T(8,128)(2,1)S(1)}, bf16[16,1024]{1,0:T(8,128)(2,1)S(1)}, u32[]{:S(2)}, u32[]{:S(2)}) collective-permute-start(bf16[16,1024]{1,0:T(8,128)(2,1)S(1)} %get-tuple-element.52), channel_id=1, source_target_pairs={{0,4},{1,5},{2,6},{3,7},{4,0},{5,1},{6,2},{7,3},{8,12},{9,13},{10,... | collective-permute-start | bytes 98312 | tf_op jit(solution)/shard_map/ppermute | solution.py:40
  48.2 1.3 %collective-permute-start.20 = (bf16[16,1024]{1,0:T(8,128)(2,1)S(1)}, bf16[16,1024]{1,0:T(8,128)(2,1)S(1)}, u32[]{:S(2)}, u32[]{:S(2)}) collective-permute-start(bf16[16,1024]{1,0:T(8,128)(2,1)S(1)} %get-tuple-element.53), channel_id=1, source_target_pairs={{0,2},{1,3},{2,0},{3,1},{4,6},{5,7},{6,4},{7,5},{8,10},{9,11},{10,... | collective-permute-start | bytes 98312 | tf_op jit(solution)/shard_map/ppermute | solution.py:40
  49.5 1.4 %collective-permute-done.18.refs_1_ = bf16[16,1024]{1,0:T(8,128)(2,1)S(1)} collective-permute-done((bf16[16,1024]{1,0:T(8,128)(2,1)S(1)}, bf16[16,1024]{1,0:T(8,128)(2,1)S(1)}, u32[]{:S(2)}, u32[]{:S(2)}) %collective-permute-start.18) | collective-permute-done | bytes 32800 | tf_op jit(solution)/shard_map/ppermute | solution.py:40
  50.9 1.5 %collective-permute-done.19.refs_2_ = bf16[16,1024]{1,0:T(8,128)(2,1)S(1)} collective-permute-done((bf16[16,1024]{1,0:T(8,128)(2,1)S(1)}, bf16[16,1024]{1,0:T(8,128)(2,1)S(1)}, u32[]{:S(2)}, u32[]{:S(2)}) %collective-permute-start.19) | collective-permute-done | bytes 32800 | tf_op jit(solution)/shard_map/ppermute | solution.py:40
  52.5 0.0 collective-permute-done.20.refs_3_
  52.5 0.6 %shard_map.94 = bf16[16,1024]{1,0:T(8,128)(2,1)} custom-call(f32[16,1024]{1,0:T(8,128)S(1)} %get-tuple-element.50.refs_0_, bf16[16,1024]{1,0:T(8,128)(2,1)S(1)} %collective-permute-done.18.refs_1_, bf16[16,1024]{1,0:T(8,128)(2,1)S(1)} %collective-permute-done.19.refs_2_, bf16[16,1024]{1,0:T(8,128)(2,1)S(1)} %collective-permute-done.20.refs_3_), custom_call_target="tpu_custom_call" | custom-call | tf_op jit(solution)/shard_map/pallas_call | solution.py:62
  (6 shorter events, 0.1 us)
Async XLA Ops:
  0.0 8.0 %copy-start.2 = (s32[4,16]{1,0:T(4,128)S(1)}, s32[4,16]{1,0:T(4,128)}, u32[]{:S(2)}) copy-start(s32[4,16]{1,0:T(4,128)} %ids_ref.1) | copy-start | bytes 772
  2.8 7.8 %collective-permute-start.3 = (bf16[16,2048]{1,0:T(8,128)(2,1)S(1)}, bf16[16,2048]{1,0:T(8,128)(2,1)S(1)}, u32[]{:S(2)}, u32[]{:S(2)}) collective-permute-start(bf16[16,2048]{1,0:T(8,128)(2,1)S(1)} %get-tuple-element.36), channel_id=1, source_target_pairs={{0,4},{1,5},{2,6},{3,7},{4,0},{5,1},{6,2},{7,3},{8,12},{9,13},{10,... | collective-permute-start | bytes 196616 | tf_op jit(solution)/shard_map/ppermute | solution.py:40
  8.1 3.5 %copy-start.1 = (bf16[1024,2048]{1,0:T(8,128)(2,1)S(1)}, bf16[1024,2048]{1,0:T(8,128)(2,1)}, u32[]{:S(2)}) copy-start(bf16[1024,2048]{1,0:T(8,128)(2,1)} %refs_4_.1) | copy-start | bytes 12582916
  11.5 9.9 %copy-start = (bf16[2048,1024]{1,0:T(8,128)(2,1)S(1)}, bf16[2048,1024]{1,0:T(8,128)(2,1)}, u32[]{:S(2)}) copy-start(bf16[2048,1024]{1,0:T(8,128)(2,1)} %refs_0_.3) | copy-start | bytes 12582916
  11.5 25.0 %collective-permute-start.14 = (bf16[1024,2048]{1,0:T(8,128)(2,1)S(1)}, bf16[1024,2048]{1,0:T(8,128)(2,1)S(1)}, u32[]{:S(2)}, u32[]{:S(2)}) collective-permute-start(bf16[1024,2048]{1,0:T(8,128)(2,1)S(1)} %copy-done.1), channel_id=1, source_target_pairs={{0,8},{1,9},{2,10},{3,11},{4,12},{5,13},{6,14},{7,15},{8,0},{9,1},... | collective-permute-start | bytes 12582920 | tf_op jit(solution)/shard_map/ppermute | solution.py:40
  11.5 7.2 %collective-permute-start.4 = (bf16[32,2048]{1,0:T(8,128)(2,1)S(1)}, bf16[32,2048]{1,0:T(8,128)(2,1)S(1)}, u32[]{:S(2)}, u32[]{:S(2)}) collective-permute-start(bf16[32,2048]{1,0:T(8,128)(2,1)S(1)} %pad_maximum_fusion.refs_0_._), channel_id=1, source_target_pairs={{0,3},{1,2},{2,1},{3,0},{4,7},{5,6},{6,5},{7,4},{8,11},{9,10},{10,... | collective-permute-start | bytes 393224 | tf_op jit(solution)/shard_map/ppermute | solution.py:40
  14.0 7.2 %collective-permute-start.5 = (bf16[32,2048]{1,0:T(8,128)(2,1)S(1)}, bf16[32,2048]{1,0:T(8,128)(2,1)S(1)}, u32[]{:S(2)}, u32[]{:S(2)}) collective-permute-start(bf16[32,2048]{1,0:T(8,128)(2,1)S(1)} %pad_maximum_fusion.refs_0_._), channel_id=1, source_target_pairs={{0,2},{1,3},{2,0},{3,1},{4,6},{5,7},{6,4},{7,5},{8,10},{9,11},{10,... | collective-permute-start | bytes 393224 | tf_op jit(solution)/shard_map/ppermute | solution.py:40
  14.5 6.7 %collective-permute-start.6 = (bf16[32,2048]{1,0:T(8,128)(2,1)S(1)}, bf16[32,2048]{1,0:T(8,128)(2,1)S(1)}, u32[]{:S(2)}, u32[]{:S(2)}) collective-permute-start(bf16[32,2048]{1,0:T(8,128)(2,1)S(1)} %pad_maximum_fusion.refs_0_._), channel_id=1, source_target_pairs={{0,1},{1,0},{2,3},{3,2},{4,5},{5,4},{6,7},{7,6},{8,9},{9,8},{10,11... | collective-permute-start | bytes 393224 | tf_op jit(solution)/shard_map/ppermute | solution.py:40
  18.5 11.6 %collective-permute-start.10 = (bf16[512,512]{1,0:T(8,128)(2,1)S(1)}, bf16[512,512]{1,0:T(8,128)(2,1)S(1)}, u32[]{:S(2)}, u32[]{:S(2)}) collective-permute-start(bf16[512,512]{1,0:T(8,128)(2,1)S(1)} %get-tuple-element.42), channel_id=1, source_target_pairs={{0,8},{1,9},{2,10},{3,11},{4,12},{5,13},{6,14},{7,15},{8,0},{9,1},... | collective-permute-start | bytes 1572872 | tf_op jit(solution)/shard_map/ppermute | solution.py:40
  18.7 11.4 %collective-permute-start.9 = (bf16[512,512]{1,0:T(8,128)(2,1)S(1)}, bf16[512,512]{1,0:T(8,128)(2,1)S(1)}, u32[]{:S(2)}, u32[]{:S(2)}) collective-permute-start(bf16[512,512]{1,0:T(8,128)(2,1)S(1)} %get-tuple-element.41), channel_id=1, source_target_pairs={{0,8},{1,9},{2,10},{3,11},{4,12},{5,13},{6,14},{7,15},{8,0},{9,1},... | collective-permute-start | bytes 1572872 | tf_op jit(solution)/shard_map/ppermute | solution.py:40
  22.7 1.5 %collective-permute-start.7 = (bf16[64,1536]{1,0:T(8,128)(2,1)S(1)}, bf16[64,1536]{1,0:T(8,128)(2,1)S(1)}, u32[]{:S(2)}, u32[]{:S(2)}) collective-permute-start(bf16[64,1536]{1,0:T(8,128)(2,1)S(1)} %shard_map.87), channel_id=1, source_target_pairs={{0,8},{1,9},{2,10},{3,11},{4,12},{5,13},{6,14},{7,15},{8,0},{9,1},... | collective-permute-start | bytes 589832 | tf_op jit(solution)/shard_map/ppermute | solution.py:40
  24.3 5.8 %collective-permute-start.8 = (bf16[128,512]{1,0:T(8,128)(2,1)S(1)}, bf16[128,512]{1,0:T(8,128)(2,1)S(1)}, u32[]{:S(2)}, u32[]{:S(2)}) collective-permute-start(bf16[128,512]{1,0:T(8,128)(2,1)S(1)} %get-tuple-element.40), channel_id=1, source_target_pairs={{0,16},{1,17},{2,18},{3,19},{4,20},{5,21},{6,22},{7,23},{8,24},{9,... | collective-permute-start | bytes 393224 | tf_op jit(solution)/shard_map/ppermute | solution.py:40
  31.3 1.9 %collective-permute-start.11 = (bf16[32,640]{1,0:T(8,128)(2,1)S(1)}, bf16[32,640]{1,0:T(8,128)(2,1)S(1)}, u32[]{:S(2)}, u32[]{:S(2)}) collective-permute-start(bf16[32,640]{1,0:T(8,128)(2,1)S(1)} %get-tuple-element.44), channel_id=1, source_target_pairs={{0,8},{1,9},{2,10},{3,11},{4,12},{5,13},{6,14},{7,15},{8,0},{9,1},... | collective-permute-start | bytes 122888 | tf_op jit(solution)/shard_map/ppermute | solution.py:40
  31.4 4.1 %collective-permute-start.12 = (bf16[32,640]{1,0:T(8,128)(2,1)S(1)}, bf16[32,640]{1,0:T(8,128)(2,1)S(1)}, u32[]{:S(2)}, u32[]{:S(2)}) collective-permute-start(bf16[32,640]{1,0:T(8,128)(2,1)S(1)} %get-tuple-element.43.refs_0_), channel_id=1, source_target_pairs={{0,16},{1,17},{2,18},{3,19},{4,20},{5,21},{6,22},{7,23},{8,24},{9,... | collective-permute-start | bytes 122888 | tf_op jit(solution)/shard_map/ppermute | solution.py:40
  33.0 3.5 %collective-permute-start.13 = (bf16[32,640]{1,0:T(8,128)(2,1)S(1)}, bf16[32,640]{1,0:T(8,128)(2,1)S(1)}, u32[]{:S(2)}, u32[]{:S(2)}) collective-permute-start(bf16[32,640]{1,0:T(8,128)(2,1)S(1)} %get-tuple-element.44), channel_id=1, source_target_pairs={{0,24},{1,25},{2,26},{3,27},{4,28},{5,29},{6,30},{7,31},{8,16},{9,... | collective-permute-start | bytes 122888 | tf_op jit(solution)/shard_map/ppermute | solution.py:40
  38.4 5.6 %collective-permute-start.15 = (bf16[2,16,1024]{2,1,0:T(8,128)(2,1)S(1)}, bf16[2,16,1024]{2,1,0:T(8,128)(2,1)S(1)}, u32[]{:S(2)}, u32[]{:S(2)}) collective-permute-start(bf16[2,16,1024]{2,1,0:T(8,128)(2,1)S(1)} %get-tuple-element.46), channel_id=1, source_target_pairs={{0,17},{1,16},{2,19},{3,18},{4,21},{5,20},{6,23},{7,22},{8,25},{9,... | collective-permute-start | bytes 196616 | tf_op jit(solution)/shard_map/ppermute | solution.py:40
  40.2 4.3 %collective-permute-start.16 = (bf16[2,16,1024]{2,1,0:T(8,128)(2,1)S(1)}, bf16[2,16,1024]{2,1,0:T(8,128)(2,1)S(1)}, u32[]{:S(2)}, u32[]{:S(2)}) collective-permute-start(bf16[2,16,1024]{2,1,0:T(8,128)(2,1)S(1)} %get-tuple-element.47), channel_id=1, source_target_pairs={{0,1},{1,0},{2,3},{3,2},{4,5},{5,4},{6,7},{7,6},{8,9},{9,8},{10,11... | collective-permute-start | bytes 196616 | tf_op jit(solution)/shard_map/ppermute | solution.py:40
  40.8 4.3 %collective-permute-start.17 = (bf16[2,16,1024]{2,1,0:T(8,128)(2,1)S(1)}, bf16[2,16,1024]{2,1,0:T(8,128)(2,1)S(1)}, u32[]{:S(2)}, u32[]{:S(2)}) collective-permute-start(bf16[2,16,1024]{2,1,0:T(8,128)(2,1)S(1)} %get-tuple-element.48), channel_id=1, source_target_pairs={{0,16},{1,17},{2,18},{3,19},{4,20},{5,21},{6,22},{7,23},{8,24},{9,... | collective-permute-start | bytes 196616 | tf_op jit(solution)/shard_map/ppermute | solution.py:40
  45.1 5.8 %collective-permute-start.18 = (bf16[16,1024]{1,0:T(8,128)(2,1)S(1)}, bf16[16,1024]{1,0:T(8,128)(2,1)S(1)}, u32[]{:S(2)}, u32[]{:S(2)}) collective-permute-start(bf16[16,1024]{1,0:T(8,128)(2,1)S(1)} %get-tuple-element.51), channel_id=1, source_target_pairs={{0,6},{1,7},{2,4},{3,5},{4,2},{5,3},{6,0},{7,1},{8,14},{9,15},{10,... | collective-permute-start | bytes 98312 | tf_op jit(solution)/shard_map/ppermute | solution.py:40
  47.6 4.8 %collective-permute-start.19 = (bf16[16,1024]{1,0:T(8,128)(2,1)S(1)}, bf16[16,1024]{1,0:T(8,128)(2,1)S(1)}, u32[]{:S(2)}, u32[]{:S(2)}) collective-permute-start(bf16[16,1024]{1,0:T(8,128)(2,1)S(1)} %get-tuple-element.52), channel_id=1, source_target_pairs={{0,4},{1,5},{2,6},{3,7},{4,0},{5,1},{6,2},{7,3},{8,12},{9,13},{10,... | collective-permute-start | bytes 98312 | tf_op jit(solution)/shard_map/ppermute | solution.py:40
  48.2 4.3 %collective-permute-start.20 = (bf16[16,1024]{1,0:T(8,128)(2,1)S(1)}, bf16[16,1024]{1,0:T(8,128)(2,1)S(1)}, u32[]{:S(2)}, u32[]{:S(2)}) collective-permute-start(bf16[16,1024]{1,0:T(8,128)(2,1)S(1)} %get-tuple-element.53), channel_id=1, source_target_pairs={{0,2},{1,3},{2,0},{3,1},{4,6},{5,7},{6,4},{7,5},{8,10},{9,11},{10,... | collective-permute-start | bytes 98312 | tf_op jit(solution)/shard_map/ppermute | solution.py:40

commit v4 on v3

--- a/solution.py
+++ b/solution.py
@@ -504,7 +504,7 @@
     def kernel(*refs):
         parts, refs = refs[: plan.seq], refs[plan.seq :]
         (own_ref, swapped_ref), refs = refs[:2], refs[2:]
-        outs, (joined, held) = refs[: len(keys)], refs[len(keys) :]
+        outs, (joined,) = refs[: len(keys)], refs[len(keys) :]
         seq_index = lax.axis_index("seq")
         chip, core = seq_index // CORES, lax.rem(seq_index, CORES)
         part_index = lax.rem(lax.axis_index("head"), plan.parts)
@@ -526,16 +526,18 @@
                 scales = [jnp.exp(one - top) for one in logs]
                 mixed = sum(f * source[:, lanes].astype(F32) for f, source in zip(scales, sources))
                 mixed = (mixed / sum(scales)).astype(BF16)
-                joined[:, pl.ds(pl.multiple_of(first + head * HD, HD), HD)] = mixed
+                window = pl.ds(pl.multiple_of(first + head * HD, HD), HD)
+                for owner in range(plan.chips):
+                    rows_of = mixed[owner * share : (owner + 1) * share]
+                    joined[aligned(owner ^ chip, share), window] = rows_of
         left = joined[...]
         for dx in list(range(plan.parts))[::-1]:
             lanes = aligned(part_index ^ dx, columns)
             for weight, block in ((own_ref, core), (swapped_ref, 1 - core)):
                 product = jnp.dot(left, weight[:, lanes], preferred_element_type=F32)
-                held[...] = product
                 for dy in range(plan.chips):
                     out = outs[keys.index((dy, dx))]
-                    out[block] = held[aligned(chip ^ dy, share), :].astype(out.dtype)
+                    out[block] = product[dy * share : (dy + 1) * share].astype(out.dtype)
 
     shape = (CORES, share, columns)
     outs = [jax.ShapeDtypeStruct(shape, BF16 if any(key) else F32) for key in keys]
@@ -544,7 +546,7 @@
         outs,
         [VMEM_SPEC] * (plan.seq + 2),
         [VMEM_SPEC] * len(keys),
-        [pltpu.VMEM((rows, plan.width), BF16), pltpu.VMEM((rows, columns), F32)],
+        [pltpu.VMEM((rows, plan.width), BF16)],
         24,
         *attended,
         own,

time: 53.3 us -> 53.2 us (level)
  no operation moved by 1% of the time
where the time goes in v4:
time: 53.2 us; the launch traced here: 53 us
  starting transfers between devices  19.5 us (37%)
  Pallas kernels  16.2 us (30%)
  waiting for transfers between devices  14.6 us (27%)
  local copies, waits for them, and re-layouts  1.55 us (3%)
  between operations  0.83 us (2%)
    ppermute x18, starting transfers between devices, send(): return lax.ppermute(value, ('seq', 'head'), pairs)  19.5 us
    pallas_call x13, Pallas kernels, call(): pl.pallas_call(kernel, out_shape=out_shape, in_specs=in_specs, out_specs=...  16.2 us
    ppermute x18, waiting for transfers between devices, send(): return lax.ppermute(value, ('seq', 'head'), pairs)  14.6 us
  transfers between devices with their start and end apart: 18, of which 11 were waited for; matrix products, arithmetic and copies ran while one was open for 1% of the time, Pallas kernels for 21%

profile of v4, /device:TPU:0, one launch (start us, length us, event | category | flops | bytes accessed | tf_op | source)
XLA Modules:
  0.0 53.0 jit_solution(7085507942119844889)
XLA Ops:
  0.0 0.0 copy-start.2
  0.0 2.7 %shard_map.82 = (bf16[16,2048]{1,0:T(8,128)(2,1)S(1)}, bf16[64,128]{1,0:T(8,128)(2,1)S(1)}, f32[8,128]{1,0:T(8,128)S(1)}) custom-call(s32[4,16]{1,0:T(4,128)} %ids_ref.1, bf16[1024,2048]{1,0:T(8,128)(2,1)} %embed_ref.1), custom_call_target="tpu_custom_call" | custom-call | tf_op jit(solution)/shard_map/pallas_call | solution.py:62
  2.8 4.1 %collective-permute-start.3 = (bf16[16,2048]{1,0:T(8,128)(2,1)S(1)}, bf16[16,2048]{1,0:T(8,128)(2,1)S(1)}, u32[]{:S(2)}, u32[]{:S(2)}) collective-permute-start(bf16[16,2048]{1,0:T(8,128)(2,1)S(1)} %get-tuple-element.36), channel_id=1, source_target_pairs={{0,4},{1,5},{2,6},{3,7},{4,0},{5,1},{6,2},{7,3},{8,12},{9,13},{10,... | collective-permute-start | bytes 196616 | tf_op jit(solution)/shard_map/ppermute | solution.py:40
  6.9 0.5 slice.3
  8.0 0.0 copy-done.2
  8.1 0.0 copy-start.1
  8.1 2.4 %shard_map.83.refs_1_ = bf16[2048,1024]{1,0:T(8,128)(2,1)S(1)} custom-call(bf16[64,2048]{1,0:T(8,128)(2,1)S(1)} %get-tuple-element.59._.rest_ref, bf16[2048,1024]{1,0:T(8,128)(2,1)} %source_ref.2), custom_call_target="tpu_custom_call" | custom-call | tf_op jit(solution)/shard_map/pallas_call | solution.py:62
  10.5 0.0 collective-permute-done.3
  10.5 1.0 %copy-done.1 = bf16[1024,2048]{1,0:T(8,128)(2,1)S(1)} copy-done((bf16[1024,2048]{1,0:T(8,128)(2,1)S(1)}, bf16[1024,2048]{1,0:T(8,128)(2,1)}, u32[]{:S(2)}) %copy-start.1) | copy-done | bytes 4194328
  11.5 0.0 copy-start
  11.5 0.0 collective-permute-start.14
  11.5 2.5 %collective-permute-start.4 = (bf16[32,2048]{1,0:T(8,128)(2,1)S(1)}, bf16[32,2048]{1,0:T(8,128)(2,1)S(1)}, u32[]{:S(2)}, u32[]{:S(2)}) collective-permute-start(bf16[32,2048]{1,0:T(8,128)(2,1)S(1)} %pad_maximum_fusion.refs_0_._), channel_id=1, source_target_pairs={{0,3},{1,2},{2,1},{3,0},{4,7},{5,6},{6,5},{7,4},{8,11},{9,10},{10,... | collective-permute-start | bytes 393224 | tf_op jit(solution)/shard_map/ppermute | solution.py:40
  14.0 0.4 collective-permute-start.5
  14.5 0.5 %collective-permute-start.6 = (bf16[32,2048]{1,0:T(8,128)(2,1)S(1)}, bf16[32,2048]{1,0:T(8,128)(2,1)S(1)}, u32[]{:S(2)}, u32[]{:S(2)}) collective-permute-start(bf16[32,2048]{1,0:T(8,128)(2,1)S(1)} %pad_maximum_fusion.refs_0_._), channel_id=1, source_target_pairs={{0,1},{1,0},{2,3},{3,2},{4,5},{5,4},{6,7},{7,6},{8,9},{9,8},{10,11... | collective-permute-start | bytes 393224 | tf_op jit(solution)/shard_map/ppermute | solution.py:40
  15.0 2.2 %shard_map.85.refs_2_ = bf16[2048,1024]{1,0:T(8,128)(2,1)S(1)} custom-call(bf16[32,2048]{1,0:T(8,128)(2,1)S(1)} %pad_maximum_fusion.refs_0_._, bf16[2048,1024]{1,0:T(8,128)(2,1)} %source_ref.3), custom_call_target="tpu_custom_call" | custom-call | tf_op jit(solution)/shard_map/pallas_call | solution.py:62
  17.2 1.2 %shard_map.90 = (bf16[512,512]{1,0:T(8,128)(2,1)S(1)}, bf16[512,512]{1,0:T(8,128)(2,1)S(1)}) custom-call(bf16[32,2048]{1,0:T(8,128)(2,1)S(1)} %pad_maximum_fusion.refs_0_._, bf16[512,1024]{1,0:T(8,128)(2,1)} %keys_ref.3, bf16[512,1024]{1,0:T(8,128)(2,1)} %values_ref.3), custom_call_target="tpu_custom_call" | custom-call | tf_op jit(solution)/shard_map/pallas_call | solution.py:62
  18.5 0.1 collective-permute-start.10
  18.6 0.2 collective-permute-done.4.refs_1_
  18.7 0.3 collective-permute-start.9
  19.1 2.2 %collective-permute-done.5.refs_2_ = bf16[32,2048]{1,0:T(8,128)(2,1)S(1)} collective-permute-done((bf16[32,2048]{1,0:T(8,128)(2,1)S(1)}, bf16[32,2048]{1,0:T(8,128)(2,1)S(1)}, u32[]{:S(2)}, u32[]{:S(2)}) %collective-permute-start.5) | collective-permute-done | bytes 131104 | tf_op jit(solution)/shard_map/ppermute | solution.py:40
  21.2 0.0 collective-permute-done.6.refs_3_
  21.2 0.2 shard_map.84.rows_ref
  21.5 0.0 copy-done
  21.5 1.2 %shard_map.87 = bf16[64,1536]{1,0:T(8,128)(2,1)S(1)} custom-call(bf16[64,2048]{1,0:T(8,128)(2,1)S(1)} %shard_map.84.rows_ref, bf16[2048,1024]{1,0:T(8,128)(2,1)S(1)} %copy-done, bf16[2048,1024]{1,0:T(8,128)(2,1)S(1)} %shard_map.83.refs_1_, bf16[2048,1024]{1,0:T(8,128)(2,1)S(1)} %shard_map.85.refs_2_), custom_call_target="tpu_custom_call" | custom-call | tf_op jit(solution)/shard_map/pallas_call | solution.py:62
  22.7 0.1 collective-permute-start.7
  22.8 1.2 %shard_map.86.own_ref = f32[64,1536]{1,0:T(8,128)S(1)} custom-call(bf16[64,2048]{1,0:T(8,128)(2,1)S(1)} %shard_map.84.rows_ref, bf16[2048,1024]{1,0:T(8,128)(2,1)S(1)} %copy-done, bf16[2048,1024]{1,0:T(8,128)(2,1)S(1)} %shard_map.83.refs_1_, bf16[2048,1024]{1,0:T(8,128)(2,1)S(1)} %shard_map.85.refs_2_), custom_call_target="tpu_custom_call" | custom-call | tf_op jit(solution)/shard_map/pallas_call | solution.py:62
  24.1 0.2 collective-permute-done.7.received_ref
  24.2 0.1 shard_map.88
  24.3 1.6 %collective-permute-start.8 = (bf16[128,512]{1,0:T(8,128)(2,1)S(1)}, bf16[128,512]{1,0:T(8,128)(2,1)S(1)}, u32[]{:S(2)}, u32[]{:S(2)}) collective-permute-start(bf16[128,512]{1,0:T(8,128)(2,1)S(1)} %get-tuple-element.40), channel_id=1, source_target_pairs={{0,16},{1,17},{2,18},{3,19},{4,20},{5,21},{6,22},{7,23},{8,24},{9,... | collective-permute-start | bytes 393224 | tf_op jit(solution)/shard_map/ppermute | solution.py:40
  25.9 0.1 fusion.2
  26.0 0.1 pad_maximum_fusion.1
  26.1 1.2 %shard_map.89.refs_2_ = bf16[1024,512]{1,0:T(8,128)(2,1)S(1)} custom-call(f32[128,512]{1,0:T(8,128)S(1)} %get-tuple-element.39._.refs_0_, bf16[512,1024]{1,0:T(8,128)(2,1)} %keys_ref.3, bf16[512,1024]{1,0:T(8,128)(2,1)} %values_ref.3), custom_call_target="tpu_custom_call" | custom-call | tf_op jit(solution)/shard_map/pallas_call | solution.py:62
  27.3 2.8 %collective-permute-done.8.refs_1_ = bf16[128,512]{1,0:T(8,128)(2,1)S(1)} collective-permute-done((bf16[128,512]{1,0:T(8,128)(2,1)S(1)}, bf16[128,512]{1,0:T(8,128)(2,1)S(1)}, u32[]{:S(2)}, u32[]{:S(2)}) %collective-permute-start.8) | collective-permute-done | bytes 131104 | tf_op jit(solution)/shard_map/ppermute | solution.py:40
  30.1 0.0 collective-permute-done.10.refs_4_
  30.1 0.0 collective-permute-done.9.refs_3_
  30.1 1.2 %shard_map.91 = (bf16[32,640]{1,0:T(8,128)(2,1)S(1)}, bf16[32,640]{1,0:T(8,128)(2,1)S(1)}) custom-call(f32[128,512]{1,0:T(8,128)S(1)} %get-tuple-element.39._.refs_0_, bf16[128,512]{1,0:T(8,128)(2,1)S(1)} %collective-permute-done.8.refs_1_, bf16[1024,512]{1,0:T(8,128)(2,1)S(1)} %shard_map.89.refs_2_, bf16[512,512]{1,0:T(8,128)(2,1)S(1)} %collective-permute-done.9.refs_3_, ...), custom_call_target="tpu_custom_call" | custom-call | tf_op jit(solution)/shard_map/pallas_call | solution.py:62
  31.3 0.1 collective-permute-start.11
  31.4 1.6 %collective-permute-start.12 = (bf16[32,640]{1,0:T(8,128)(2,1)S(1)}, bf16[32,640]{1,0:T(8,128)(2,1)S(1)}, u32[]{:S(2)}, u32[]{:S(2)}) collective-permute-start(bf16[32,640]{1,0:T(8,128)(2,1)S(1)} %get-tuple-element.43.refs_0_), channel_id=1, source_target_pairs={{0,16},{1,17},{2,18},{3,19},{4,20},{5,21},{6,22},{7,23},{8,24},{9,... | collective-permute-start | bytes 122888 | tf_op jit(solution)/shard_map/ppermute | solution.py:40
  33.0 0.3 collective-permute-start.13
  33.3 0.0 collective-permute-done.11.refs_1_
  33.3 2.2 %collective-permute-done.12.refs_2_ = bf16[32,640]{1,0:T(8,128)(2,1)S(1)} collective-permute-done((bf16[32,640]{1,0:T(8,128)(2,1)S(1)}, bf16[32,640]{1,0:T(8,128)(2,1)S(1)}, u32[]{:S(2)}, u32[]{:S(2)}) %collective-permute-start.12) | collective-permute-done | bytes 40992 | tf_op jit(solution)/shard_map/ppermute | solution.py:40
  35.5 1.0 %collective-permute-done.13.refs_3_ = bf16[32,640]{1,0:T(8,128)(2,1)S(1)} collective-permute-done((bf16[32,640]{1,0:T(8,128)(2,1)S(1)}, bf16[32,640]{1,0:T(8,128)(2,1)S(1)}, u32[]{:S(2)}, u32[]{:S(2)}) %collective-permute-start.13) | collective-permute-done | bytes 40992 | tf_op jit(solution)/shard_map/ppermute | solution.py:40
  36.5 0.0 collective-permute-done.14.refs_5_
  36.5 1.8 %shard_map.92 = (f32[2,16,1024]{2,1,0:T(8,128)S(1)}, bf16[2,16,1024]{2,1,0:T(8,128)(2,1)S(1)}, bf16[2,16,1024]{2,1,0:T(8,128)(2,1)S(1)}, bf16[2,16,1024]{2,1,0:T(8,128)(2,1)S(1)}) custom-call(bf16[32,640]{1,0:T(8,128)(2,1)S(1)} %get-tuple-element.43.refs_0_, bf16[32,640]{1,0:T(8,128)(2,1)S(1)} %collective-permute-done.11.refs_1_, ...), custom_call_target="tpu_custom_call" | custom-call | tf_op jit(solution)/shard_map/pallas_call | solution.py:62
  38.4 1.7 %collective-permute-start.15 = (bf16[2,16,1024]{2,1,0:T(8,128)(2,1)S(1)}, bf16[2,16,1024]{2,1,0:T(8,128)(2,1)S(1)}, u32[]{:S(2)}, u32[]{:S(2)}) collective-permute-start(bf16[2,16,1024]{2,1,0:T(8,128)(2,1)S(1)} %get-tuple-element.46), channel_id=1, source_target_pairs={{0,17},{1,16},{2,19},{3,18},{4,21},{5,20},{6,23},{7,22},{8,25},{9,... | collective-permute-start | bytes 196616 | tf_op jit(solution)/shard_map/ppermute | solution.py:40
  40.1 0.6 %collective-permute-start.16 = (bf16[2,16,1024]{2,1,0:T(8,128)(2,1)S(1)}, bf16[2,16,1024]{2,1,0:T(8,128)(2,1)S(1)}, u32[]{:S(2)}, u32[]{:S(2)}) collective-permute-start(bf16[2,16,1024]{2,1,0:T(8,128)(2,1)S(1)} %get-tuple-element.47), channel_id=1, source_target_pairs={{0,1},{1,0},{2,3},{3,2},{4,5},{5,4},{6,7},{7,6},{8,9},{9,8},{10,11... | collective-permute-start | bytes 196616 | tf_op jit(solution)/shard_map/ppermute | solution.py:40
  40.7 1.2 %collective-permute-start.17 = (bf16[2,16,1024]{2,1,0:T(8,128)(2,1)S(1)}, bf16[2,16,1024]{2,1,0:T(8,128)(2,1)S(1)}, u32[]{:S(2)}, u32[]{:S(2)}) collective-permute-start(bf16[2,16,1024]{2,1,0:T(8,128)(2,1)S(1)} %get-tuple-element.48), channel_id=1, source_target_pairs={{0,16},{1,17},{2,18},{3,19},{4,20},{5,21},{6,22},{7,23},{8,24},{9,... | collective-permute-start | bytes 196616 | tf_op jit(solution)/shard_map/ppermute | solution.py:40
  41.9 2.0 %collective-permute-done.15.refs_0_ = bf16[2,16,1024]{2,1,0:T(8,128)(2,1)S(1)} collective-permute-done((bf16[2,16,1024]{2,1,0:T(8,128)(2,1)S(1)}, bf16[2,16,1024]{2,1,0:T(8,128)(2,1)S(1)}, u32[]{:S(2)}, u32[]{:S(2)}) %collective-permute-start.15) | collective-permute-done | bytes 65568 | tf_op jit(solution)/shard_map/ppermute | solution.py:40
  43.9 0.4 collective-permute-done.16.refs_1_
  44.3 0.6 %collective-permute-done.17.refs_2_ = bf16[2,16,1024]{2,1,0:T(8,128)(2,1)S(1)} collective-permute-done((bf16[2,16,1024]{2,1,0:T(8,128)(2,1)S(1)}, bf16[2,16,1024]{2,1,0:T(8,128)(2,1)S(1)}, u32[]{:S(2)}, u32[]{:S(2)}) %collective-permute-start.17) | collective-permute-done | bytes 65568 | tf_op jit(solution)/shard_map/ppermute | solution.py:40
  45.0 2.5 %collective-permute-start.18 = (bf16[16,1024]{1,0:T(8,128)(2,1)S(1)}, bf16[16,1024]{1,0:T(8,128)(2,1)S(1)}, u32[]{:S(2)}, u32[]{:S(2)}) collective-permute-start(bf16[16,1024]{1,0:T(8,128)(2,1)S(1)} %get-tuple-element.51), channel_id=1, source_target_pairs={{0,6},{1,7},{2,4},{3,5},{4,2},{5,3},{6,0},{7,1},{8,14},{9,15},{10,... | collective-permute-start | bytes 98312 | tf_op jit(solution)/shard_map/ppermute | solution.py:40
  47.5 0.6 %collective-permute-start.19 = (bf16[16,1024]{1,0:T(8,128)(2,1)S(1)}, bf16[16,1024]{1,0:T(8,128)(2,1)S(1)}, u32[]{:S(2)}, u32[]{:S(2)}) collective-permute-start(bf16[16,1024]{1,0:T(8,128)(2,1)S(1)} %get-tuple-element.52), channel_id=1, source_target_pairs={{0,4},{1,5},{2,6},{3,7},{4,0},{5,1},{6,2},{7,3},{8,12},{9,13},{10,... | collective-permute-start | bytes 98312 | tf_op jit(solution)/shard_map/ppermute | solution.py:40
  48.1 1.3 %collective-permute-start.20 = (bf16[16,1024]{1,0:T(8,128)(2,1)S(1)}, bf16[16,1024]{1,0:T(8,128)(2,1)S(1)}, u32[]{:S(2)}, u32[]{:S(2)}) collective-permute-start(bf16[16,1024]{1,0:T(8,128)(2,1)S(1)} %get-tuple-element.53), channel_id=1, source_target_pairs={{0,2},{1,3},{2,0},{3,1},{4,6},{5,7},{6,4},{7,5},{8,10},{9,11},{10,... | collective-permute-start | bytes 98312 | tf_op jit(solution)/shard_map/ppermute | solution.py:40
  49.5 1.4 %collective-permute-done.18.refs_1_ = bf16[16,1024]{1,0:T(8,128)(2,1)S(1)} collective-permute-done((bf16[16,1024]{1,0:T(8,128)(2,1)S(1)}, bf16[16,1024]{1,0:T(8,128)(2,1)S(1)}, u32[]{:S(2)}, u32[]{:S(2)}) %collective-permute-start.18) | collective-permute-done | bytes 32800 | tf_op jit(solution)/shard_map/ppermute | solution.py:40
  50.8 1.5 %collective-permute-done.19.refs_2_ = bf16[16,1024]{1,0:T(8,128)(2,1)S(1)} collective-permute-done((bf16[16,1024]{1,0:T(8,128)(2,1)S(1)}, bf16[16,1024]{1,0:T(8,128)(2,1)S(1)}, u32[]{:S(2)}, u32[]{:S(2)}) %collective-permute-start.19) | collective-permute-done | bytes 32800 | tf_op jit(solution)/shard_map/ppermute | solution.py:40
  52.4 0.0 collective-permute-done.20.refs_3_
  52.4 0.6 %shard_map.94 = bf16[16,1024]{1,0:T(8,128)(2,1)} custom-call(f32[16,1024]{1,0:T(8,128)S(1)} %get-tuple-element.50.refs_0_, bf16[16,1024]{1,0:T(8,128)(2,1)S(1)} %collective-permute-done.18.refs_1_, bf16[16,1024]{1,0:T(8,128)(2,1)S(1)} %collective-permute-done.19.refs_2_, bf16[16,1024]{1,0:T(8,128)(2,1)S(1)} %collective-permute-done.20.refs_3_), custom_call_target="tpu_custom_call" | custom-call | tf_op jit(solution)/shard_map/pallas_call | solution.py:62
  (6 shorter events, 0.1 us)
Async XLA Ops:
  0.0 8.0 %copy-start.2 = (s32[4,16]{1,0:T(4,128)S(1)}, s32[4,16]{1,0:T(4,128)}, u32[]{:S(2)}) copy-start(s32[4,16]{1,0:T(4,128)} %ids_ref.1) | copy-start | bytes 772
  2.8 7.8 %collective-permute-start.3 = (bf16[16,2048]{1,0:T(8,128)(2,1)S(1)}, bf16[16,2048]{1,0:T(8,128)(2,1)S(1)}, u32[]{:S(2)}, u32[]{:S(2)}) collective-permute-start(bf16[16,2048]{1,0:T(8,128)(2,1)S(1)} %get-tuple-element.36), channel_id=1, source_target_pairs={{0,4},{1,5},{2,6},{3,7},{4,0},{5,1},{6,2},{7,3},{8,12},{9,13},{10,... | collective-permute-start | bytes 196616 | tf_op jit(solution)/shard_map/ppermute | solution.py:40
  8.1 3.5 %copy-start.1 = (bf16[1024,2048]{1,0:T(8,128)(2,1)S(1)}, bf16[1024,2048]{1,0:T(8,128)(2,1)}, u32[]{:S(2)}) copy-start(bf16[1024,2048]{1,0:T(8,128)(2,1)} %refs_4_.1) | copy-start | bytes 12582916
  11.5 9.9 %copy-start = (bf16[2048,1024]{1,0:T(8,128)(2,1)S(1)}, bf16[2048,1024]{1,0:T(8,128)(2,1)}, u32[]{:S(2)}) copy-start(bf16[2048,1024]{1,0:T(8,128)(2,1)} %refs_0_.3) | copy-start | bytes 12582916
  11.5 25.0 %collective-permute-start.14 = (bf16[1024,2048]{1,0:T(8,128)(2,1)S(1)}, bf16[1024,2048]{1,0:T(8,128)(2,1)S(1)}, u32[]{:S(2)}, u32[]{:S(2)}) collective-permute-start(bf16[1024,2048]{1,0:T(8,128)(2,1)S(1)} %copy-done.1), channel_id=1, source_target_pairs={{0,8},{1,9},{2,10},{3,11},{4,12},{5,13},{6,14},{7,15},{8,0},{9,1},... | collective-permute-start | bytes 12582920 | tf_op jit(solution)/shard_map/ppermute | solution.py:40
  11.5 7.2 %collective-permute-start.4 = (bf16[32,2048]{1,0:T(8,128)(2,1)S(1)}, bf16[32,2048]{1,0:T(8,128)(2,1)S(1)}, u32[]{:S(2)}, u32[]{:S(2)}) collective-permute-start(bf16[32,2048]{1,0:T(8,128)(2,1)S(1)} %pad_maximum_fusion.refs_0_._), channel_id=1, source_target_pairs={{0,3},{1,2},{2,1},{3,0},{4,7},{5,6},{6,5},{7,4},{8,11},{9,10},{10,... | collective-permute-start | bytes 393224 | tf_op jit(solution)/shard_map/ppermute | solution.py:40
  14.0 7.2 %collective-permute-start.5 = (bf16[32,2048]{1,0:T(8,128)(2,1)S(1)}, bf16[32,2048]{1,0:T(8,128)(2,1)S(1)}, u32[]{:S(2)}, u32[]{:S(2)}) collective-permute-start(bf16[32,2048]{1,0:T(8,128)(2,1)S(1)} %pad_maximum_fusion.refs_0_._), channel_id=1, source_target_pairs={{0,2},{1,3},{2,0},{3,1},{4,6},{5,7},{6,4},{7,5},{8,10},{9,11},{10,... | collective-permute-start | bytes 393224 | tf_op jit(solution)/shard_map/ppermute | solution.py:40
  14.5 6.7 %collective-permute-start.6 = (bf16[32,2048]{1,0:T(8,128)(2,1)S(1)}, bf16[32,2048]{1,0:T(8,128)(2,1)S(1)}, u32[]{:S(2)}, u32[]{:S(2)}) collective-permute-start(bf16[32,2048]{1,0:T(8,128)(2,1)S(1)} %pad_maximum_fusion.refs_0_._), channel_id=1, source_target_pairs={{0,1},{1,0},{2,3},{3,2},{4,5},{5,4},{6,7},{7,6},{8,9},{9,8},{10,11... | collective-permute-start | bytes 393224 | tf_op jit(solution)/shard_map/ppermute | solution.py:40
  18.5 11.6 %collective-permute-start.10 = (bf16[512,512]{1,0:T(8,128)(2,1)S(1)}, bf16[512,512]{1,0:T(8,128)(2,1)S(1)}, u32[]{:S(2)}, u32[]{:S(2)}) collective-permute-start(bf16[512,512]{1,0:T(8,128)(2,1)S(1)} %get-tuple-element.42), channel_id=1, source_target_pairs={{0,8},{1,9},{2,10},{3,11},{4,12},{5,13},{6,14},{7,15},{8,0},{9,1},... | collective-permute-start | bytes 1572872 | tf_op jit(solution)/shard_map/ppermute | solution.py:40
  18.7 11.4 %collective-permute-start.9 = (bf16[512,512]{1,0:T(8,128)(2,1)S(1)}, bf16[512,512]{1,0:T(8,128)(2,1)S(1)}, u32[]{:S(2)}, u32[]{:S(2)}) collective-permute-start(bf16[512,512]{1,0:T(8,128)(2,1)S(1)} %get-tuple-element.41), channel_id=1, source_target_pairs={{0,8},{1,9},{2,10},{3,11},{4,12},{5,13},{6,14},{7,15},{8,0},{9,1},... | collective-permute-start | bytes 1572872 | tf_op jit(solution)/shard_map/ppermute | solution.py:40
  22.7 1.5 %collective-permute-start.7 = (bf16[64,1536]{1,0:T(8,128)(2,1)S(1)}, bf16[64,1536]{1,0:T(8,128)(2,1)S(1)}, u32[]{:S(2)}, u32[]{:S(2)}) collective-permute-start(bf16[64,1536]{1,0:T(8,128)(2,1)S(1)} %shard_map.87), channel_id=1, source_target_pairs={{0,8},{1,9},{2,10},{3,11},{4,12},{5,13},{6,14},{7,15},{8,0},{9,1},... | collective-permute-start | bytes 589832 | tf_op jit(solution)/shard_map/ppermute | solution.py:40
  24.3 5.8 %collective-permute-start.8 = (bf16[128,512]{1,0:T(8,128)(2,1)S(1)}, bf16[128,512]{1,0:T(8,128)(2,1)S(1)}, u32[]{:S(2)}, u32[]{:S(2)}) collective-permute-start(bf16[128,512]{1,0:T(8,128)(2,1)S(1)} %get-tuple-element.40), channel_id=1, source_target_pairs={{0,16},{1,17},{2,18},{3,19},{4,20},{5,21},{6,22},{7,23},{8,24},{9,... | collective-permute-start | bytes 393224 | tf_op jit(solution)/shard_map/ppermute | solution.py:40
  31.3 1.9 %collective-permute-start.11 = (bf16[32,640]{1,0:T(8,128)(2,1)S(1)}, bf16[32,640]{1,0:T(8,128)(2,1)S(1)}, u32[]{:S(2)}, u32[]{:S(2)}) collective-permute-start(bf16[32,640]{1,0:T(8,128)(2,1)S(1)} %get-tuple-element.44), channel_id=1, source_target_pairs={{0,8},{1,9},{2,10},{3,11},{4,12},{5,13},{6,14},{7,15},{8,0},{9,1},... | collective-permute-start | bytes 122888 | tf_op jit(solution)/shard_map/ppermute | solution.py:40
  31.4 4.1 %collective-permute-start.12 = (bf16[32,640]{1,0:T(8,128)(2,1)S(1)}, bf16[32,640]{1,0:T(8,128)(2,1)S(1)}, u32[]{:S(2)}, u32[]{:S(2)}) collective-permute-start(bf16[32,640]{1,0:T(8,128)(2,1)S(1)} %get-tuple-element.43.refs_0_), channel_id=1, source_target_pairs={{0,16},{1,17},{2,18},{3,19},{4,20},{5,21},{6,22},{7,23},{8,24},{9,... | collective-permute-start | bytes 122888 | tf_op jit(solution)/shard_map/ppermute | solution.py:40
  33.0 3.5 %collective-permute-start.13 = (bf16[32,640]{1,0:T(8,128)(2,1)S(1)}, bf16[32,640]{1,0:T(8,128)(2,1)S(1)}, u32[]{:S(2)}, u32[]{:S(2)}) collective-permute-start(bf16[32,640]{1,0:T(8,128)(2,1)S(1)} %get-tuple-element.44), channel_id=1, source_target_pairs={{0,24},{1,25},{2,26},{3,27},{4,28},{5,29},{6,30},{7,31},{8,16},{9,... | collective-permute-start | bytes 122888 | tf_op jit(solution)/shard_map/ppermute | solution.py:40
  38.4 5.5 %collective-permute-start.15 = (bf16[2,16,1024]{2,1,0:T(8,128)(2,1)S(1)}, bf16[2,16,1024]{2,1,0:T(8,128)(2,1)S(1)}, u32[]{:S(2)}, u32[]{:S(2)}) collective-permute-start(bf16[2,16,1024]{2,1,0:T(8,128)(2,1)S(1)} %get-tuple-element.46), channel_id=1, source_target_pairs={{0,17},{1,16},{2,19},{3,18},{4,21},{5,20},{6,23},{7,22},{8,25},{9,... | collective-permute-start | bytes 196616 | tf_op jit(solution)/shard_map/ppermute | solution.py:40
  40.1 4.3 %collective-permute-start.16 = (bf16[2,16,1024]{2,1,0:T(8,128)(2,1)S(1)}, bf16[2,16,1024]{2,1,0:T(8,128)(2,1)S(1)}, u32[]{:S(2)}, u32[]{:S(2)}) collective-permute-start(bf16[2,16,1024]{2,1,0:T(8,128)(2,1)S(1)} %get-tuple-element.47), channel_id=1, source_target_pairs={{0,1},{1,0},{2,3},{3,2},{4,5},{5,4},{6,7},{7,6},{8,9},{9,8},{10,11... | collective-permute-start | bytes 196616 | tf_op jit(solution)/shard_map/ppermute | solution.py:40
  40.7 4.3 %collective-permute-start.17 = (bf16[2,16,1024]{2,1,0:T(8,128)(2,1)S(1)}, bf16[2,16,1024]{2,1,0:T(8,128)(2,1)S(1)}, u32[]{:S(2)}, u32[]{:S(2)}) collective-permute-start(bf16[2,16,1024]{2,1,0:T(8,128)(2,1)S(1)} %get-tuple-element.48), channel_id=1, source_target_pairs={{0,16},{1,17},{2,18},{3,19},{4,20},{5,21},{6,22},{7,23},{8,24},{9,... | collective-permute-start | bytes 196616 | tf_op jit(solution)/shard_map/ppermute | solution.py:40
  45.0 5.8 %collective-permute-start.18 = (bf16[16,1024]{1,0:T(8,128)(2,1)S(1)}, bf16[16,1024]{1,0:T(8,128)(2,1)S(1)}, u32[]{:S(2)}, u32[]{:S(2)}) collective-permute-start(bf16[16,1024]{1,0:T(8,128)(2,1)S(1)} %get-tuple-element.51), channel_id=1, source_target_pairs={{0,6},{1,7},{2,4},{3,5},{4,2},{5,3},{6,0},{7,1},{8,14},{9,15},{10,... | collective-permute-start | bytes 98312 | tf_op jit(solution)/shard_map/ppermute | solution.py:40
  47.5 4.8 %collective-permute-start.19 = (bf16[16,1024]{1,0:T(8,128)(2,1)S(1)}, bf16[16,1024]{1,0:T(8,128)(2,1)S(1)}, u32[]{:S(2)}, u32[]{:S(2)}) collective-permute-start(bf16[16,1024]{1,0:T(8,128)(2,1)S(1)} %get-tuple-element.52), channel_id=1, source_target_pairs={{0,4},{1,5},{2,6},{3,7},{4,0},{5,1},{6,2},{7,3},{8,12},{9,13},{10,... | collective-permute-start | bytes 98312 | tf_op jit(solution)/shard_map/ppermute | solution.py:40
  48.1 4.3 %collective-permute-start.20 = (bf16[16,1024]{1,0:T(8,128)(2,1)S(1)}, bf16[16,1024]{1,0:T(8,128)(2,1)S(1)}, u32[]{:S(2)}, u32[]{:S(2)}) collective-permute-start(bf16[16,1024]{1,0:T(8,128)(2,1)S(1)} %get-tuple-element.53), channel_id=1, source_target_pairs={{0,2},{1,3},{2,0},{3,1},{4,6},{5,7},{6,4},{7,5},{8,10},{9,11},{10,... | collective-permute-start | bytes 98312 | tf_op jit(solution)/shard_map/ppermute | solution.py:40

commit v5 on v4

--- a/solution.py
+++ b/solution.py
@@ -246,7 +246,7 @@
 
 
 def gather_embedded(
-    plan, gen_ids, embed_rows, w_key, w_value, prompt_keys, prompt_values, w_out
+    plan, gen_ids, embed_rows, w_key, w_value, prompt_keys, prompt_values, swapped_out
 ):
     rows, places, beyond = pick(plan, gen_ids, embed_rows)
     rest = lax.cond(
@@ -257,8 +257,7 @@
     w_key = bring(rest, w_key)
     across = [plan.over_head(rows, step * plan.inner) for step in range(1, plan.outer)]
     near = jnp.concatenate([rows, *across])
-    near, w_key, w_out = lax.optimization_barrier((near, w_key, w_out))
-    swapped_out = plan.over_seq(w_out, 1)
+    near, w_key, swapped_out = lax.optimization_barrier((near, w_key, swapped_out))
     given = prompt_to_swap(plan, near, prompt_keys, prompt_values)
     w_value = bring(near, w_value)
     blocks = [near] + [plan.over_head(near, step) for step in range(1, plan.inner)[::-1]]
@@ -615,12 +614,14 @@
 def solution(mesh):
     def body(gen_ids, embed_rows, w_query, w_key, w_value, w_out, prompt_keys, prompt_values):
         plan = Plan(mesh, gen_ids, w_query, w_out, prompt_keys)
+        swapped_out = plan.over_seq(w_out, 1)
         embedded, w_key, w_value, given, swapped_out = gather_embedded(
-            plan, gen_ids, embed_rows, w_key, w_value, prompt_keys, prompt_values, w_out
+            plan, gen_ids, embed_rows, w_key, w_value, prompt_keys, prompt_values, swapped_out
         )
         swapped = [plan.over_seq(part, 1) for part in given]
         parts = project(plan, embedded, (w_query, w_key, w_value))
         kept = prompt_half(plan, prompt_keys, prompt_values, parts[0])
+        swapped_out = bring(parts[0], swapped_out)
         attended = attend(plan, parts, kept, swapped, angle_tables(plan))
         return sum_parts(plan, multiply_out(plan, attended, w_out, swapped_out))
 

time: 53.2 us -> 53.1 us (level)
  Pallas kernels: 16.2 us -> 18.3 us
  waiting for transfers between devices: 14.6 us -> 12.9 us
  local copies, waits for them, and re-layouts: 1.55 us -> 0.55 us
    pallas_call x13 -> x14, Pallas kernels: 16.2 us -> 18.3 us  [call(): pl.pallas_call(kernel, out_shape=out_shape, in_specs=in_specs, out_specs=...]
    ppermute x18, waiting for transfers between devices: 14.6 us -> 12.9 us  [send(): return lax.ppermute(value, ('seq', 'head'), pairs)]
    unnamed x6, local copies, waits for them, and re-layouts: 1.02 us -> 0.02 us
  transfers between devices with their start and end apart: 18 -> 18, of which waited for: 11 -> 11; matrix products, arithmetic and copies ran while one was open for 1% -> 1% of each run, Pallas kernels for 21% -> 28%
where the time goes in v5:
time: 53.1 us; the launch traced here: 52.9 us
  starting transfers between devices  20 us (38%)
  Pallas kernels  18.3 us (34%)
  waiting for transfers between devices  12.9 us (24%)
  between operations  0.86 us (2%)
  local copies, waits for them, and re-layouts  0.55 us (1%)
    ppermute x18, starting transfers between devices, send(): return lax.ppermute(value, ('seq', 'head'), pairs)  20 us
    pallas_call x14, Pallas kernels, call(): pl.pallas_call(kernel, out_shape=out_shape, in_specs=in_specs, out_specs=...  18.3 us
    ppermute x18, waiting for transfers between devices, send(): return lax.ppermute(value, ('seq', 'head'), pairs)  12.9 us
  transfers between devices with their start and end apart: 18, of which 11 were waited for; matrix products, arithmetic and copies ran while one was open for 1% of the time, Pallas kernels for 28%

profile of v5, /device:TPU:0, one launch (start us, length us, event | category | flops | bytes accessed | tf_op | source)
XLA Modules:
  0.0 52.9 jit_solution(13181963277364786671)
XLA Ops:
  0.0 0.0 copy-start.2
  0.0 0.5 collective-permute-start.4
  0.5 2.7 %shard_map.82 = (bf16[16,2048]{1,0:T(8,128)(2,1)S(1)}, bf16[64,128]{1,0:T(8,128)(2,1)S(1)}, f32[8,128]{1,0:T(8,128)S(1)}) custom-call(s32[4,16]{1,0:T(4,128)} %ids_ref.1, bf16[1024,2048]{1,0:T(8,128)(2,1)} %embed_ref.1), custom_call_target="tpu_custom_call" | custom-call | tf_op jit(solution)/shard_map/pallas_call | solution.py:62
  3.2 3.7 %collective-permute-start.3 = (bf16[16,2048]{1,0:T(8,128)(2,1)S(1)}, bf16[16,2048]{1,0:T(8,128)(2,1)S(1)}, u32[]{:S(2)}, u32[]{:S(2)}) collective-permute-start(bf16[16,2048]{1,0:T(8,128)(2,1)S(1)} %get-tuple-element.36), channel_id=1, source_target_pairs={{0,4},{1,5},{2,6},{3,7},{4,0},{5,1},{6,2},{7,3},{8,12},{9,13},{10,... | collective-permute-start | bytes 196616 | tf_op jit(solution)/shard_map/ppermute | solution.py:40
  6.9 0.5 slice.3
  8.0 0.0 copy-done.2
  8.1 2.2 %shard_map.83.refs_1_ = bf16[2048,1024]{1,0:T(8,128)(2,1)S(1)} custom-call(bf16[64,2048]{1,0:T(8,128)(2,1)S(1)} %get-tuple-element.59._.rest_ref, bf16[2048,1024]{1,0:T(8,128)(2,1)} %source_ref.2), custom_call_target="tpu_custom_call" | custom-call | tf_op jit(solution)/shard_map/pallas_call | solution.py:62
  10.3 0.5 collective-permute-done.3
  10.8 0.0 copy-start
  10.8 0.0 collective-permute-done.4.source_ref
  10.8 2.1 %collective-permute-start.5 = (bf16[32,2048]{1,0:T(8,128)(2,1)S(1)}, bf16[32,2048]{1,0:T(8,128)(2,1)S(1)}, u32[]{:S(2)}, u32[]{:S(2)}) collective-permute-start(bf16[32,2048]{1,0:T(8,128)(2,1)S(1)} %pad_maximum_fusion.refs_0_._), channel_id=1, source_target_pairs={{0,3},{1,2},{2,1},{3,0},{4,7},{5,6},{6,5},{7,4},{8,11},{9,10},{10,... | collective-permute-start | bytes 393224 | tf_op jit(solution)/shard_map/ppermute | solution.py:40
  12.9 1.0 %collective-permute-start.6 = (bf16[32,2048]{1,0:T(8,128)(2,1)S(1)}, bf16[32,2048]{1,0:T(8,128)(2,1)S(1)}, u32[]{:S(2)}, u32[]{:S(2)}) collective-permute-start(bf16[32,2048]{1,0:T(8,128)(2,1)S(1)} %pad_maximum_fusion.refs_0_._), channel_id=1, source_target_pairs={{0,2},{1,3},{2,0},{3,1},{4,6},{5,7},{6,4},{7,5},{8,10},{9,11},{10,... | collective-permute-start | bytes 393224 | tf_op jit(solution)/shard_map/ppermute | solution.py:40
  13.9 0.5 collective-permute-start.7
  14.4 2.2 %shard_map.85.refs_2_ = bf16[2048,1024]{1,0:T(8,128)(2,1)S(1)} custom-call(bf16[32,2048]{1,0:T(8,128)(2,1)S(1)} %pad_maximum_fusion.refs_0_._, bf16[2048,1024]{1,0:T(8,128)(2,1)} %source_ref.3), custom_call_target="tpu_custom_call" | custom-call | tf_op jit(solution)/shard_map/pallas_call | solution.py:62
  16.6 1.2 %shard_map.90 = (bf16[512,512]{1,0:T(8,128)(2,1)S(1)}, bf16[512,512]{1,0:T(8,128)(2,1)S(1)}) custom-call(bf16[32,2048]{1,0:T(8,128)(2,1)S(1)} %pad_maximum_fusion.refs_0_._, bf16[512,1024]{1,0:T(8,128)(2,1)} %keys_ref.3, bf16[512,1024]{1,0:T(8,128)(2,1)} %values_ref.3), custom_call_target="tpu_custom_call" | custom-call | tf_op jit(solution)/shard_map/pallas_call | solution.py:62
  17.8 0.1 collective-permute-start.10
  17.9 0.5 collective-permute-start.11
  18.4 0.0 collective-permute-done.5.refs_1_
  18.4 1.1 %collective-permute-done.6.refs_2_ = bf16[32,2048]{1,0:T(8,128)(2,1)S(1)} collective-permute-done((bf16[32,2048]{1,0:T(8,128)(2,1)S(1)}, bf16[32,2048]{1,0:T(8,128)(2,1)S(1)}, u32[]{:S(2)}, u32[]{:S(2)}) %collective-permute-start.6) | collective-permute-done | bytes 131104 | tf_op jit(solution)/shard_map/ppermute | solution.py:40
  19.5 0.1 collective-permute-done.7.refs_3_
  19.6 0.2 shard_map.84.rows_ref
  19.8 0.0 copy-done
  19.8 1.2 %shard_map.87 = bf16[64,1536]{1,0:T(8,128)(2,1)S(1)} custom-call(bf16[64,2048]{1,0:T(8,128)(2,1)S(1)} %shard_map.84.rows_ref, bf16[2048,1024]{1,0:T(8,128)(2,1)S(1)} %copy-done, bf16[2048,1024]{1,0:T(8,128)(2,1)S(1)} %shard_map.83.refs_1_, bf16[2048,1024]{1,0:T(8,128)(2,1)S(1)} %shard_map.85.refs_2_), custom_call_target="tpu_custom_call" | custom-call | tf_op jit(solution)/shard_map/pallas_call | solution.py:62
  21.1 0.1 collective-permute-start.8
  21.2 1.2 %shard_map.86.own_ref = f32[64,1536]{1,0:T(8,128)S(1)} custom-call(bf16[64,2048]{1,0:T(8,128)(2,1)S(1)} %shard_map.84.rows_ref, bf16[2048,1024]{1,0:T(8,128)(2,1)S(1)} %copy-done, bf16[2048,1024]{1,0:T(8,128)(2,1)S(1)} %shard_map.83.refs_1_, bf16[2048,1024]{1,0:T(8,128)(2,1)S(1)} %shard_map.85.refs_2_), custom_call_target="tpu_custom_call" | custom-call | tf_op jit(solution)/shard_map/pallas_call | solution.py:62
  22.4 0.2 collective-permute-done.8.received_ref
  22.6 0.1 shard_map.88
  22.7 1.6 %collective-permute-start.9 = (bf16[128,512]{1,0:T(8,128)(2,1)S(1)}, bf16[128,512]{1,0:T(8,128)(2,1)S(1)}, u32[]{:S(2)}, u32[]{:S(2)}) collective-permute-start(bf16[128,512]{1,0:T(8,128)(2,1)S(1)} %get-tuple-element.40), channel_id=1, source_target_pairs={{0,16},{1,17},{2,18},{3,19},{4,20},{5,21},{6,22},{7,23},{8,24},{9,... | collective-permute-start | bytes 393224 | tf_op jit(solution)/shard_map/ppermute | solution.py:40
  24.2 0.1 fusion.2
  24.4 0.1 pad_maximum_fusion.1
  24.4 1.2 %shard_map.89.refs_2_ = bf16[1024,512]{1,0:T(8,128)(2,1)S(1)} custom-call(f32[128,512]{1,0:T(8,128)S(1)} %get-tuple-element.39._.refs_0_, bf16[512,1024]{1,0:T(8,128)(2,1)} %keys_ref.3, bf16[512,1024]{1,0:T(8,128)(2,1)} %values_ref.3), custom_call_target="tpu_custom_call" | custom-call | tf_op jit(solution)/shard_map/pallas_call | solution.py:62
  25.7 2.8 %collective-permute-done.9.refs_1_ = bf16[128,512]{1,0:T(8,128)(2,1)S(1)} collective-permute-done((bf16[128,512]{1,0:T(8,128)(2,1)S(1)}, bf16[128,512]{1,0:T(8,128)(2,1)S(1)}, u32[]{:S(2)}, u32[]{:S(2)}) %collective-permute-start.9) | collective-permute-done | bytes 131104 | tf_op jit(solution)/shard_map/ppermute | solution.py:40
  28.5 0.0 collective-permute-done.10.refs_3_
  28.5 0.0 collective-permute-done.11.refs_4_
  28.5 1.2 %shard_map.91 = (bf16[32,640]{1,0:T(8,128)(2,1)S(1)}, bf16[32,640]{1,0:T(8,128)(2,1)S(1)}) custom-call(f32[128,512]{1,0:T(8,128)S(1)} %get-tuple-element.39._.refs_0_, bf16[128,512]{1,0:T(8,128)(2,1)S(1)} %collective-permute-done.9.refs_1_, bf16[1024,512]{1,0:T(8,128)(2,1)S(1)} %shard_map.89.refs_2_, bf16[512,512]{1,0:T(8,128)(2,1)S(1)} %collective-permute-done.10.refs_3_, ...), custom_call_target="tpu_custom_call" | custom-call | tf_op jit(solution)/shard_map/pallas_call | solution.py:62
  29.7 0.1 collective-permute-start.12
  29.8 0.0 copy-start.1
  29.8 1.6 %collective-permute-start.13 = (bf16[32,640]{1,0:T(8,128)(2,1)S(1)}, bf16[32,640]{1,0:T(8,128)(2,1)S(1)}, u32[]{:S(2)}, u32[]{:S(2)}) collective-permute-start(bf16[32,640]{1,0:T(8,128)(2,1)S(1)} %get-tuple-element.43.refs_0_), channel_id=1, source_target_pairs={{0,16},{1,17},{2,18},{3,19},{4,20},{5,21},{6,22},{7,23},{8,24},{9,... | collective-permute-start | bytes 122888 | tf_op jit(solution)/shard_map/ppermute | solution.py:40
  31.4 0.3 collective-permute-start.14
  31.6 2.2 %shard_map.92.refs_5_ = bf16[1024,2048]{1,0:T(8,128)(2,1)S(1)} custom-call(f32[128,512]{1,0:T(8,128)S(1)} %get-tuple-element.39._.refs_0_, bf16[1024,2048]{1,0:T(8,128)(2,1)} %collective-permute-done.4.source_ref), custom_call_target="tpu_custom_call" | custom-call | tf_op jit(solution)/shard_map/pallas_call | solution.py:62
  33.8 0.0 collective-permute-done.12.refs_1_
  33.9 0.0 collective-permute-done.13.refs_2_
  33.9 1.0 %collective-permute-done.14.refs_3_ = bf16[32,640]{1,0:T(8,128)(2,1)S(1)} collective-permute-done((bf16[32,640]{1,0:T(8,128)(2,1)S(1)}, bf16[32,640]{1,0:T(8,128)(2,1)S(1)}, u32[]{:S(2)}, u32[]{:S(2)}) %collective-permute-start.14) | collective-permute-done | bytes 40992 | tf_op jit(solution)/shard_map/ppermute | solution.py:40
  34.9 0.0 copy-done.1
  34.9 1.8 %shard_map.93 = (f32[2,16,1024]{2,1,0:T(8,128)S(1)}, bf16[2,16,1024]{2,1,0:T(8,128)(2,1)S(1)}, bf16[2,16,1024]{2,1,0:T(8,128)(2,1)S(1)}, bf16[2,16,1024]{2,1,0:T(8,128)(2,1)S(1)}) custom-call(bf16[32,640]{1,0:T(8,128)(2,1)S(1)} %get-tuple-element.43.refs_0_, bf16[32,640]{1,0:T(8,128)(2,1)S(1)} %collective-permute-done.12.refs_1_, ...), custom_call_target="tpu_custom_call" | custom-call | tf_op jit(solution)/shard_map/pallas_call | solution.py:62
  36.7 1.7 %collective-permute-start.15 = (bf16[2,16,1024]{2,1,0:T(8,128)(2,1)S(1)}, bf16[2,16,1024]{2,1,0:T(8,128)(2,1)S(1)}, u32[]{:S(2)}, u32[]{:S(2)}) collective-permute-start(bf16[2,16,1024]{2,1,0:T(8,128)(2,1)S(1)} %get-tuple-element.46), channel_id=1, source_target_pairs={{0,17},{1,16},{2,19},{3,18},{4,21},{5,20},{6,23},{7,22},{8,25},{9,... | collective-permute-start | bytes 196616 | tf_op jit(solution)/shard_map/ppermute | solution.py:40
  38.4 0.6 %collective-permute-start.16 = (bf16[2,16,1024]{2,1,0:T(8,128)(2,1)S(1)}, bf16[2,16,1024]{2,1,0:T(8,128)(2,1)S(1)}, u32[]{:S(2)}, u32[]{:S(2)}) collective-permute-start(bf16[2,16,1024]{2,1,0:T(8,128)(2,1)S(1)} %get-tuple-element.47), channel_id=1, source_target_pairs={{0,1},{1,0},{2,3},{3,2},{4,5},{5,4},{6,7},{7,6},{8,9},{9,8},{10,11... | collective-permute-start | bytes 196616 | tf_op jit(solution)/shard_map/ppermute | solution.py:40
  39.0 1.2 %collective-permute-start.17 = (bf16[2,16,1024]{2,1,0:T(8,128)(2,1)S(1)}, bf16[2,16,1024]{2,1,0:T(8,128)(2,1)S(1)}, u32[]{:S(2)}, u32[]{:S(2)}) collective-permute-start(bf16[2,16,1024]{2,1,0:T(8,128)(2,1)S(1)} %get-tuple-element.48), channel_id=1, source_target_pairs={{0,16},{1,17},{2,18},{3,19},{4,20},{5,21},{6,22},{7,23},{8,24},{9,... | collective-permute-start | bytes 196616 | tf_op jit(solution)/shard_map/ppermute | solution.py:40
  40.2 2.1 %collective-permute-done.15.refs_0_ = bf16[2,16,1024]{2,1,0:T(8,128)(2,1)S(1)} collective-permute-done((bf16[2,16,1024]{2,1,0:T(8,128)(2,1)S(1)}, bf16[2,16,1024]{2,1,0:T(8,128)(2,1)S(1)}, u32[]{:S(2)}, u32[]{:S(2)}) %collective-permute-start.15) | collective-permute-done | bytes 65568 | tf_op jit(solution)/shard_map/ppermute | solution.py:40
  42.3 0.4 collective-permute-done.16.refs_1_
  42.7 0.6 %collective-permute-done.17.refs_2_ = bf16[2,16,1024]{2,1,0:T(8,128)(2,1)S(1)} collective-permute-done((bf16[2,16,1024]{2,1,0:T(8,128)(2,1)S(1)}, bf16[2,16,1024]{2,1,0:T(8,128)(2,1)S(1)}, u32[]{:S(2)}, u32[]{:S(2)}) %collective-permute-start.17) | collective-permute-done | bytes 65568 | tf_op jit(solution)/shard_map/ppermute | solution.py:40
  43.4 4.1 %collective-permute-start.18 = (bf16[16,1024]{1,0:T(8,128)(2,1)S(1)}, bf16[16,1024]{1,0:T(8,128)(2,1)S(1)}, u32[]{:S(2)}, u32[]{:S(2)}) collective-permute-start(bf16[16,1024]{1,0:T(8,128)(2,1)S(1)} %get-tuple-element.51), channel_id=1, source_target_pairs={{0,6},{1,7},{2,4},{3,5},{4,2},{5,3},{6,0},{7,1},{8,14},{9,15},{10,... | collective-permute-start | bytes 98312 | tf_op jit(solution)/shard_map/ppermute | solution.py:40
  47.4 0.0 collective-permute-start.19
  47.4 0.6 %collective-permute-start.20 = (bf16[16,1024]{1,0:T(8,128)(2,1)S(1)}, bf16[16,1024]{1,0:T(8,128)(2,1)S(1)}, u32[]{:S(2)}, u32[]{:S(2)}) collective-permute-start(bf16[16,1024]{1,0:T(8,128)(2,1)S(1)} %get-tuple-element.53), channel_id=1, source_target_pairs={{0,2},{1,3},{2,0},{3,1},{4,6},{5,7},{6,4},{7,5},{8,10},{9,11},{10,... | collective-permute-start | bytes 98312 | tf_op jit(solution)/shard_map/ppermute | solution.py:40
  48.1 1.7 %collective-permute-done.18.refs_1_ = bf16[16,1024]{1,0:T(8,128)(2,1)S(1)} collective-permute-done((bf16[16,1024]{1,0:T(8,128)(2,1)S(1)}, bf16[16,1024]{1,0:T(8,128)(2,1)S(1)}, u32[]{:S(2)}, u32[]{:S(2)}) %collective-permute-start.18) | collective-permute-done | bytes 32800 | tf_op jit(solution)/shard_map/ppermute | solution.py:40
  49.7 2.5 %collective-permute-done.19.refs_2_ = bf16[16,1024]{1,0:T(8,128)(2,1)S(1)} collective-permute-done((bf16[16,1024]{1,0:T(8,128)(2,1)S(1)}, bf16[16,1024]{1,0:T(8,128)(2,1)S(1)}, u32[]{:S(2)}, u32[]{:S(2)}) %collective-permute-start.19) | collective-permute-done | bytes 32800 | tf_op jit(solution)/shard_map/ppermute | solution.py:40
  52.3 0.0 collective-permute-done.20.refs_3_
  52.3 0.6 %shard_map.95 = bf16[16,1024]{1,0:T(8,128)(2,1)} custom-call(f32[16,1024]{1,0:T(8,128)S(1)} %get-tuple-element.50.refs_0_, bf16[16,1024]{1,0:T(8,128)(2,1)S(1)} %collective-permute-done.18.refs_1_, bf16[16,1024]{1,0:T(8,128)(2,1)S(1)} %collective-permute-done.19.refs_2_, bf16[16,1024]{1,0:T(8,128)(2,1)S(1)} %collective-permute-done.20.refs_3_), custom_call_target="tpu_custom_call" | custom-call | tf_op jit(solution)/shard_map/pallas_call | solution.py:62
  (6 shorter events, 0.1 us)
Async XLA Ops:
  0.0 8.0 %copy-start.2 = (s32[4,16]{1,0:T(4,128)S(1)}, s32[4,16]{1,0:T(4,128)}, u32[]{:S(2)}) copy-start(s32[4,16]{1,0:T(4,128)} %ids_ref.1) | copy-start | bytes 772
  0.0 10.8 %collective-permute-start.4 = (bf16[1024,2048]{1,0:T(8,128)(2,1)}, bf16[1024,2048]{1,0:T(8,128)(2,1)}, u32[]{:S(2)}, u32[]{:S(2)}) collective-permute-start(bf16[1024,2048]{1,0:T(8,128)(2,1)} %refs_4_.1), channel_id=1, source_target_pairs={{0,8},{1,9},{2,10},{3,11},{4,12},{5,13},{6,14},{7,15},{8,0},{9,1},... | collective-permute-start | bytes 12582920 | tf_op jit(solution)/shard_map/ppermute | solution.py:40
  3.2 7.6 %collective-permute-start.3 = (bf16[16,2048]{1,0:T(8,128)(2,1)S(1)}, bf16[16,2048]{1,0:T(8,128)(2,1)S(1)}, u32[]{:S(2)}, u32[]{:S(2)}) collective-permute-start(bf16[16,2048]{1,0:T(8,128)(2,1)S(1)} %get-tuple-element.36), channel_id=1, source_target_pairs={{0,4},{1,5},{2,6},{3,7},{4,0},{5,1},{6,2},{7,3},{8,12},{9,13},{10,... | collective-permute-start | bytes 196616 | tf_op jit(solution)/shard_map/ppermute | solution.py:40
  10.8 9.0 %copy-start = (bf16[2048,1024]{1,0:T(8,128)(2,1)S(1)}, bf16[2048,1024]{1,0:T(8,128)(2,1)}, u32[]{:S(2)}) copy-start(bf16[2048,1024]{1,0:T(8,128)(2,1)} %refs_0_.3) | copy-start | bytes 12582916
  10.8 7.6 %collective-permute-start.5 = (bf16[32,2048]{1,0:T(8,128)(2,1)S(1)}, bf16[32,2048]{1,0:T(8,128)(2,1)S(1)}, u32[]{:S(2)}, u32[]{:S(2)}) collective-permute-start(bf16[32,2048]{1,0:T(8,128)(2,1)S(1)} %pad_maximum_fusion.refs_0_._), channel_id=1, source_target_pairs={{0,3},{1,2},{2,1},{3,0},{4,7},{5,6},{6,5},{7,4},{8,11},{9,10},{10,... | collective-permute-start | bytes 393224 | tf_op jit(solution)/shard_map/ppermute | solution.py:40
  12.9 6.6 %collective-permute-start.6 = (bf16[32,2048]{1,0:T(8,128)(2,1)S(1)}, bf16[32,2048]{1,0:T(8,128)(2,1)S(1)}, u32[]{:S(2)}, u32[]{:S(2)}) collective-permute-start(bf16[32,2048]{1,0:T(8,128)(2,1)S(1)} %pad_maximum_fusion.refs_0_._), channel_id=1, source_target_pairs={{0,2},{1,3},{2,0},{3,1},{4,6},{5,7},{6,4},{7,5},{8,10},{9,11},{10,... | collective-permute-start | bytes 393224 | tf_op jit(solution)/shard_map/ppermute | solution.py:40
  13.9 5.7 %collective-permute-start.7 = (bf16[32,2048]{1,0:T(8,128)(2,1)S(1)}, bf16[32,2048]{1,0:T(8,128)(2,1)S(1)}, u32[]{:S(2)}, u32[]{:S(2)}) collective-permute-start(bf16[32,2048]{1,0:T(8,128)(2,1)S(1)} %pad_maximum_fusion.refs_0_._), channel_id=1, source_target_pairs={{0,1},{1,0},{2,3},{3,2},{4,5},{5,4},{6,7},{7,6},{8,9},{9,8},{10,11... | collective-permute-start | bytes 393224 | tf_op jit(solution)/shard_map/ppermute | solution.py:40
  17.8 10.6 %collective-permute-start.10 = (bf16[512,512]{1,0:T(8,128)(2,1)S(1)}, bf16[512,512]{1,0:T(8,128)(2,1)S(1)}, u32[]{:S(2)}, u32[]{:S(2)}) collective-permute-start(bf16[512,512]{1,0:T(8,128)(2,1)S(1)} %get-tuple-element.41), channel_id=1, source_target_pairs={{0,8},{1,9},{2,10},{3,11},{4,12},{5,13},{6,14},{7,15},{8,0},{9,1},... | collective-permute-start | bytes 1572872 | tf_op jit(solution)/shard_map/ppermute | solution.py:40
  17.9 10.6 %collective-permute-start.11 = (bf16[512,512]{1,0:T(8,128)(2,1)S(1)}, bf16[512,512]{1,0:T(8,128)(2,1)S(1)}, u32[]{:S(2)}, u32[]{:S(2)}) collective-permute-start(bf16[512,512]{1,0:T(8,128)(2,1)S(1)} %get-tuple-element.42), channel_id=1, source_target_pairs={{0,8},{1,9},{2,10},{3,11},{4,12},{5,13},{6,14},{7,15},{8,0},{9,1},... | collective-permute-start | bytes 1572872 | tf_op jit(solution)/shard_map/ppermute | solution.py:40
  21.1 1.5 %collective-permute-start.8 = (bf16[64,1536]{1,0:T(8,128)(2,1)S(1)}, bf16[64,1536]{1,0:T(8,128)(2,1)S(1)}, u32[]{:S(2)}, u32[]{:S(2)}) collective-permute-start(bf16[64,1536]{1,0:T(8,128)(2,1)S(1)} %shard_map.87), channel_id=1, source_target_pairs={{0,8},{1,9},{2,10},{3,11},{4,12},{5,13},{6,14},{7,15},{8,0},{9,1},... | collective-permute-start | bytes 589832 | tf_op jit(solution)/shard_map/ppermute | solution.py:40
  22.7 5.8 %collective-permute-start.9 = (bf16[128,512]{1,0:T(8,128)(2,1)S(1)}, bf16[128,512]{1,0:T(8,128)(2,1)S(1)}, u32[]{:S(2)}, u32[]{:S(2)}) collective-permute-start(bf16[128,512]{1,0:T(8,128)(2,1)S(1)} %get-tuple-element.40), channel_id=1, source_target_pairs={{0,16},{1,17},{2,18},{3,19},{4,20},{5,21},{6,22},{7,23},{8,24},{9,... | collective-permute-start | bytes 393224 | tf_op jit(solution)/shard_map/ppermute | solution.py:40
  29.7 4.2 %collective-permute-start.12 = (bf16[32,640]{1,0:T(8,128)(2,1)S(1)}, bf16[32,640]{1,0:T(8,128)(2,1)S(1)}, u32[]{:S(2)}, u32[]{:S(2)}) collective-permute-start(bf16[32,640]{1,0:T(8,128)(2,1)S(1)} %get-tuple-element.44), channel_id=1, source_target_pairs={{0,8},{1,9},{2,10},{3,11},{4,12},{5,13},{6,14},{7,15},{8,0},{9,1},... | collective-permute-start | bytes 122888 | tf_op jit(solution)/shard_map/ppermute | solution.py:40
  29.8 5.1 %copy-start.1 = (bf16[1024,2048]{1,0:T(8,128)(2,1)S(1)}, bf16[1024,2048]{1,0:T(8,128)(2,1)}, u32[]{:S(2)}) copy-start(bf16[1024,2048]{1,0:T(8,128)(2,1)} %refs_4_.1) | copy-start | bytes 12582916
  29.8 4.1 %collective-permute-start.13 = (bf16[32,640]{1,0:T(8,128)(2,1)S(1)}, bf16[32,640]{1,0:T(8,128)(2,1)S(1)}, u32[]{:S(2)}, u32[]{:S(2)}) collective-permute-start(bf16[32,640]{1,0:T(8,128)(2,1)S(1)} %get-tuple-element.43.refs_0_), channel_id=1, source_target_pairs={{0,16},{1,17},{2,18},{3,19},{4,20},{5,21},{6,22},{7,23},{8,24},{9,... | collective-permute-start | bytes 122888 | tf_op jit(solution)/shard_map/ppermute | solution.py:40
  31.4 3.5 %collective-permute-start.14 = (bf16[32,640]{1,0:T(8,128)(2,1)S(1)}, bf16[32,640]{1,0:T(8,128)(2,1)S(1)}, u32[]{:S(2)}, u32[]{:S(2)}) collective-permute-start(bf16[32,640]{1,0:T(8,128)(2,1)S(1)} %get-tuple-element.44), channel_id=1, source_target_pairs={{0,24},{1,25},{2,26},{3,27},{4,28},{5,29},{6,30},{7,31},{8,16},{9,... | collective-permute-start | bytes 122888 | tf_op jit(solution)/shard_map/ppermute | solution.py:40
  36.7 5.6 %collective-permute-start.15 = (bf16[2,16,1024]{2,1,0:T(8,128)(2,1)S(1)}, bf16[2,16,1024]{2,1,0:T(8,128)(2,1)S(1)}, u32[]{:S(2)}, u32[]{:S(2)}) collective-permute-start(bf16[2,16,1024]{2,1,0:T(8,128)(2,1)S(1)} %get-tuple-element.46), channel_id=1, source_target_pairs={{0,17},{1,16},{2,19},{3,18},{4,21},{5,20},{6,23},{7,22},{8,25},{9,... | collective-permute-start | bytes 196616 | tf_op jit(solution)/shard_map/ppermute | solution.py:40
  38.4 4.3 %collective-permute-start.16 = (bf16[2,16,1024]{2,1,0:T(8,128)(2,1)S(1)}, bf16[2,16,1024]{2,1,0:T(8,128)(2,1)S(1)}, u32[]{:S(2)}, u32[]{:S(2)}) collective-permute-start(bf16[2,16,1024]{2,1,0:T(8,128)(2,1)S(1)} %get-tuple-element.47), channel_id=1, source_target_pairs={{0,1},{1,0},{2,3},{3,2},{4,5},{5,4},{6,7},{7,6},{8,9},{9,8},{10,11... | collective-permute-start | bytes 196616 | tf_op jit(solution)/shard_map/ppermute | solution.py:40
  39.0 4.3 %collective-permute-start.17 = (bf16[2,16,1024]{2,1,0:T(8,128)(2,1)S(1)}, bf16[2,16,1024]{2,1,0:T(8,128)(2,1)S(1)}, u32[]{:S(2)}, u32[]{:S(2)}) collective-permute-start(bf16[2,16,1024]{2,1,0:T(8,128)(2,1)S(1)} %get-tuple-element.48), channel_id=1, source_target_pairs={{0,16},{1,17},{2,18},{3,19},{4,20},{5,21},{6,22},{7,23},{8,24},{9,... | collective-permute-start | bytes 196616 | tf_op jit(solution)/shard_map/ppermute | solution.py:40
  43.4 6.4 %collective-permute-start.18 = (bf16[16,1024]{1,0:T(8,128)(2,1)S(1)}, bf16[16,1024]{1,0:T(8,128)(2,1)S(1)}, u32[]{:S(2)}, u32[]{:S(2)}) collective-permute-start(bf16[16,1024]{1,0:T(8,128)(2,1)S(1)} %get-tuple-element.51), channel_id=1, source_target_pairs={{0,6},{1,7},{2,4},{3,5},{4,2},{5,3},{6,0},{7,1},{8,14},{9,15},{10,... | collective-permute-start | bytes 98312 | tf_op jit(solution)/shard_map/ppermute | solution.py:40
  47.4 4.8 %collective-permute-start.19 = (bf16[16,1024]{1,0:T(8,128)(2,1)S(1)}, bf16[16,1024]{1,0:T(8,128)(2,1)S(1)}, u32[]{:S(2)}, u32[]{:S(2)}) collective-permute-start(bf16[16,1024]{1,0:T(8,128)(2,1)S(1)} %get-tuple-element.52), channel_id=1, source_target_pairs={{0,4},{1,5},{2,6},{3,7},{4,0},{5,1},{6,2},{7,3},{8,12},{9,13},{10,... | collective-permute-start | bytes 98312 | tf_op jit(solution)/shard_map/ppermute | solution.py:40
  47.4 4.8 %collective-permute-start.20 = (bf16[16,1024]{1,0:T(8,128)(2,1)S(1)}, bf16[16,1024]{1,0:T(8,128)(2,1)S(1)}, u32[]{:S(2)}, u32[]{:S(2)}) collective-permute-start(bf16[16,1024]{1,0:T(8,128)(2,1)S(1)} %get-tuple-element.53), channel_id=1, source_target_pairs={{0,2},{1,3},{2,0},{3,1},{4,6},{5,7},{6,4},{7,5},{8,10},{9,11},{10,... | collective-permute-start | bytes 98312 | tf_op jit(solution)/shard_map/ppermute | solution.py:40

commit v6 on v2

--- a/solution.py
+++ b/solution.py
@@ -99,7 +99,7 @@
             copies.append(
                 pltpu.make_async_copy(embed_ref.at[window], held.at[window], sems.at[piece])
             )
-            copies[-1].start()
+            copies[-1].start(priority=piece % 2)
         base = (lax.axis_index("head") * vocab).astype(F32)
         first, second = iota((tokens, tokens), 0), iota((tokens, tokens), 1)
         ids_copy.wait()
@@ -223,8 +223,8 @@
             )
             for k in range(pieces)
         ]
-        for copy in copies:
-            copy.start()
+        for k, copy in enumerate(copies):
+            copy.start(priority=k % 2)
         for copy in copies:
             copy.wait()
 
@@ -268,7 +268,7 @@
 
 
 def gather_embedded(
-    plan, gen_ids, embed_rows, w_key, w_value, prompt_keys, prompt_values, w_out
+    plan, gen_ids, embed_rows, w_key, w_value, prompt_keys, prompt_values, swapped_out
 ):
     rows = pick(plan, gen_ids, embed_rows)
     places, beyond = find_places(plan, rows, gen_ids, embed_rows.shape[0])
@@ -280,8 +280,7 @@
     w_key = bring(rest, w_key)
     across = [plan.over_head(rows, step * plan.inner) for step in range(1, plan.outer)]
     near = jnp.concatenate([rows, *across])
-    near, w_key, w_out = lax.optimization_barrier((near, w_key, w_out))
-    swapped_out = plan.over_seq(w_out, 1)
+    near, w_key, swapped_out = lax.optimization_barrier((near, w_key, swapped_out))
     given = prompt_to_swap(plan, near, prompt_keys, prompt_values)
     w_value = bring(near, w_value)
     blocks = [near] + [plan.over_head(near, step) for step in range(1, plan.inner)[::-1]]
@@ -527,7 +526,7 @@
     def kernel(*refs):
         parts, refs = refs[: plan.seq], refs[plan.seq :]
         (own_ref, swapped_ref), refs = refs[:2], refs[2:]
-        outs, (joined, held) = refs[: len(keys)], refs[len(keys) :]
+        outs, (joined,) = refs[: len(keys)], refs[len(keys) :]
         seq_index = lax.axis_index("seq")
         chip, core = seq_index // CORES, lax.rem(seq_index, CORES)
         part_index = lax.rem(lax.axis_index("head"), plan.parts)
@@ -549,16 +548,18 @@
                 scales = [jnp.exp(one - top) for one in logs]
                 mixed = sum(f * source[:, lanes].astype(F32) for f, source in zip(scales, sources))
                 mixed = (mixed / sum(scales)).astype(BF16)
-                joined[:, pl.ds(pl.multiple_of(first + head * HD, HD), HD)] = mixed
+                window = pl.ds(pl.multiple_of(first + head * HD, HD), HD)
+                for owner in range(plan.chips):
+                    rows_of = mixed[owner * share : (owner + 1) * share]
+                    joined[aligned(owner ^ chip, share), window] = rows_of
         left = joined[...]
         for dx in list(range(plan.parts))[::-1]:
             lanes = aligned(part_index ^ dx, columns)
             for weight, block in ((own_ref, core), (swapped_ref, 1 - core)):
                 product = jnp.dot(left, weight[:, lanes], preferred_element_type=F32)
-                held[...] = product
                 for dy in range(plan.chips):
                     out = outs[keys.index((dy, dx))]
-                    out[block] = held[aligned(chip ^ dy, share), :].astype(out.dtype)
+                    out[block] = product[dy * share : (dy + 1) * share].astype(out.dtype)
 
     shape = (CORES, share, columns)
     outs = [jax.ShapeDtypeStruct(shape, BF16 if any(key) else F32) for key in keys]
@@ -567,7 +568,7 @@
         outs,
         [VMEM_SPEC] * (plan.seq + 2),
         [VMEM_SPEC] * len(keys),
-        [pltpu.VMEM((rows, plan.width), BF16), pltpu.VMEM((rows, columns), F32)],
+        [pltpu.VMEM((rows, plan.width), BF16)],
         24,
         *attended,
         own,
@@ -636,12 +637,14 @@
 def solution(mesh):
     def body(gen_ids, embed_rows, w_query, w_key, w_value, w_out, prompt_keys, prompt_values):
         plan = Plan(mesh, gen_ids, w_query, w_out, prompt_keys)
+        swapped_out = plan.over_seq(w_out, 1)
         embedded, w_key, w_value, given, swapped_out = gather_embedded(
-            plan, gen_ids, embed_rows, w_key, w_value, prompt_keys, prompt_values, w_out
+            plan, gen_ids, embed_rows, w_key, w_value, prompt_keys, prompt_values, swapped_out
         )
         swapped = [plan.over_seq(part, 1) for part in given]
         parts = project(plan, embedded, (w_query, w_key, w_value))
         kept = prompt_half(plan, prompt_keys, prompt_values, parts[0])
+        swapped_out = bring(parts[0], swapped_out)
         attended = attend(plan, parts, kept, swapped, angle_tables(plan))
         return sum_parts(plan, multiply_out(plan, attended, w_out, swapped_out))
 

time: 54.2 us -> 53.1 us (0.980)
  waiting for transfers between devices: 14.2 us -> 12.2 us
  Pallas kernels: 17.5 us -> 19.2 us
  local copies, waits for them, and re-layouts: 1.59 us -> 0.55 us
    ppermute x18, waiting for transfers between devices: 14.2 us -> 12.2 us  [send(): return lax.ppermute(value, ('seq', 'head'), pairs)]
    pallas_call x14 -> x15, Pallas kernels: 17.5 us -> 19.2 us  [call(): pl.pallas_call(kernel, out_shape=out_shape, in_specs=in_specs, out_specs=...]
    unnamed x6, local copies, waits for them, and re-layouts: 1.05 us -> 0.02 us
  transfers between devices with their start and end apart: 18 -> 18, of which waited for: 12 -> 9; matrix products, arithmetic and copies ran while one was open for 1% -> 1% of each run, Pallas kernels for 22% -> 29%
where the time goes in v6:
time: 53.1 us; the launch traced here: 52.9 us
  starting transfers between devices  19.8 us (37%)
  Pallas kernels  19.2 us (36%)
  waiting for transfers between devices  12.2 us (23%)
  between operations  0.88 us (2%)
  local copies, waits for them, and re-layouts  0.55 us (1%)
    ppermute x18, starting transfers between devices, send(): return lax.ppermute(value, ('seq', 'head'), pairs)  19.8 us
    pallas_call x15, Pallas kernels, call(): pl.pallas_call(kernel, out_shape=out_shape, in_specs=in_specs, out_specs=...  19.2 us
    ppermute x18, waiting for transfers between devices, send(): return lax.ppermute(value, ('seq', 'head'), pairs)  12.2 us
  transfers between devices with their start and end apart: 18, of which 9 were waited for; matrix products, arithmetic and copies ran while one was open for 1% of the time, Pallas kernels for 29%

profile of v6, /device:TPU:0, one launch (start us, length us, event | category | flops | bytes accessed | tf_op | source)
XLA Modules:
  0.0 52.9 jit_solution(9872404953428414108)
XLA Ops:
  0.0 0.0 copy-start.2
  0.0 0.5 collective-permute-start.4
  0.5 2.6 %shard_map.82._ = bf16[16,2048]{1,0:T(8,128)(2,1)S(1)} custom-call(s32[4,16]{1,0:T(4,128)} %ids_ref.3, bf16[1024,2048]{1,0:T(8,128)(2,1)} %embed_ref.1), custom_call_target="tpu_custom_call" | custom-call | tf_op jit(solution)/shard_map/pallas_call | solution.py:62
  3.1 3.7 %collective-permute-start.3 = (bf16[16,2048]{1,0:T(8,128)(2,1)S(1)}, bf16[16,2048]{1,0:T(8,128)(2,1)S(1)}, u32[]{:S(2)}, u32[]{:S(2)}) collective-permute-start(bf16[16,2048]{1,0:T(8,128)(2,1)S(1)} %shard_map.82._), channel_id=1, source_target_pairs={{0,4},{1,5},{2,6},{3,7},{4,0},{5,1},{6,2},{7,3},{8,12},{9,13},{10,... | collective-permute-start | bytes 196616 | tf_op jit(solution)/shard_map/ppermute | solution.py:40
  6.7 1.1 %shard_map.83 = (bf16[64,128]{1,0:T(8,128)(2,1)S(1)}, f32[8,128]{1,0:T(8,128)S(1)}) custom-call(bf16[16,2048]{1,0:T(8,128)(2,1)S(1)} %shard_map.82._, s32[4,16]{1,0:T(4,128)} %ids_ref.3), custom_call_target="tpu_custom_call" | custom-call | tf_op jit(solution)/shard_map/pallas_call | solution.py:62
  7.8 0.5 slice.3
  9.0 0.0 copy-done.2
  9.1 2.2 %shard_map.84.refs_1_ = bf16[2048,1024]{1,0:T(8,128)(2,1)S(1)} custom-call(bf16[64,2048]{1,0:T(8,128)(2,1)S(1)} %get-tuple-element.57._.rest_ref, bf16[2048,1024]{1,0:T(8,128)(2,1)} %source_ref.2), custom_call_target="tpu_custom_call" | custom-call | tf_op jit(solution)/shard_map/pallas_call | solution.py:62
  11.3 0.0 collective-permute-done.3
  11.3 0.0 copy-start
  11.3 0.0 collective-permute-done.4.source_ref
  11.3 2.6 %collective-permute-start.5 = (bf16[32,2048]{1,0:T(8,128)(2,1)S(1)}, bf16[32,2048]{1,0:T(8,128)(2,1)S(1)}, u32[]{:S(2)}, u32[]{:S(2)}) collective-permute-start(bf16[32,2048]{1,0:T(8,128)(2,1)S(1)} %pad_maximum_fusion.refs_0_._), channel_id=1, source_target_pairs={{0,3},{1,2},{2,1},{3,0},{4,7},{5,6},{6,5},{7,4},{8,11},{9,10},{10,... | collective-permute-start | bytes 393224 | tf_op jit(solution)/shard_map/ppermute | solution.py:40
  13.9 0.4 collective-permute-start.6
  14.4 0.5 %collective-permute-start.7 = (bf16[32,2048]{1,0:T(8,128)(2,1)S(1)}, bf16[32,2048]{1,0:T(8,128)(2,1)S(1)}, u32[]{:S(2)}, u32[]{:S(2)}) collective-permute-start(bf16[32,2048]{1,0:T(8,128)(2,1)S(1)} %pad_maximum_fusion.refs_0_._), channel_id=1, source_target_pairs={{0,1},{1,0},{2,3},{3,2},{4,5},{5,4},{6,7},{7,6},{8,9},{9,8},{10,11... | collective-permute-start | bytes 393224 | tf_op jit(solution)/shard_map/ppermute | solution.py:40
  14.9 2.2 %shard_map.86.refs_2_ = bf16[2048,1024]{1,0:T(8,128)(2,1)S(1)} custom-call(bf16[32,2048]{1,0:T(8,128)(2,1)S(1)} %pad_maximum_fusion.refs_0_._, bf16[2048,1024]{1,0:T(8,128)(2,1)} %source_ref.3), custom_call_target="tpu_custom_call" | custom-call | tf_op jit(solution)/shard_map/pallas_call | solution.py:62
  17.1 1.2 %shard_map.91 = (bf16[512,512]{1,0:T(8,128)(2,1)S(1)}, bf16[512,512]{1,0:T(8,128)(2,1)S(1)}) custom-call(bf16[32,2048]{1,0:T(8,128)(2,1)S(1)} %pad_maximum_fusion.refs_0_._, bf16[512,1024]{1,0:T(8,128)(2,1)} %keys_ref.3, bf16[512,1024]{1,0:T(8,128)(2,1)} %values_ref.3), custom_call_target="tpu_custom_call" | custom-call | tf_op jit(solution)/shard_map/pallas_call | solution.py:62
  18.3 0.1 collective-permute-start.10
  18.4 0.5 collective-permute-start.11
  18.9 0.0 collective-permute-done.5.refs_1_
  18.9 1.7 %collective-permute-done.6.refs_2_ = bf16[32,2048]{1,0:T(8,128)(2,1)S(1)} collective-permute-done((bf16[32,2048]{1,0:T(8,128)(2,1)S(1)}, bf16[32,2048]{1,0:T(8,128)(2,1)S(1)}, u32[]{:S(2)}, u32[]{:S(2)}) %collective-permute-start.6) | collective-permute-done | bytes 131104 | tf_op jit(solution)/shard_map/ppermute | solution.py:40
  20.6 0.0 collective-permute-done.7.refs_3_
  20.6 0.2 shard_map.85.rows_ref
  20.9 0.0 copy-done
  20.9 1.2 %shard_map.88 = bf16[64,1536]{1,0:T(8,128)(2,1)S(1)} custom-call(bf16[64,2048]{1,0:T(8,128)(2,1)S(1)} %shard_map.85.rows_ref, bf16[2048,1024]{1,0:T(8,128)(2,1)S(1)} %copy-done, bf16[2048,1024]{1,0:T(8,128)(2,1)S(1)} %shard_map.84.refs_1_, bf16[2048,1024]{1,0:T(8,128)(2,1)S(1)} %shard_map.86.refs_2_), custom_call_target="tpu_custom_call" | custom-call | tf_op jit(solution)/shard_map/pallas_call | solution.py:62
  22.1 0.1 collective-permute-start.8
  22.2 1.2 %shard_map.87.own_ref = f32[64,1536]{1,0:T(8,128)S(1)} custom-call(bf16[64,2048]{1,0:T(8,128)(2,1)S(1)} %shard_map.85.rows_ref, bf16[2048,1024]{1,0:T(8,128)(2,1)S(1)} %copy-done, bf16[2048,1024]{1,0:T(8,128)(2,1)S(1)} %shard_map.84.refs_1_, bf16[2048,1024]{1,0:T(8,128)(2,1)S(1)} %shard_map.86.refs_2_), custom_call_target="tpu_custom_call" | custom-call | tf_op jit(solution)/shard_map/pallas_call | solution.py:62
  23.4 0.2 collective-permute-done.8.received_ref
  23.6 0.1 shard_map.89
  23.7 1.6 %collective-permute-start.9 = (bf16[128,512]{1,0:T(8,128)(2,1)S(1)}, bf16[128,512]{1,0:T(8,128)(2,1)S(1)}, u32[]{:S(2)}, u32[]{:S(2)}) collective-permute-start(bf16[128,512]{1,0:T(8,128)(2,1)S(1)} %get-tuple-element.38), channel_id=1, source_target_pairs={{0,16},{1,17},{2,18},{3,19},{4,20},{5,21},{6,22},{7,23},{8,24},{9,... | collective-permute-start | bytes 393224 | tf_op jit(solution)/shard_map/ppermute | solution.py:40
  25.3 0.1 fusion.2
  25.4 0.1 pad_maximum_fusion.1
  25.5 1.2 %shard_map.90.refs_2_ = bf16[1024,512]{1,0:T(8,128)(2,1)S(1)} custom-call(f32[128,512]{1,0:T(8,128)S(1)} %get-tuple-element.37._.refs_0_, bf16[512,1024]{1,0:T(8,128)(2,1)} %keys_ref.3, bf16[512,1024]{1,0:T(8,128)(2,1)} %values_ref.3), custom_call_target="tpu_custom_call" | custom-call | tf_op jit(solution)/shard_map/pallas_call | solution.py:62
  26.7 2.8 %collective-permute-done.9.refs_1_ = bf16[128,512]{1,0:T(8,128)(2,1)S(1)} collective-permute-done((bf16[128,512]{1,0:T(8,128)(2,1)S(1)}, bf16[128,512]{1,0:T(8,128)(2,1)S(1)}, u32[]{:S(2)}, u32[]{:S(2)}) %collective-permute-start.9) | collective-permute-done | bytes 131104 | tf_op jit(solution)/shard_map/ppermute | solution.py:40
  29.5 0.0 collective-permute-done.10.refs_3_
  29.5 0.0 collective-permute-done.11.refs_4_
  29.5 1.2 %shard_map.92 = (bf16[32,640]{1,0:T(8,128)(2,1)S(1)}, bf16[32,640]{1,0:T(8,128)(2,1)S(1)}) custom-call(f32[128,512]{1,0:T(8,128)S(1)} %get-tuple-element.37._.refs_0_, bf16[128,512]{1,0:T(8,128)(2,1)S(1)} %collective-permute-done.9.refs_1_, bf16[1024,512]{1,0:T(8,128)(2,1)S(1)} %shard_map.90.refs_2_, bf16[512,512]{1,0:T(8,128)(2,1)S(1)} %collective-permute-done.10.refs_3_, ...), custom_call_target="tpu_custom_call" | custom-call | tf_op jit(solution)/shard_map/pallas_call | solution.py:62
  30.7 0.1 collective-permute-start.12
  30.8 0.0 copy-start.1
  30.8 1.6 %collective-permute-start.13 = (bf16[32,640]{1,0:T(8,128)(2,1)S(1)}, bf16[32,640]{1,0:T(8,128)(2,1)S(1)}, u32[]{:S(2)}, u32[]{:S(2)}) collective-permute-start(bf16[32,640]{1,0:T(8,128)(2,1)S(1)} %get-tuple-element.41.refs_0_), channel_id=1, source_target_pairs={{0,16},{1,17},{2,18},{3,19},{4,20},{5,21},{6,22},{7,23},{8,24},{9,... | collective-permute-start | bytes 122888 | tf_op jit(solution)/shard_map/ppermute | solution.py:40
  32.4 0.3 collective-permute-start.14
  32.7 2.2 %shard_map.93.refs_5_ = bf16[1024,2048]{1,0:T(8,128)(2,1)S(1)} custom-call(f32[128,512]{1,0:T(8,128)S(1)} %get-tuple-element.37._.refs_0_, bf16[1024,2048]{1,0:T(8,128)(2,1)} %collective-permute-done.4.source_ref), custom_call_target="tpu_custom_call" | custom-call | tf_op jit(solution)/shard_map/pallas_call | solution.py:62
  34.9 0.0 collective-permute-done.12.refs_1_
  34.9 0.0 collective-permute-done.13.refs_2_
  34.9 1.0 %collective-permute-done.14.refs_3_ = bf16[32,640]{1,0:T(8,128)(2,1)S(1)} collective-permute-done((bf16[32,640]{1,0:T(8,128)(2,1)S(1)}, bf16[32,640]{1,0:T(8,128)(2,1)S(1)}, u32[]{:S(2)}, u32[]{:S(2)}) %collective-permute-start.14) | collective-permute-done | bytes 40992 | tf_op jit(solution)/shard_map/ppermute | solution.py:40
  35.9 0.0 copy-done.1
  35.9 1.8 %shard_map.94 = (f32[2,16,1024]{2,1,0:T(8,128)S(1)}, bf16[2,16,1024]{2,1,0:T(8,128)(2,1)S(1)}, bf16[2,16,1024]{2,1,0:T(8,128)(2,1)S(1)}, bf16[2,16,1024]{2,1,0:T(8,128)(2,1)S(1)}) custom-call(bf16[32,640]{1,0:T(8,128)(2,1)S(1)} %get-tuple-element.41.refs_0_, bf16[32,640]{1,0:T(8,128)(2,1)S(1)} %collective-permute-done.12.refs_1_, ...), custom_call_target="tpu_custom_call" | custom-call | tf_op jit(solution)/shard_map/pallas_call | solution.py:62
  37.8 1.8 %collective-permute-start.15 = (bf16[2,16,1024]{2,1,0:T(8,128)(2,1)S(1)}, bf16[2,16,1024]{2,1,0:T(8,128)(2,1)S(1)}, u32[]{:S(2)}, u32[]{:S(2)}) collective-permute-start(bf16[2,16,1024]{2,1,0:T(8,128)(2,1)S(1)} %get-tuple-element.44), channel_id=1, source_target_pairs={{0,17},{1,16},{2,19},{3,18},{4,21},{5,20},{6,23},{7,22},{8,25},{9,... | collective-permute-start | bytes 196616 | tf_op jit(solution)/shard_map/ppermute | solution.py:40
  39.5 0.6 %collective-permute-start.16 = (bf16[2,16,1024]{2,1,0:T(8,128)(2,1)S(1)}, bf16[2,16,1024]{2,1,0:T(8,128)(2,1)S(1)}, u32[]{:S(2)}, u32[]{:S(2)}) collective-permute-start(bf16[2,16,1024]{2,1,0:T(8,128)(2,1)S(1)} %get-tuple-element.45), channel_id=1, source_target_pairs={{0,1},{1,0},{2,3},{3,2},{4,5},{5,4},{6,7},{7,6},{8,9},{9,8},{10,11... | collective-permute-start | bytes 196616 | tf_op jit(solution)/shard_map/ppermute | solution.py:40
  40.1 1.2 %collective-permute-start.17 = (bf16[2,16,1024]{2,1,0:T(8,128)(2,1)S(1)}, bf16[2,16,1024]{2,1,0:T(8,128)(2,1)S(1)}, u32[]{:S(2)}, u32[]{:S(2)}) collective-permute-start(bf16[2,16,1024]{2,1,0:T(8,128)(2,1)S(1)} %get-tuple-element.46), channel_id=1, source_target_pairs={{0,16},{1,17},{2,18},{3,19},{4,20},{5,21},{6,22},{7,23},{8,24},{9,... | collective-permute-start | bytes 196616 | tf_op jit(solution)/shard_map/ppermute | solution.py:40
  41.3 2.1 %collective-permute-done.15.refs_0_ = bf16[2,16,1024]{2,1,0:T(8,128)(2,1)S(1)} collective-permute-done((bf16[2,16,1024]{2,1,0:T(8,128)(2,1)S(1)}, bf16[2,16,1024]{2,1,0:T(8,128)(2,1)S(1)}, u32[]{:S(2)}, u32[]{:S(2)}) %collective-permute-start.15) | collective-permute-done | bytes 65568 | tf_op jit(solution)/shard_map/ppermute | solution.py:40
  43.3 0.4 collective-permute-done.16.refs_1_
  43.8 0.6 %collective-permute-done.17.refs_2_ = bf16[2,16,1024]{2,1,0:T(8,128)(2,1)S(1)} collective-permute-done((bf16[2,16,1024]{2,1,0:T(8,128)(2,1)S(1)}, bf16[2,16,1024]{2,1,0:T(8,128)(2,1)S(1)}, u32[]{:S(2)}, u32[]{:S(2)}) %collective-permute-start.17) | collective-permute-done | bytes 65568 | tf_op jit(solution)/shard_map/ppermute | solution.py:40
  44.4 3.0 %collective-permute-start.18 = (bf16[16,1024]{1,0:T(8,128)(2,1)S(1)}, bf16[16,1024]{1,0:T(8,128)(2,1)S(1)}, u32[]{:S(2)}, u32[]{:S(2)}) collective-permute-start(bf16[16,1024]{1,0:T(8,128)(2,1)S(1)} %get-tuple-element.49), channel_id=1, source_target_pairs={{0,6},{1,7},{2,4},{3,5},{4,2},{5,3},{6,0},{7,1},{8,14},{9,15},{10,... | collective-permute-start | bytes 98312 | tf_op jit(solution)/shard_map/ppermute | solution.py:40
  47.5 0.1 collective-permute-start.19
  47.5 1.3 %collective-permute-start.20 = (bf16[16,1024]{1,0:T(8,128)(2,1)S(1)}, bf16[16,1024]{1,0:T(8,128)(2,1)S(1)}, u32[]{:S(2)}, u32[]{:S(2)}) collective-permute-start(bf16[16,1024]{1,0:T(8,128)(2,1)S(1)} %get-tuple-element.51), channel_id=1, source_target_pairs={{0,2},{1,3},{2,0},{3,1},{4,6},{5,7},{6,4},{7,5},{8,10},{9,11},{10,... | collective-permute-start | bytes 98312 | tf_op jit(solution)/shard_map/ppermute | solution.py:40
  48.9 1.3 %collective-permute-done.18.refs_1_ = bf16[16,1024]{1,0:T(8,128)(2,1)S(1)} collective-permute-done((bf16[16,1024]{1,0:T(8,128)(2,1)S(1)}, bf16[16,1024]{1,0:T(8,128)(2,1)S(1)}, u32[]{:S(2)}, u32[]{:S(2)}) %collective-permute-start.18) | collective-permute-done | bytes 32800 | tf_op jit(solution)/shard_map/ppermute | solution.py:40
  50.2 2.1 %collective-permute-done.19.refs_2_ = bf16[16,1024]{1,0:T(8,128)(2,1)S(1)} collective-permute-done((bf16[16,1024]{1,0:T(8,128)(2,1)S(1)}, bf16[16,1024]{1,0:T(8,128)(2,1)S(1)}, u32[]{:S(2)}, u32[]{:S(2)}) %collective-permute-start.19) | collective-permute-done | bytes 32800 | tf_op jit(solution)/shard_map/ppermute | solution.py:40
  52.3 0.0 collective-permute-done.20.refs_3_
  52.3 0.6 %shard_map.96 = bf16[16,1024]{1,0:T(8,128)(2,1)} custom-call(f32[16,1024]{1,0:T(8,128)S(1)} %get-tuple-element.48.refs_0_, bf16[16,1024]{1,0:T(8,128)(2,1)S(1)} %collective-permute-done.18.refs_1_, bf16[16,1024]{1,0:T(8,128)(2,1)S(1)} %collective-permute-done.19.refs_2_, bf16[16,1024]{1,0:T(8,128)(2,1)S(1)} %collective-permute-done.20.refs_3_), custom_call_target="tpu_custom_call" | custom-call | tf_op jit(solution)/shard_map/pallas_call | solution.py:62
  (6 shorter events, 0.1 us)
Async XLA Ops:
  0.0 9.0 %copy-start.2 = (s32[4,16]{1,0:T(4,128)S(1)}, s32[4,16]{1,0:T(4,128)}, u32[]{:S(2)}) copy-start(s32[4,16]{1,0:T(4,128)} %ids_ref.3) | copy-start | bytes 772
  0.0 11.3 %collective-permute-start.4 = (bf16[1024,2048]{1,0:T(8,128)(2,1)}, bf16[1024,2048]{1,0:T(8,128)(2,1)}, u32[]{:S(2)}, u32[]{:S(2)}) collective-permute-start(bf16[1024,2048]{1,0:T(8,128)(2,1)} %refs_4_.1), channel_id=1, source_target_pairs={{0,8},{1,9},{2,10},{3,11},{4,12},{5,13},{6,14},{7,15},{8,0},{9,1},... | collective-permute-start | bytes 12582920 | tf_op jit(solution)/shard_map/ppermute | solution.py:40
  3.1 8.2 %collective-permute-start.3 = (bf16[16,2048]{1,0:T(8,128)(2,1)S(1)}, bf16[16,2048]{1,0:T(8,128)(2,1)S(1)}, u32[]{:S(2)}, u32[]{:S(2)}) collective-permute-start(bf16[16,2048]{1,0:T(8,128)(2,1)S(1)} %shard_map.82._), channel_id=1, source_target_pairs={{0,4},{1,5},{2,6},{3,7},{4,0},{5,1},{6,2},{7,3},{8,12},{9,13},{10,... | collective-permute-start | bytes 196616 | tf_op jit(solution)/shard_map/ppermute | solution.py:40
  11.3 9.6 %copy-start = (bf16[2048,1024]{1,0:T(8,128)(2,1)S(1)}, bf16[2048,1024]{1,0:T(8,128)(2,1)}, u32[]{:S(2)}) copy-start(bf16[2048,1024]{1,0:T(8,128)(2,1)} %refs_0_.3) | copy-start | bytes 12582916
  11.3 7.6 %collective-permute-start.5 = (bf16[32,2048]{1,0:T(8,128)(2,1)S(1)}, bf16[32,2048]{1,0:T(8,128)(2,1)S(1)}, u32[]{:S(2)}, u32[]{:S(2)}) collective-permute-start(bf16[32,2048]{1,0:T(8,128)(2,1)S(1)} %pad_maximum_fusion.refs_0_._), channel_id=1, source_target_pairs={{0,3},{1,2},{2,1},{3,0},{4,7},{5,6},{6,5},{7,4},{8,11},{9,10},{10,... | collective-permute-start | bytes 393224 | tf_op jit(solution)/shard_map/ppermute | solution.py:40
  13.9 6.7 %collective-permute-start.6 = (bf16[32,2048]{1,0:T(8,128)(2,1)S(1)}, bf16[32,2048]{1,0:T(8,128)(2,1)S(1)}, u32[]{:S(2)}, u32[]{:S(2)}) collective-permute-start(bf16[32,2048]{1,0:T(8,128)(2,1)S(1)} %pad_maximum_fusion.refs_0_._), channel_id=1, source_target_pairs={{0,2},{1,3},{2,0},{3,1},{4,6},{5,7},{6,4},{7,5},{8,10},{9,11},{10,... | collective-permute-start | bytes 393224 | tf_op jit(solution)/shard_map/ppermute | solution.py:40
  14.4 6.3 %collective-permute-start.7 = (bf16[32,2048]{1,0:T(8,128)(2,1)S(1)}, bf16[32,2048]{1,0:T(8,128)(2,1)S(1)}, u32[]{:S(2)}, u32[]{:S(2)}) collective-permute-start(bf16[32,2048]{1,0:T(8,128)(2,1)S(1)} %pad_maximum_fusion.refs_0_._), channel_id=1, source_target_pairs={{0,1},{1,0},{2,3},{3,2},{4,5},{5,4},{6,7},{7,6},{8,9},{9,8},{10,11... | collective-permute-start | bytes 393224 | tf_op jit(solution)/shard_map/ppermute | solution.py:40
  18.3 11.2 %collective-permute-start.10 = (bf16[512,512]{1,0:T(8,128)(2,1)S(1)}, bf16[512,512]{1,0:T(8,128)(2,1)S(1)}, u32[]{:S(2)}, u32[]{:S(2)}) collective-permute-start(bf16[512,512]{1,0:T(8,128)(2,1)S(1)} %get-tuple-element.39), channel_id=1, source_target_pairs={{0,8},{1,9},{2,10},{3,11},{4,12},{5,13},{6,14},{7,15},{8,0},{9,1},... | collective-permute-start | bytes 1572872 | tf_op jit(solution)/shard_map/ppermute | solution.py:40
  18.4 11.1 %collective-permute-start.11 = (bf16[512,512]{1,0:T(8,128)(2,1)S(1)}, bf16[512,512]{1,0:T(8,128)(2,1)S(1)}, u32[]{:S(2)}, u32[]{:S(2)}) collective-permute-start(bf16[512,512]{1,0:T(8,128)(2,1)S(1)} %get-tuple-element.40), channel_id=1, source_target_pairs={{0,8},{1,9},{2,10},{3,11},{4,12},{5,13},{6,14},{7,15},{8,0},{9,1},... | collective-permute-start | bytes 1572872 | tf_op jit(solution)/shard_map/ppermute | solution.py:40
  22.1 1.5 %collective-permute-start.8 = (bf16[64,1536]{1,0:T(8,128)(2,1)S(1)}, bf16[64,1536]{1,0:T(8,128)(2,1)S(1)}, u32[]{:S(2)}, u32[]{:S(2)}) collective-permute-start(bf16[64,1536]{1,0:T(8,128)(2,1)S(1)} %shard_map.88), channel_id=1, source_target_pairs={{0,8},{1,9},{2,10},{3,11},{4,12},{5,13},{6,14},{7,15},{8,0},{9,1},... | collective-permute-start | bytes 589832 | tf_op jit(solution)/shard_map/ppermute | solution.py:40
  23.7 5.8 %collective-permute-start.9 = (bf16[128,512]{1,0:T(8,128)(2,1)S(1)}, bf16[128,512]{1,0:T(8,128)(2,1)S(1)}, u32[]{:S(2)}, u32[]{:S(2)}) collective-permute-start(bf16[128,512]{1,0:T(8,128)(2,1)S(1)} %get-tuple-element.38), channel_id=1, source_target_pairs={{0,16},{1,17},{2,18},{3,19},{4,20},{5,21},{6,22},{7,23},{8,24},{9,... | collective-permute-start | bytes 393224 | tf_op jit(solution)/shard_map/ppermute | solution.py:40
  30.7 4.2 %collective-permute-start.12 = (bf16[32,640]{1,0:T(8,128)(2,1)S(1)}, bf16[32,640]{1,0:T(8,128)(2,1)S(1)}, u32[]{:S(2)}, u32[]{:S(2)}) collective-permute-start(bf16[32,640]{1,0:T(8,128)(2,1)S(1)} %get-tuple-element.42), channel_id=1, source_target_pairs={{0,8},{1,9},{2,10},{3,11},{4,12},{5,13},{6,14},{7,15},{8,0},{9,1},... | collective-permute-start | bytes 122888 | tf_op jit(solution)/shard_map/ppermute | solution.py:40
  30.8 5.1 %copy-start.1 = (bf16[1024,2048]{1,0:T(8,128)(2,1)S(1)}, bf16[1024,2048]{1,0:T(8,128)(2,1)}, u32[]{:S(2)}) copy-start(bf16[1024,2048]{1,0:T(8,128)(2,1)} %refs_4_.1) | copy-start | bytes 12582916
  30.8 4.1 %collective-permute-start.13 = (bf16[32,640]{1,0:T(8,128)(2,1)S(1)}, bf16[32,640]{1,0:T(8,128)(2,1)S(1)}, u32[]{:S(2)}, u32[]{:S(2)}) collective-permute-start(bf16[32,640]{1,0:T(8,128)(2,1)S(1)} %get-tuple-element.41.refs_0_), channel_id=1, source_target_pairs={{0,16},{1,17},{2,18},{3,19},{4,20},{5,21},{6,22},{7,23},{8,24},{9,... | collective-permute-start | bytes 122888 | tf_op jit(solution)/shard_map/ppermute | solution.py:40
  32.4 3.5 %collective-permute-start.14 = (bf16[32,640]{1,0:T(8,128)(2,1)S(1)}, bf16[32,640]{1,0:T(8,128)(2,1)S(1)}, u32[]{:S(2)}, u32[]{:S(2)}) collective-permute-start(bf16[32,640]{1,0:T(8,128)(2,1)S(1)} %get-tuple-element.42), channel_id=1, source_target_pairs={{0,24},{1,25},{2,26},{3,27},{4,28},{5,29},{6,30},{7,31},{8,16},{9,... | collective-permute-start | bytes 122888 | tf_op jit(solution)/shard_map/ppermute | solution.py:40
  37.8 5.6 %collective-permute-start.15 = (bf16[2,16,1024]{2,1,0:T(8,128)(2,1)S(1)}, bf16[2,16,1024]{2,1,0:T(8,128)(2,1)S(1)}, u32[]{:S(2)}, u32[]{:S(2)}) collective-permute-start(bf16[2,16,1024]{2,1,0:T(8,128)(2,1)S(1)} %get-tuple-element.44), channel_id=1, source_target_pairs={{0,17},{1,16},{2,19},{3,18},{4,21},{5,20},{6,23},{7,22},{8,25},{9,... | collective-permute-start | bytes 196616 | tf_op jit(solution)/shard_map/ppermute | solution.py:40
  39.5 4.3 %collective-permute-start.16 = (bf16[2,16,1024]{2,1,0:T(8,128)(2,1)S(1)}, bf16[2,16,1024]{2,1,0:T(8,128)(2,1)S(1)}, u32[]{:S(2)}, u32[]{:S(2)}) collective-permute-start(bf16[2,16,1024]{2,1,0:T(8,128)(2,1)S(1)} %get-tuple-element.45), channel_id=1, source_target_pairs={{0,1},{1,0},{2,3},{3,2},{4,5},{5,4},{6,7},{7,6},{8,9},{9,8},{10,11... | collective-permute-start | bytes 196616 | tf_op jit(solution)/shard_map/ppermute | solution.py:40
  40.1 4.3 %collective-permute-start.17 = (bf16[2,16,1024]{2,1,0:T(8,128)(2,1)S(1)}, bf16[2,16,1024]{2,1,0:T(8,128)(2,1)S(1)}, u32[]{:S(2)}, u32[]{:S(2)}) collective-permute-start(bf16[2,16,1024]{2,1,0:T(8,128)(2,1)S(1)} %get-tuple-element.46), channel_id=1, source_target_pairs={{0,16},{1,17},{2,18},{3,19},{4,20},{5,21},{6,22},{7,23},{8,24},{9,... | collective-permute-start | bytes 196616 | tf_op jit(solution)/shard_map/ppermute | solution.py:40
  44.4 5.8 %collective-permute-start.18 = (bf16[16,1024]{1,0:T(8,128)(2,1)S(1)}, bf16[16,1024]{1,0:T(8,128)(2,1)S(1)}, u32[]{:S(2)}, u32[]{:S(2)}) collective-permute-start(bf16[16,1024]{1,0:T(8,128)(2,1)S(1)} %get-tuple-element.49), channel_id=1, source_target_pairs={{0,6},{1,7},{2,4},{3,5},{4,2},{5,3},{6,0},{7,1},{8,14},{9,15},{10,... | collective-permute-start | bytes 98312 | tf_op jit(solution)/shard_map/ppermute | solution.py:40
  47.5 4.8 %collective-permute-start.19 = (bf16[16,1024]{1,0:T(8,128)(2,1)S(1)}, bf16[16,1024]{1,0:T(8,128)(2,1)S(1)}, u32[]{:S(2)}, u32[]{:S(2)}) collective-permute-start(bf16[16,1024]{1,0:T(8,128)(2,1)S(1)} %get-tuple-element.50), channel_id=1, source_target_pairs={{0,4},{1,5},{2,6},{3,7},{4,0},{5,1},{6,2},{7,3},{8,12},{9,13},{10,... | collective-permute-start | bytes 98312 | tf_op jit(solution)/shard_map/ppermute | solution.py:40
  47.5 4.8 %collective-permute-start.20 = (bf16[16,1024]{1,0:T(8,128)(2,1)S(1)}, bf16[16,1024]{1,0:T(8,128)(2,1)S(1)}, u32[]{:S(2)}, u32[]{:S(2)}) collective-permute-start(bf16[16,1024]{1,0:T(8,128)(2,1)S(1)} %get-tuple-element.51), channel_id=1, source_target_pairs={{0,2},{1,3},{2,0},{3,1},{4,6},{5,7},{6,4},{7,5},{8,10},{9,11},{10,... | collective-permute-start | bytes 98312 | tf_op jit(solution)/shard_map/ppermute | solution.py:40
